TPU v7x, 256 devices: a whole 4x4x8 slice. The times are simulated.
256 devices in a mesh: stream: 8 (over z), girth: 8 (over x, core), prop: 4 (over y).
Axes of the slice: x: 4, y: 4, z: 8, core: 2. Of those that a mesh axis runs over, the one named last changes fastest.
Arguments:
- velocity: float32 [3, 64, 128, 1024], P(None, 'stream', 'girth', 'prop'), may hold values from -6 to 6
- eddy_visc: float32 [64, 128, 1024], P('stream', 'girth', 'prop'), may hold values from 0.05 to 0.5
- solid: int32 [64, 128, 1024], P('stream', 'girth', 'prop'), may hold values 0 or 1
- pressure_old: float32 [64, 128, 1024], P('stream', 'girth', 'prop'), may hold values from -6 to 6
- relaxation: float32 [64, 128, 1024], P('stream', 'girth', 'prop'), may hold values from 0.05 to 0.5
- host_cell: int32 [3, 1024], replicated, may hold values from 0 to 1022, as said below
- offsets: float32 [3, 1024], replicated, may hold values from 0 to 1
- blade_motion: float32 [3, 1024], replicated, may hold values from -12 to 12
- force_coeff: float32 [1024], replicated, may hold values from 0.05 to 0.5
Outputs:
- velocity_new: float32 [3, 64, 128, 1024], P(None, 'stream', 'girth', 'prop')
- pressure: float32 [64, 128, 1024], P('stream', 'girth', 'prop')
- blade_velocity: float32 [3, 1024], replicated
Inputs may be any that keep to these rules, and one draw needn't show every extreme that they name: host_cell[0] lies in 31 to 33; host_cell[1] lies in 0 to 126 and host_cell[2] in 0 to 1022, so that all 8 corners are inside the grid.
All inputs are finite; a program needn't handle non-finite values. No bound on the sum of `solid` on one device may be relied on, other than what follows from the above.
Results may differ from a plain program's by a relative error of at most 0.0001.
Values sent between devices are 32-bit elements; how exact they have to be, the bound alone decides.
No kernel may reach another device: no remote copies, remote signals or barrier semaphores. Data moves between devices by JAX's collectives and lax.ppermute only.
A program may use at most 128 MiB of HBM per device.

v0:
```python
import jax
import jax.numpy as jnp
from jax import lax
from jax.sharding import PartitionSpec as P

CG_ITERS = 2


DT = 0.1


def padded_2(shard, sides, width):
    for axis, dim in sides:
        count, length = (lax.axis_size(axis), shard.shape[dim])
        up = [(i, (i + 1) % count) for i in range(count - 1)]
        down = [(j, i) for i, j in up]
        last = lax.slice_in_dim(shard, length - width, length, axis=dim)
        initial = lax.slice_in_dim(shard, 0, width, axis=dim)
        before = lax.ppermute(last, axis, up)
        after = lax.ppermute(initial, axis, down)
        shard = jnp.concatenate([before, shard, after], axis=dim)
    return shard


def inner(padded):
    return padded[..., 1:-1, 1:-1, 1:-1]


def neighbours(padded):
    plus = [padded[..., 2:, 1:-1, 1:-1], padded[..., 1:-1, 2:, 1:-1], padded[..., 1:-1, 1:-1, 2:]]
    minus = [
        padded[..., :-2, 1:-1, 1:-1],
        padded[..., 1:-1, :-2, 1:-1],
        padded[..., 1:-1, 1:-1, :-2],
    ]
    return (plus, minus)


def predict(padded_vel, visc_region, keep_region):
    center = inner(padded_vel)
    plus, minus = neighbours(padded_vel)
    lap = plus[0] + minus[0] + plus[1] + minus[1] + plus[2] + minus[2] - 6.0 * center
    conv = sum((center[d][None] * (plus[d] - minus[d]) * 0.5 for d in range(3)))
    return keep_region[None] * (center + DT * (visc_region[None] * lap - conv))


def operate(field, relaxation):
    padded = padded_2(field, (("stream", 0), ("girth", 1), ("prop", 2)), 1)
    plus, minus = neighbours(padded)
    return (
        (6.0 + relaxation) * field - (plus[0] + minus[0] + plus[1] + minus[1] + plus[2] + minus[2]),
        padded,
    )


def squares(residual):
    return lax.psum(jnp.sum(residual * residual), ("stream", "girth", "prop"))


def shards(
    velocity,
    eddy_visc,
    solid,
    pressure_old,
    relaxation,
    host_cell,
    offsets,
    blade_motion,
    force_coeff,
):
    keep = 1.0 - solid.astype(jnp.float32)
    padded_vel = padded_2(velocity, (("stream", 1), ("girth", 2), ("prop", 3)), 1)
    predicted = predict(padded_vel, eddy_visc, keep)
    padded_pred = padded_2(predicted, (("stream", 1), ("girth", 2), ("prop", 3)), 1)
    plus, minus = neighbours(padded_pred)
    div = sum(((plus[d][d] - minus[d][d]) * 0.5 for d in range(3)))
    source = -div / DT
    pressure = pressure_old
    start_image, padded_sum = operate(pressure_old, relaxation)
    residual = source - start_image
    direction = residual
    norm_now = squares(residual)
    for step in range(CG_ITERS):
        image, padded_dir = operate(direction, relaxation)
        alpha = norm_now / lax.psum(jnp.sum(direction * image), ("stream", "girth", "prop"))
        pressure = pressure + alpha * direction
        padded_sum = padded_sum + alpha * padded_dir
        residual = residual - alpha * image
        norm_next = squares(residual)
        direction = residual + norm_next / norm_now * direction
        norm_now = norm_next
    padded_p = padded_2(pressure, (("stream", 0), ("girth", 1), ("prop", 2)), 1)
    plus, minus = neighbours(padded_p)
    corrected = jnp.stack(
        [keep * (predicted[d] - DT * (plus[d] - minus[d]) * 0.5) for d in range(3)]
    )
    size_x, size_y, size_z = pressure.shape
    cells = size_x * size_y * size_z
    start_x = lax.axis_index("stream") * size_x
    start_y = lax.axis_index("girth") * size_y
    start_z = lax.axis_index("prop") * size_z
    flat_vel = corrected.reshape(3, cells)
    corners = []
    partial_value = jnp.zeros(blade_motion.shape, jnp.float32)
    for a in range(2):
        for b in range(2):
            for c in range(2):
                weight = jnp.ones(force_coeff.shape, jnp.float32)
                for d, bit in enumerate((a, b, c)):
                    weight = weight * (offsets[d] if bit else 1.0 - offsets[d])
                local_x = host_cell[0] + a - start_x
                local_y = host_cell[1] + b - start_y
                local_z = host_cell[2] + c - start_z
                owned = (
                    (local_x >= 0)
                    & (local_x < size_x)
                    & (local_y >= 0)
                    & (local_y < size_y)
                    & (local_z >= 0)
                    & (local_z < size_z)
                )
                where = jnp.clip((local_x * size_y + local_y) * size_z + local_z, 0, cells - 1)
                scaled = weight * owned.astype(jnp.float32)
                corners.append((where, scaled))
                partial_value = partial_value + jnp.take(flat_vel, where, axis=1) * scaled[None, :]
    point_vel = lax.psum(partial_value, ("stream", "girth", "prop"))
    slip = point_vel - blade_motion
    speed = jnp.sqrt(jnp.sum(slip * slip, axis=0) + 1.0)
    point_force = -force_coeff[None, :] * speed[None, :] * slip
    body_force = jnp.zeros((3, cells), jnp.float32)
    for where, scaled in corners:
        body_force = body_force.at[:, where].add(point_force * scaled[None, :])
    velocity_new = corrected + DT * body_force.reshape(corrected.shape)
    return (velocity_new, pressure, point_vel)


def solution(mesh):
    placed = (
        P(None, "stream", "girth", "prop"),
        P("stream", "girth", "prop"),
        P("stream", "girth", "prop"),
        P("stream", "girth", "prop"),
        P("stream", "girth", "prop"),
        P(),
        P(),
        P(),
        P(),
    )
    return jax.shard_map(
        shards,
        mesh=mesh,
        in_specs=placed,
        out_specs=(P(None, "stream", "girth", "prop"), P("stream", "girth", "prop"), P()),
        check_vma=False,
    )
```

profile of v0, /device:TPU:1, one launch (start us, length us, event | category | flops | bytes accessed | tf_op | source)
XLA Modules:
  0.0 718.9 jit_solution(16943027640471843795)
XLA Ops:
  1.6 4.4 collective-permute-start.1
  5.9 1.3 collective-permute-start
  8.0 4.2 collective-permute-start.13
  12.1 1.3 collective-permute-start.12
  20.2 3.2 collective-permute-start.2
  23.4 3.0 collective-permute-start.3
  29.0 4.0 collective-permute-start.5
  33.1 1.9 collective-permute-start.14
  35.0 4.8 collective-permute-start.15
  39.8 1.6 collective-permute-done.5
  41.4 2.0 add_multiply_fusion
  43.4 1.3 collective-permute-start.6
  44.7 4.9 collective-permute-start.7
  50.9 3.1 collective-permute-start.8
  54.0 3.0 collective-permute-start.9
  57.1 1.3 collective-permute-start.16
  58.4 4.7 collective-permute-start.17
  64.8 4.0 collective-permute-start.11
  69.7 6.1 collective-permute-done.10
  76.9 1.4 fusion.30
  78.3 1.3 collective-permute-start.18
  79.6 5.2 collective-permute-start.19
  85.7 3.4 collective-permute-start.20
  89.2 2.7 collective-permute-start.21
  92.9 1.3 collective-permute-start.22
  94.2 4.7 collective-permute-start.23
  99.0 1.7 collective-permute-done.22
  102.0 1.7 multiply_reduce_fusion.1
  103.7 83.0 %all-reduce = (f32[]{:T(128)}, f32[]{:T(128)}) all-reduce(f32[]{:T(128)} %get-tuple-element.14, f32[]{:T(128)} %get-tuple-element.13), channel_id=1, replica_groups=mesh['stream'=8,'girth'=8,'prop'=4] {'stream','girth','prop'}, use_global_device_ids=true, to_apply=%region_1.0 | all-reduce | flops 2 | bytes 16 | tf_op jit(solution)/shard_map/psum | solution.py:57
  188.7 74.7 %psum.37 = f32[]{:T(128)} all-reduce(f32[]{:T(128)} %multiply_reduce_fusion), channel_id=1, replica_groups=mesh['stream'=8,'girth'=8,'prop'=4] {'stream','girth','prop'}, use_global_device_ids=true, to_apply=%region_5.0 | all-reduce | flops 1 | bytes 8 | tf_op jit(solution)/shard_map/psum | solution.py:57
  264.7 1.3 collective-permute-start.24
  266.0 4.0 collective-permute-start.25
  270.9 3.7 collective-permute-start.26
  274.6 2.9 collective-permute-start.27
  278.4 1.3 collective-permute-start.28
  279.7 4.0 collective-permute-start.29
  283.7 1.9 collective-permute-done.28
  287.3 75.6 %psum.38 = f32[]{:T(128)} all-reduce(f32[]{:T(128)} %fusion.17), channel_id=1, replica_groups=mesh['stream'=8,'girth'=8,'prop'=4] {'stream','girth','prop'}, use_global_device_ids=true, to_apply=%region_7.0 | all-reduce | flops 1 | bytes 8 | tf_op jit(solution)/shard_map/psum | solution.py:85
  364.3 1.3 collective-permute-start.30
  365.6 4.3 collective-permute-start.31
  370.7 3.4 collective-permute-start.32
  374.1 2.8 collective-permute-start.33
  379.2 4.0 collective-permute-start.35
  383.5 1.4 collective-permute-done.34
  386.7 8.5 %copy.32 = f32[3,32768]{0,1:T(8,128)} copy(f32[3,32768]{1,0:T(4,128)S(1)} %pad_maximum_fusion.2) | data formatting | bytes 786432 | tf_op jit(solution)/shard_map/stack | solution.py:94
  395.2 8.6 %gather_fusion = f32[1024,3]{1,0:T(8,128)S(1)} fusion(f32[3,32768]{0,1:T(8,128)} %copy.32, s32[1024]{0:T(1024)S(1)} %get-tuple-element.111), kind=kCustom, calls=%fused_computation.clone | custom fusion | bytes 28672 | tf_op jit(solution)/shard_map/jit(_take)/gather | solution.py:125
  403.9 8.6 %gather_fusion.1 = f32[1024,3]{1,0:T(8,128)S(1)} fusion(f32[3,32768]{0,1:T(8,128)} %copy.32, s32[1024]{0:T(1024)S(1)} %get-tuple-element.112), kind=kCustom, calls=%fused_computation.1.clone | custom fusion | bytes 28672 | tf_op jit(solution)/shard_map/jit(_take)/gather | solution.py:125
  412.7 8.6 %gather_fusion.2 = f32[1024,3]{1,0:T(8,128)S(1)} fusion(f32[3,32768]{0,1:T(8,128)} %copy.32, s32[1024]{0:T(1024)S(1)} %get-tuple-element.113), kind=kCustom, calls=%fused_computation.2.clone | custom fusion | bytes 28672 | tf_op jit(solution)/shard_map/jit(_take)/gather | solution.py:125
  421.5 8.6 %gather_fusion.3 = f32[1024,3]{1,0:T(8,128)S(1)} fusion(f32[3,32768]{0,1:T(8,128)} %copy.32, s32[1024]{0:T(1024)S(1)} %get-tuple-element.114), kind=kCustom, calls=%fused_computation.3.clone | custom fusion | bytes 28672 | tf_op jit(solution)/shard_map/jit(_take)/gather | solution.py:125
  430.3 8.6 %gather_fusion.4 = f32[1024,3]{1,0:T(8,128)S(1)} fusion(f32[3,32768]{0,1:T(8,128)} %copy.32, s32[1024]{0:T(1024)S(1)} %get-tuple-element.115), kind=kCustom, calls=%fused_computation.4.clone | custom fusion | bytes 28672 | tf_op jit(solution)/shard_map/jit(_take)/gather | solution.py:125
  439.1 8.6 %gather_fusion.5 = f32[1024,3]{1,0:T(8,128)S(1)} fusion(f32[3,32768]{0,1:T(8,128)} %copy.32, s32[1024]{0:T(1024)S(1)} %get-tuple-element.116), kind=kCustom, calls=%fused_computation.5.clone | custom fusion | bytes 28672 | tf_op jit(solution)/shard_map/jit(_take)/gather | solution.py:125
  447.9 8.6 %gather_fusion.6 = f32[1024,3]{1,0:T(8,128)S(1)} fusion(f32[3,32768]{0,1:T(8,128)} %copy.32, s32[1024]{0:T(1024)S(1)} %get-tuple-element.117), kind=kCustom, calls=%fused_computation.6.clone | custom fusion | bytes 28672 | tf_op jit(solution)/shard_map/jit(_take)/gather | solution.py:125
  456.6 8.6 %gather_fusion.7 = f32[1024,3]{1,0:T(8,128)S(1)} fusion(f32[3,32768]{0,1:T(8,128)} %copy.32, s32[1024]{0:T(1024)S(1)} %get-tuple-element.118), kind=kCustom, calls=%fused_computation.7.clone | custom fusion | bytes 28672 | tf_op jit(solution)/shard_map/jit(_take)/gather | solution.py:125
  465.5 77.6 %psum.39 = f32[3,1024]{1,0:T(4,128)S(1)} all-reduce(f32[3,1024]{1,0:T(4,128)S(1)} %fusion.44), channel_id=1, replica_groups=mesh['stream'=8,'girth'=8,'prop'=4] {'stream','girth','prop'}, use_global_device_ids=true, to_apply=%region_8.10 | all-reduce | flops 3072 | bytes 24576 | tf_op jit(solution)/shard_map/psum | solution.py:126
  547.5 14.8 %scatter_custom_fusion = f32[3,32768]{0,1:T(8,128)} fusion(s32[1024]{0:T(1024)S(1)} %bitcast.169, f32[1024,3]{1,0:T(8,128)} %copy.48, f32[]{:T(128)} %constant.17.clone.1), kind=kCustom, calls=%fused_computation.17 | custom fusion | flops 3072 | bytes 393728 | tf_op jit(solution)/shard_map/scatter-add | solution.py:132
  562.3 19.5 %scatter_fusion = f32[3,32768]{0,1:T(8,128)} fusion(f32[3,32768]{0,1:T(8,128)} %scatter_custom_fusion, s32[1024]{0:T(1024)S(1)} %bitcast.168, f32[1024,3]{1,0:T(8,128)} %copy.49), kind=kCustom, calls=%fused_computation.9 | custom fusion | flops 3072 | bytes 40960 | tf_op jit(solution)/shard_map/scatter-add | solution.py:132
  581.8 19.5 %scatter_fusion.1 = f32[3,32768]{0,1:T(8,128)} fusion(f32[3,32768]{0,1:T(8,128)} %scatter_fusion, s32[1024]{0:T(1024)S(1)} %bitcast.164, f32[1024,3]{1,0:T(8,128)} %copy.50), kind=kCustom, calls=%fused_computation.10 | custom fusion | flops 3072 | bytes 40960 | tf_op jit(solution)/shard_map/scatter-add | solution.py:132
  601.3 19.1 %scatter_fusion.2 = f32[3,32768]{0,1:T(8,128)} fusion(f32[3,32768]{0,1:T(8,128)} %scatter_fusion.1, s32[1024]{0:T(1024)S(1)} %bitcast.167, f32[1024,3]{1,0:T(8,128)S(1)} %copy.51), kind=kCustom, calls=%fused_computation.11 | custom fusion | flops 3072 | bytes 40960 | tf_op jit(solution)/shard_map/scatter-add | solution.py:132
  620.4 19.1 %scatter_fusion.3 = f32[3,32768]{0,1:T(8,128)} fusion(f32[3,32768]{0,1:T(8,128)} %scatter_fusion.2, s32[1024]{0:T(1024)S(1)} %bitcast.163, f32[1024,3]{1,0:T(8,128)S(1)} %copy.52), kind=kCustom, calls=%fused_computation.12 | custom fusion | flops 3072 | bytes 40960 | tf_op jit(solution)/shard_map/scatter-add | solution.py:132
  639.4 19.1 %scatter_fusion.4 = f32[3,32768]{0,1:T(8,128)} fusion(f32[3,32768]{0,1:T(8,128)} %scatter_fusion.3, s32[1024]{0:T(1024)S(1)} %bitcast.166, f32[1024,3]{1,0:T(8,128)S(1)} %copy.53), kind=kCustom, calls=%fused_computation.13 | custom fusion | flops 3072 | bytes 40960 | tf_op jit(solution)/shard_map/scatter-add | solution.py:132
  658.5 19.1 %scatter_fusion.5 = f32[3,32768]{0,1:T(8,128)} fusion(f32[3,32768]{0,1:T(8,128)} %scatter_fusion.4, s32[1024]{0:T(1024)S(1)} %bitcast.165, f32[1024,3]{1,0:T(8,128)S(1)} %copy.54), kind=kCustom, calls=%fused_computation.14 | custom fusion | flops 3072 | bytes 40960 | tf_op jit(solution)/shard_map/scatter-add | solution.py:132
  677.6 19.1 %scatter_fusion.6 = f32[3,32768]{0,1:T(8,128)} fusion(f32[3,32768]{0,1:T(8,128)} %scatter_fusion.5, s32[1024]{0:T(1024)S(1)} %bitcast.162, f32[1024,3]{1,0:T(8,128)S(1)} %copy.55), kind=kCustom, calls=%fused_computation.15 | custom fusion | flops 3072 | bytes 40960 | tf_op jit(solution)/shard_map/scatter-add | solution.py:132
  696.7 11.4 %broadcast_multiply_fusion = f32[3,32768]{0,1:T(8,128)} fusion(f32[3,32768]{0,1:T(8,128)} %scatter_fusion.6), kind=kLoop, calls=%fused_computation.16 | loop fusion | flops 98304 | bytes 786432 | tf_op jit(solution)/shard_map/mul | solution.py:133
  708.1 10.0 %copy.56 = f32[3,8,16,256]{3,2,1,0:T(8,128)S(1)} copy(f32[3,8,16,256]{0,3,2,1:T(8,128)} %bitcast.126) | data formatting | bytes 786432 | tf_op jit(solution)/shard_map/mul | solution.py:133
  (125 shorter events, 34.8 us)
Async XLA Ops:
  0.6 363.6 %copy-start.1 = (f32[8,16,256]{2,1,0:T(8,128)S(1)}, f32[8,16,256]{2,1,0:T(8,128)}, u32[]{:S(2)}) copy-start(f32[8,16,256]{2,1,0:T(8,128)} %param.14) | copy-start | bytes 393220
  0.6 382.5 %copy-start.2 = (s32[8,16,256]{2,1,0:T(8,128)S(1)}, s32[8,16,256]{2,1,0:T(8,128)}, u32[]{:S(2)}) copy-start(s32[8,16,256]{2,1,0:T(8,128)} %param.13) | copy-start | bytes 393220
  0.7 285.8 %copy-start.3 = (f32[8,16,256]{2,1,0:T(8,128)S(1)}, f32[8,16,256]{2,1,0:T(8,128)}, u32[]{:S(2)}) copy-start(f32[8,16,256]{2,1,0:T(8,128)} %param.15) | copy-start | bytes 393220
  1.6 17.5 %collective-permute-start.1 = (f32[3,1,16,256]{3,2,1,0:T(8,128)S(1)}, f32[3,1,16,256]{3,2,1,0:T(8,128)S(1)}, u32[]{:S(2)}, u32[]{:S(2)}) collective-permute-start(f32[3,1,16,256]{3,2,1,0:T(8,128)S(1)} %get-tuple-element.60), channel_id=1, source_target_pairs={{0,32},{32,64},{64,96},{96,128},{128,160},{160,192},{192,224},{1,3... | collective-permute-start | bytes 147464 | tf_op jit(solution)/shard_map/ppermute | solution.py:19
  5.9 14.2 %collective-permute-start = (f32[3,1,16,256]{3,2,1,0:T(8,128)S(1)}, f32[3,1,16,256]{3,2,1,0:T(8,128)S(1)}, u32[]{:S(2)}, u32[]{:S(2)}) collective-permute-start(f32[3,1,16,256]{3,2,1,0:T(8,128)S(1)} %get-tuple-element.59), channel_id=1, source_target_pairs={{32,0},{64,32},{96,64},{128,96},{160,128},{192,160},{224,192},{33,... | collective-permute-start | bytes 147464 | tf_op jit(solution)/shard_map/ppermute | solution.py:20
  8.0 10.2 %collective-permute-start.13 = (f32[1,16,256]{2,1,0:T(8,128)S(1)}, f32[1,16,256]{2,1,0:T(8,128)S(1)}, u32[]{:S(2)}, u32[]{:S(2)}) collective-permute-start(f32[1,16,256]{2,1,0:T(8,128)S(1)} %get-tuple-element.84), channel_id=1, source_target_pairs={{0,32},{32,64},{64,96},{96,128},{128,160},{160,192},{192,224},{1,3... | collective-permute-start | bytes 49160 | tf_op jit(solution)/shard_map/ppermute | solution.py:19
  12.1 14.3 %collective-permute-start.12 = (f32[1,16,256]{2,1,0:T(8,128)S(1)}, f32[1,16,256]{2,1,0:T(8,128)S(1)}, u32[]{:S(2)}, u32[]{:S(2)}) collective-permute-start(f32[1,16,256]{2,1,0:T(8,128)S(1)} %get-tuple-element.83), channel_id=1, source_target_pairs={{32,0},{64,32},{96,64},{128,96},{160,128},{192,160},{224,192},{33,... | collective-permute-start | bytes 49160 | tf_op jit(solution)/shard_map/ppermute | solution.py:20
  20.2 6.3 collective-permute-start.2
  23.4 4.0 collective-permute-start.3
  27.7 12.1 %collective-permute-start.4 = (f32[3,10,18,1]{3,2,1,0:T(8,128)S(1)}, f32[3,10,18,1]{3,2,1,0:T(8,128)S(1)}, u32[]{:S(2)}, u32[]{:S(2)}) collective-permute-start(f32[3,10,18,1]{3,2,1,0:T(8,128)S(1)} %get-tuple-element.46), channel_id=1, source_target_pairs={{1,0},{2,1},{3,2},{5,4},{6,5},{7,6},{9,8},{10,9},{11,10},{13,12},{... | collective-permute-start | bytes 6488 | tf_op jit(solution)/shard_map/ppermute | solution.py:20
  29.0 12.4 %collective-permute-start.5 = (f32[3,10,18,1]{3,2,1,0:T(8,128)S(1)}, f32[3,10,18,1]{3,2,1,0:T(8,128)S(1)}, u32[]{:S(2)}, u32[]{:S(2)}) collective-permute-start(f32[3,10,18,1]{3,2,1,0:T(8,128)S(1)} %get-tuple-element.47), channel_id=1, source_target_pairs={{0,1},{1,2},{2,3},{4,5},{5,6},{6,7},{8,9},{9,10},{10,11},{12,13},{... | collective-permute-start | bytes 6488 | tf_op jit(solution)/shard_map/ppermute | solution.py:19
  33.1 16.6 %collective-permute-start.14 = (f32[10,1,256]{2,1,0:T(1,128)S(1)}, f32[10,1,256]{2,1,0:T(1,128)S(1)}, u32[]{:S(2)}, u32[]{:S(2)}) collective-permute-start(f32[10,1,256]{2,1,0:T(1,128)S(1)} %get-tuple-element.76), channel_id=1, source_target_pairs={{4,0},{8,4},{12,8},{16,12},{20,16},{24,20},{28,24},{5,1},{9,5},{13... | collective-permute-start | bytes 30728 | tf_op jit(solution)/shard_map/ppermute | solution.py:20
  35.0 14.7 %collective-permute-start.15 = (f32[10,1,256]{2,1,0:T(1,128)S(1)}, f32[10,1,256]{2,1,0:T(1,128)S(1)}, u32[]{:S(2)}, u32[]{:S(2)}) collective-permute-start(f32[10,1,256]{2,1,0:T(1,128)S(1)} %get-tuple-element.75), channel_id=1, source_target_pairs={{0,4},{4,8},{8,12},{12,16},{16,20},{20,24},{24,28},{1,5},{5,9},{9,... | collective-permute-start | bytes 30728 | tf_op jit(solution)/shard_map/ppermute | solution.py:19
  43.4 6.3 collective-permute-start.6
  44.7 6.1 collective-permute-start.7
  50.9 12.3 %collective-permute-start.8 = (f32[3,10,1,256]{3,2,1,0:T(1,128)S(1)}, f32[3,10,1,256]{3,2,1,0:T(1,128)S(1)}, u32[]{:S(2)}, u32[]{:S(2)}) collective-permute-start(f32[3,10,1,256]{3,2,1,0:T(1,128)S(1)} %get-tuple-element.51), channel_id=1, source_target_pairs={{4,0},{8,4},{12,8},{16,12},{20,16},{24,20},{28,24},{5,1},{9,5},{13... | collective-permute-start | bytes 92168 | tf_op jit(solution)/shard_map/ppermute | solution.py:20
  54.0 9.2 %collective-permute-start.9 = (f32[3,10,1,256]{3,2,1,0:T(1,128)S(1)}, f32[3,10,1,256]{3,2,1,0:T(1,128)S(1)}, u32[]{:S(2)}, u32[]{:S(2)}) collective-permute-start(f32[3,10,1,256]{3,2,1,0:T(1,128)S(1)} %get-tuple-element.50), channel_id=1, source_target_pairs={{0,4},{4,8},{8,12},{12,16},{16,20},{20,24},{24,28},{1,5},{5,9},{9,... | collective-permute-start | bytes 92168 | tf_op jit(solution)/shard_map/ppermute | solution.py:19
  57.1 12.6 %collective-permute-start.16 = (f32[10,18,1]{2,1,0:T(8,128)S(1)}, f32[10,18,1]{2,1,0:T(8,128)S(1)}, u32[]{:S(2)}, u32[]{:S(2)}) collective-permute-start(f32[10,18,1]{2,1,0:T(8,128)S(1)} %get-tuple-element.67), channel_id=1, source_target_pairs={{1,0},{2,1},{3,2},{5,4},{6,5},{7,6},{9,8},{10,9},{11,10},{13,12},{... | collective-permute-start | bytes 2168 | tf_op jit(solution)/shard_map/ppermute | solution.py:20
  58.4 11.3 %collective-permute-start.17 = (f32[10,18,1]{2,1,0:T(8,128)S(1)}, f32[10,18,1]{2,1,0:T(8,128)S(1)}, u32[]{:S(2)}, u32[]{:S(2)}) collective-permute-start(f32[10,18,1]{2,1,0:T(8,128)S(1)} %get-tuple-element.68), channel_id=1, source_target_pairs={{0,1},{1,2},{2,3},{4,5},{5,6},{6,7},{8,9},{9,10},{10,11},{12,13},{... | collective-permute-start | bytes 2168 | tf_op jit(solution)/shard_map/ppermute | solution.py:19
  63.5 12.4 %collective-permute-start.10 = (f32[3,10,18,1]{3,2,1,0:T(8,128)S(1)}, f32[3,10,18,1]{3,2,1,0:T(8,128)S(1)}, u32[]{:S(2)}, u32[]{:S(2)}) collective-permute-start(f32[3,10,18,1]{3,2,1,0:T(8,128)S(1)} %get-tuple-element.44), channel_id=1, source_target_pairs={{1,0},{2,1},{3,2},{5,4},{6,5},{7,6},{9,8},{10,9},{11,10},{13,12},{... | collective-permute-start | bytes 6488 | tf_op jit(solution)/shard_map/ppermute | solution.py:20
  64.8 12.1 %collective-permute-start.11 = (f32[3,10,18,1]{3,2,1,0:T(8,128)S(1)}, f32[3,10,18,1]{3,2,1,0:T(8,128)S(1)}, u32[]{:S(2)}, u32[]{:S(2)}) collective-permute-start(f32[3,10,18,1]{3,2,1,0:T(8,128)S(1)} %get-tuple-element.45), channel_id=1, source_target_pairs={{0,1},{1,2},{2,3},{4,5},{5,6},{6,7},{8,9},{9,10},{10,11},{12,13},{... | collective-permute-start | bytes 6488 | tf_op jit(solution)/shard_map/ppermute | solution.py:19
  78.3 464.9 %copy-start.5 = (f32[3,1024]{1,0:T(4,128)S(1)}, f32[3,1024]{1,0:T(4,128)}, u32[]{:S(2)}) copy-start(f32[3,1024]{1,0:T(4,128)} %param.18) | copy-start | bytes 36868
  78.3 464.9 %copy-start.6 = (f32[1024]{0:T(1024)S(1)}, f32[1024]{0:T(1024)}, u32[]{:S(2)}) copy-start(f32[1024]{0:T(1024)} %param.19) | copy-start | bytes 12292
  78.3 7.4 %collective-permute-start.18 = (f32[1,16,256]{2,1,0:T(8,128)S(1)}, f32[1,16,256]{2,1,0:T(8,128)S(1)}, u32[]{:S(2)}, u32[]{:S(2)}) collective-permute-start(f32[1,16,256]{2,1,0:T(8,128)S(1)} %get-tuple-element.82), channel_id=1, source_target_pairs={{32,0},{64,32},{96,64},{128,96},{160,128},{192,160},{224,192},{33,... | collective-permute-start | bytes 49160 | tf_op jit(solution)/shard_map/ppermute | solution.py:20
  79.6 6.1 collective-permute-start.19
  85.7 7.0 collective-permute-start.20
  89.2 3.6 collective-permute-start.21
  92.9 7.7 %collective-permute-start.22 = (f32[10,18,1]{2,1,0:T(8,128)S(1)}, f32[10,18,1]{2,1,0:T(8,128)S(1)}, u32[]{:S(2)}, u32[]{:S(2)}) collective-permute-start(f32[10,18,1]{2,1,0:T(8,128)S(1)} %get-tuple-element.65), channel_id=1, source_target_pairs={{1,0},{2,1},{3,2},{5,4},{6,5},{7,6},{9,8},{10,9},{11,10},{13,12},{... | collective-permute-start | bytes 2168 | tf_op jit(solution)/shard_map/ppermute | solution.py:20
  94.2 7.7 %collective-permute-start.23 = (f32[10,18,1]{2,1,0:T(8,128)S(1)}, f32[10,18,1]{2,1,0:T(8,128)S(1)}, u32[]{:S(2)}, u32[]{:S(2)}) collective-permute-start(f32[10,18,1]{2,1,0:T(8,128)S(1)} %get-tuple-element.66), channel_id=1, source_target_pairs={{0,1},{1,2},{2,3},{4,5},{5,6},{6,7},{8,9},{9,10},{10,11},{12,13},{... | collective-permute-start | bytes 2168 | tf_op jit(solution)/shard_map/ppermute | solution.py:19
  264.7 5.3 collective-permute-start.24
  266.0 4.8 collective-permute-start.25
  270.9 6.6 collective-permute-start.26
  274.6 3.7 collective-permute-start.27
  278.4 7.2 %collective-permute-start.28 = (f32[10,18,1]{2,1,0:T(8,128)S(1)}, f32[10,18,1]{2,1,0:T(8,128)S(1)}, u32[]{:S(2)}, u32[]{:S(2)}) collective-permute-start(f32[10,18,1]{2,1,0:T(8,128)S(1)} %get-tuple-element.63), channel_id=1, source_target_pairs={{1,0},{2,1},{3,2},{5,4},{6,5},{7,6},{9,8},{10,9},{11,10},{13,12},{... | collective-permute-start | bytes 2168 | tf_op jit(solution)/shard_map/ppermute | solution.py:20
  279.7 6.8 collective-permute-start.29
  364.2 198.1 %copy-start = (f32[8,16,256]{2,1,0:T(8,128)}, f32[8,16,256]{2,1,0:T(8,128)S(1)}, u32[]{:S(2)}) copy-start(f32[8,16,256]{2,1,0:T(8,128)S(1)} %multiply_add_fusion) | copy-start | bytes 393220
  364.3 5.6 collective-permute-start.30
  365.6 5.1 collective-permute-start.31
  370.7 6.2 collective-permute-start.32
  374.1 3.6 collective-permute-start.33
  377.9 7.1 collective-permute-start.34
  379.2 6.8 collective-permute-start.35
  543.1 165.0 %copy-start.4 = (f32[3,1024]{1,0:T(4,128)}, f32[3,1024]{1,0:T(4,128)S(1)}, u32[]{:S(2)}) copy-start(f32[3,1024]{1,0:T(4,128)S(1)} %psum.39) | copy-start | bytes 36868
where the time goes:
time: 722 us; the launch traced here: 719 us
  blocking collectives  311 us (43%)
  other arithmetic  176 us (24%)
  starting transfers between devices  106 us (15%)
  local copies, waits for them, and re-layouts  98.8 us (14%)
  waiting for transfers between devices  22.2 us (3%)
    psum x2, blocking collectives, squares(): return lax.psum(jnp.sum(residual * residual), ('stream', 'girth', 'prop'))  158 us
    scatter-add x8, other arithmetic, shards(): body_force = body_force.at[:, where].add(point_force * scaled[None, :])  149 us
    psum x1, blocking collectives, shards(): point_vel = lax.psum(partial_value, ('stream', 'girth', 'prop'))  77.6 us
    psum x1, blocking collectives, shards(): lax.psum(jnp.sum(direction * image), ('stream', 'girth', 'prop'))  75.6 us
    ppermute x18, starting transfers between devices, padded_2(): before = lax.ppermute(last, axis, up)  71.6 us
    gather x16, local copies, waits for them, and re-layouts, shards(): jnp.take(flat_vel, where, axis=1) * scaled[None, :]  70.2 us
    ppermute x18, starting transfers between devices, padded_2(): after = lax.ppermute(initial, axis, down)  34.3 us
  transfers between devices with their start and end apart: 36, of which 15 were waited for; matrix products, arithmetic and copies ran while one was open for 2% of the time, Pallas kernels for 0%

commit v1 on v0

v1 whole, which is shorter than its diff:
```python
import jax
import jax.numpy as jnp
from jax import lax
from jax.experimental import pallas as pl
from jax.experimental.pallas import tpu as pltpu
from jax.sharding import PartitionSpec as P

DT = 0.1
F32 = jnp.float32
AXES = ("stream", "girth", "prop")

X, Y, Z = 8, 16, 256
YE, ZE = 24, 384
RADIUS = (4, 4, 4, 3, 3, 3, 2)
XOFF = (0, 4, 8, 12, 15, 18, 21)
XLAYERS = 23
BASE = (0, 16, 32, 48, 62, 76, 90)
LAYERS = 102
VISC, KEEP, PRES, RELAX = 3, 4, 5, 6
YLAYERS = [(f, x) for f in range(7) for x in range(1 - RADIUS[f], X - 1 + RADIUS[f])]
YPAIRS = len(YLAYERS) // 2
YUNITS = -(-YPAIRS // 16)
YTILES = YPAIRS + -(-YUNITS // 2)
WINDOW = 3
VMEM = pl.BlockSpec(memory_space=pltpu.VMEM)
PARAMS = pltpu.CompilerParams(vmem_limit_bytes=48 * 1024 * 1024)


def iota(shape, dim):
    return lax.broadcasted_iota(jnp.int32, shape, dim)


def roll(a, shift, axis):
    shift = shift % a.shape[axis]
    return a if shift == 0 else pltpu.roll(a, shift, axis)


def own_layer(refs, f, x):
    if f < 3:
        return refs[0][f, x]
    if f == KEEP:
        return 1.0 - refs[2][x].astype(F32)
    return refs[{VISC: 1, PRES: 3, RELAX: 4}[f]][x]


def pack_kernel(*args):
    refs, (up, down, z_up, z_down, uu, ud, du, dd) = args[:5], args[5:]
    for f, (r, off) in enumerate(zip(RADIUS, XOFF)):
        for i in range(r):
            up[off + i] = own_layer(refs, f, X - r + i)
            down[off + i] = own_layer(refs, f, i)
    slot = iota((Y, 128), 1) // 4

    def pack(layers, to_up, to_down):
        high = jnp.zeros((Y, 128), F32)
        low = jnp.zeros((Y, 128), F32)
        for j, layer in enumerate(layers):
            high = jnp.where(slot == j, roll(layer[:, Z - 128 :], 4 * j - 124, 1), high)
            low = jnp.where(slot == j, roll(layer[:, :128], 4 * j, 1), low)
        to_up[...] = high
        to_down[...] = low

    every = [(f, x) for f in range(7) for x in range(X)]
    for unit in range(2):
        pack(
            [own_layer(refs, f, x) for f, x in every[unit * 32 : unit * 32 + 32]],
            z_up.at[unit],
            z_down.at[unit],
        )
    tops = [(f, X - RADIUS[f] + i) for f in range(7) for i in range(RADIUS[f])]
    lows = [(f, i) for f in range(7) for i in range(RADIUS[f])]
    pack([own_layer(refs, f, x) for f, x in tops], uu, ud)
    pack([own_layer(refs, f, x) for f, x in lows], du, dd)


def inside_flags():
    out = []
    for axis in AXES:
        i = lax.axis_index(axis)
        out.append((i > 0).astype(F32))
        out.append((i < lax.axis_size(axis) - 1).astype(F32))
    return out


def layer_reader(refs, got):
    xm, xp, zm, zp, mm, mp, pm, pp = got
    in_xm, in_xp, _, _, in_zm, in_zp = inside_flags()
    lane = iota((Y, 128), 1)
    right = (lane < 4).astype(F32) * in_zp
    left = (lane >= 124).astype(F32) * in_zm

    def third(minus, plus, j):
        return roll(plus, -4 * j, 1) * right + roll(minus, 124 - 4 * j, 1) * left

    def layer(f, x):
        r = RADIUS[f]
        if x < 0:
            i = XOFF[f] + x + r
            return xm[i] * in_xm, third(mm[...], mp[...], i) * in_xm
        if x >= X:
            i = XOFF[f] + x - X
            return xp[i] * in_xp, third(pm[...], pp[...], i) * in_xp
        q = f * X + x
        return own_layer(refs, f, x), third(zm[q // 32], zp[q // 32], q % 32)

    return layer


def edge_kernel(*args):
    refs, got, (to_up, to_down) = args[:5], args[5:13], args[13:]
    layer = layer_reader(refs, got)
    low_rows = iota((8, 128), 0) < 4
    slot = iota((8, 128), 1) // 8
    highs = [jnp.zeros((8, 128), F32) for _ in range(2 * (YTILES - YPAIRS))]
    lows = list(highs)

    def pair(a, b):
        high = jnp.where(low_rows, roll(a[8:], 4, 0), b[8:])
        low = jnp.where(low_rows, a[:8], roll(b[:8], 4, 0))
        return high, low

    for t in range(YPAIRS):
        a, a3 = layer(*YLAYERS[2 * t])
        b, b3 = layer(*YLAYERS[2 * t + 1])
        for half in range(2):
            cut = slice(128 * half, 128 * half + 128)
            to_up[t, :, cut], to_down[t, :, cut] = pair(a[:, cut], b[:, cut])
        high, low = pair(a3, b3)
        unit, j = t // 16, t % 16
        highs[unit] = jnp.where(slot == j, roll(high, 8 * j + 4, 1), highs[unit])
        lows[unit] = jnp.where(slot == j, roll(low, 8 * j + 4, 1), lows[unit])
    for t in range(YPAIRS, YTILES):
        for half in range(2):
            cut = slice(128 * half, 128 * half + 128)
            to_up[t, :, cut] = highs[2 * (t - YPAIRS) + half]
            to_down[t, :, cut] = lows[2 * (t - YPAIRS) + half]


def y_plus(a):
    return roll(a, -1, 0)


def y_minus(a):
    return roll(a, 1, 0)


def z_plus(a):
    return roll(a, -1, 1)


def z_minus(a):
    return roll(a, 1, 1)


def own(a):
    return a[:Y, :Z]


def main_kernel(*args):
    refs, got = args[:5], args[5:13]
    ym, yp, host, off, payload, grads, r0_out, s_out, ext, pred, res, img = args[13:]
    layer = layer_reader(refs, got)
    in_xm, in_xp, in_ym, in_yp, in_zm, in_zp = inside_flags()

    low_rows = iota((8, 128), 0) < 4
    lane = iota((8, 128), 1)
    ends = ((lane < 4) | (lane >= 124)).astype(F32)
    zero = jnp.zeros((8, 128), F32)
    place = {key: m for m, key in enumerate(YLAYERS)}
    for f in range(7):
        for x in range(-RADIUS[f], X + RADIUS[f]):
            at = BASE[f] + x + RADIUS[f]
            base, third = layer(f, x)
            ext[at, :Y, :Z] = base
            ext[at, :Y, Z:] = third
            m = place.get((f, x))
            if m is None:
                for half in range(3):
                    ext[at, Y:, 128 * half : 128 * half + 128] = zero
                continue
            t, odd = divmod(m, 2)

            def rows(plus, minus):
                plus, minus = plus * in_yp, minus * in_ym
                if odd:
                    return jnp.where(low_rows, roll(plus, 4, 0), minus)
                return jnp.where(low_rows, plus, roll(minus, 4, 0))

            for half in range(2):
                cut = slice(128 * half, 128 * half + 128)
                ext[at, Y:, cut] = rows(yp[t, :, cut], ym[t, :, cut])
            unit, j = divmod(t, 16)
            cut = slice(128 * (unit % 2), 128 * (unit % 2) + 128)
            last = YPAIRS + unit // 2
            packed = rows(yp[last, :, cut], ym[last, :, cut])
            ext[at, Y:, Z:] = roll(packed, -8 * j - 4, 1) * ends

    row, col = iota((YE, ZE), 0), iota((YE, ZE), 1)
    in_y = jnp.where(row < Y, 1.0, jnp.where(row < Y + 4, in_yp, in_ym))
    in_z = jnp.where(
        col < Z, 1.0, jnp.where(col < Z + 4, in_zp, jnp.where(col >= ZE - 4, in_zm, 0.0))
    )
    mask = in_y * in_z

    def field(f, x):
        return ext[BASE[f] + RADIUS[f] + x]

    def in_x(x):
        return jnp.where(x < 0, in_xm, jnp.where(x >= X, in_xp, 1.0))

    def predict(i, carry):
        x = i - 3
        speed = [field(d, x) for d in range(3)]
        visc, keep = field(VISC, x), field(KEEP, x)
        for k in range(3):
            center = speed[k]
            xp, xm = field(k, x + 1), field(k, x - 1)
            yp_, ym_ = y_plus(center), y_minus(center)
            zp_, zm_ = z_plus(center), z_minus(center)
            lap = xp + xm + yp_ + ym_ + zp_ + zm_ - 6.0 * center
            conv = 0.5 * (
                speed[0] * (xp - xm) + speed[1] * (yp_ - ym_) + speed[2] * (zp_ - zm_)
            )
            pred[k, i] = keep * (center + DT * (visc * lap - conv))
        return carry

    lax.fori_loop(0, X + 6, predict, 0)

    def residual(x, interior):
        div = 0.5 * (
            pred[0, x + 4]
            - pred[0, x + 2]
            + (y_plus(pred[1, x + 3]) - y_minus(pred[1, x + 3]))
            + (z_plus(pred[2, x + 3]) - z_minus(pred[2, x + 3]))
        )
        center = field(PRES, x)
        xp, xm = field(PRES, x + 1), field(PRES, x - 1)
        yp_, ym_ = y_plus(center), y_minus(center)
        zp_, zm_ = z_plus(center), z_minus(center)
        image = (6.0 + field(RELAX, x)) * center - (xp + xm + yp_ + ym_ + zp_ + zm_)
        value = (-div / DT - image) * (mask * in_x(x))
        res[x + 2] = value
        if interior:
            keep = own(field(KEEP, x))
            for d, (p, m) in enumerate(((xp, xm), (yp_, ym_), (zp_, zm_))):
                grads[d, x] = keep * (own(pred[d, x + 3]) - DT * 0.5 * (own(p) - own(m)))
            r0_out[x] = own(value)

    def image_of(x, interior):
        center = res[x + 2]
        xp, xm = res[x + 3], res[x + 1]
        yp_, ym_ = y_plus(center), y_minus(center)
        zp_, zm_ = z_plus(center), z_minus(center)
        value = (6.0 + field(RELAX, x)) * center - (xp + xm + yp_ + ym_ + zp_ + zm_)
        value = value * (mask * in_x(x))
        img[x + 1] = value
        if interior:
            keep = own(field(KEEP, x)) * (-DT * 0.5)
            for d, (p, m) in enumerate(((xp, xm), (yp_, ym_), (zp_, zm_))):
                grads[3 + d, x] = keep * (own(p) - own(m))
            s_out[x] = own(value)

    for x in (-2, -1, X, X + 1):
        residual(x, False)
    for x in range(X):
        residual(x, True)
    for x in (-1, X):
        image_of(x, False)
    for x in range(X):
        image_of(x, True)
    sums = [jnp.zeros((Y, Z), F32) for _ in range(4)]
    for x in range(X):
        center = img[x + 1]
        xp, xm = img[x + 2], img[x]
        yp_, ym_ = y_plus(center), y_minus(center)
        zp_, zm_ = z_plus(center), z_minus(center)
        nearby = own(xp) + own(xm) + own(yp_) + own(ym_) + own(zp_) + own(zm_)
        s, r = own(center), own(res[x + 2])
        image = (6.0 + own(field(RELAX, x))) * s - nearby
        keep = own(field(KEEP, x)) * (-DT * 0.5)
        for d, (p, m) in enumerate(((xp, xm), (yp_, ym_), (zp_, zm_))):
            grads[6 + d, x] = keep * (own(p) - own(m))
        for i, (a, b) in enumerate(((r, r), (r, s), (s, s), (s, image))):
            sums[i] = sums[i] + a * b
    payload[9] = jnp.zeros((8, 128), F32)
    for i, total in enumerate(sums):
        line = jnp.sum(total[:, :128] + total[:, 128:], axis=0, keepdims=True)
        payload[9, i : i + 1] = line

    first = window_start()
    samples = grads[:, pl.ds(first, WINDOW)].reshape(9 * WINDOW * Y, Z)
    width = 256
    for c in range(host.shape[1] // width):
        cut = slice(c * width, c * width + width)
        z_weights, xy_weights = point_weights(host, off, cut, first)
        parts = lax.dot_general(
            samples,
            z_weights,
            (((1,), (0,)), ((), ())),
            precision=lax.Precision.HIGHEST,
            preferred_element_type=F32,
        ).reshape(9, WINDOW, Y, width)
        for k in range(9):
            total = parts[k, 0] * xy_weights[0]
            for l in range(1, WINDOW):
                total = total + parts[k, l] * xy_weights[l]
            line = jnp.sum(total, axis=0, keepdims=True)
            for half in range(width // 128):
                at = c * (width // 128) + half
                payload[k, at : at + 1] = line[:, half * 128 : half * 128 + 128]


def window_start():
    return jnp.where(lax.axis_index("stream") * X + X == 32, X - WINDOW, 0)


def axis_weights(host, off, d, cut, place):
    low = host[d : d + 1, cut]
    part = off[d : d + 1, cut]
    return jnp.where(place == low, 1.0 - part, 0.0) + jnp.where(place == low + 1, part, 0.0)


def point_weights(host, off, cut, first):
    width = cut.stop - cut.start
    z_place = iota((Z, width), 0) + lax.axis_index("prop") * Z
    y_place = iota((Y, width), 0) + lax.axis_index("girth") * Y
    z_weights = axis_weights(host, off, 2, cut, z_place)
    y_weights = axis_weights(host, off, 1, cut, y_place)
    x_first = lax.axis_index("stream") * X + first
    xy = [y_weights * axis_weights(host, off, 0, cut, x_first + l) for l in range(WINDOW)]
    return z_weights, xy


def final_kernel(
    total, grads, pres, r0, s, host, off, motion, coeff, velocity, pressure, points, force
):
    lines = total[9]
    rr, rs, ss, st = [jnp.sum(lines[i : i + 1], axis=1, keepdims=True) for i in range(4)]
    alpha = rr / rs
    new = rr - 2.0 * alpha * rs + alpha * alpha * ss
    beta = new / rr
    grow = 1.0 + beta
    curve = grow * grow * rs - 2.0 * grow * alpha * ss + alpha * alpha * st
    alpha2 = new / curve
    c0 = alpha + alpha2 * grow
    c1 = -alpha2 * alpha
    for k in range(3):
        value = total[k] + c0 * total[3 + k] + c1 * total[6 + k]
        for i in range(8):
            points[k : k + 1, i * 128 : i * 128 + 128] = value[i : i + 1]
    slip = points[...] - motion[...]
    speed = jnp.sqrt(jnp.sum(slip * slip, axis=0, keepdims=True) + 1.0)
    force[...] = (-DT * coeff[...] * speed) * slip
    for x in range(X):
        pressure[x] = pres[x] + c0 * r0[x] + c1 * s[x]
        for k in range(3):
            velocity[k, x] = grads[k, x] + c0 * grads[3 + k, x] + c1 * grads[6 + k, x]
    first = window_start()
    width = 256
    body = jnp.zeros((3 * WINDOW * Y, Z), F32)
    for c in range(host.shape[1] // width):
        cut = slice(c * width, c * width + width)
        z_weights, xy_weights = point_weights(host, off, cut, first)
        scaled = jnp.concatenate(
            [xy_weights[l] * force[k : k + 1, cut] for k in range(3) for l in range(WINDOW)],
            axis=0,
        )
        body = body + lax.dot_general(
            scaled,
            z_weights,
            (((1,), (1,)), ((), ())),
            precision=lax.Precision.HIGHEST,
            preferred_element_type=F32,
        )
    body = body.reshape(3, WINDOW, Y, Z)
    for k in range(3):
        for l in range(WINDOW):
            velocity[k, first + l] = velocity[k, first + l] + body[k, l]


def shift(value, steps):
    names = tuple(steps)
    sizes = [lax.axis_size(n) for n in names]
    if len(names) == 1:
        n = sizes[0]
        moves = [(i, (i + steps[names[0]]) % n) for i in range(n)]
        return lax.ppermute(value, names[0], moves)
    moves = []
    for i in range(sizes[0]):
        for j in range(sizes[1]):
            to = ((i + steps[names[0]]) % sizes[0]) * sizes[1] + (j + steps[names[1]]) % sizes[1]
            moves.append((i * sizes[1] + j, to))
    return lax.ppermute(value, names, moves)


def total_over(value, axis):
    n = lax.axis_size(axis)
    copies = jnp.broadcast_to(value[None], (n,) + value.shape)
    return jnp.sum(lax.all_to_all(copies, axis, 0, 0), axis=0)


def sds(*shape):
    return jax.ShapeDtypeStruct(shape, F32)


def call(kernel, outs, inputs, scratch=(), name=None):
    return pl.pallas_call(
        kernel,
        out_shape=outs,
        in_specs=[VMEM] * len(inputs),
        out_specs=[VMEM] * len(outs),
        scratch_shapes=scratch,
        compiler_params=PARAMS,
        name=name,
    )(*inputs)


def shards(
    velocity, eddy_visc, solid, pressure_old, relaxation, host_cell, offsets, blade_motion, force_coeff
):
    fields = (velocity, eddy_visc, solid, pressure_old, relaxation)
    points = host_cell.shape[1]
    side, unit = sds(XLAYERS, Y, Z), sds(Y, 128)
    up, down, z_up, z_down, uu, ud, du, dd = call(
        pack_kernel,
        (side, side, sds(2, Y, 128), sds(2, Y, 128), unit, unit, unit, unit),
        fields,
        name="pack",
    )
    got = (
        shift(up, {"stream": 1}),
        shift(down, {"stream": -1}),
        shift(z_up, {"prop": 1}),
        shift(z_down, {"prop": -1}),
        shift(uu, {"stream": 1, "prop": 1}),
        shift(ud, {"stream": 1, "prop": -1}),
        shift(du, {"stream": -1, "prop": 1}),
        shift(dd, {"stream": -1, "prop": -1}),
    )
    edge = sds(YTILES, 8, Z)
    y_up, y_down = call(edge_kernel, (edge, edge), fields + got, name="edges")
    ym, yp = shift(y_up, {"girth": 1}), shift(y_down, {"girth": -1})
    block = sds(X, Y, Z)
    payload, grads, r0, s = call(
        main_kernel,
        (sds(10, 8, 128), sds(9, X, Y, Z), block, block),
        fields + got + (ym, yp, host_cell, offsets),
        [
            pltpu.VMEM((LAYERS, YE, ZE), F32),
            pltpu.VMEM((3, X + 6, YE, ZE), F32),
            pltpu.VMEM((X + 4, YE, ZE), F32),
            pltpu.VMEM((X + 2, YE, ZE), F32),
        ],
        name="main",
    )
    total = payload
    for axis in ("girth", "prop", "stream"):
        total = total_over(total, axis)
    return call(
        final_kernel,
        (sds(3, X, Y, Z), block, sds(3, points)),
        (
            total,
            grads,
            pressure_old,
            r0,
            s,
            host_cell,
            offsets,
            blade_motion,
            force_coeff.reshape(1, points),
        ),
        [pltpu.VMEM((3, points), F32)],
        name="final",
    )


def solution(mesh):
    placed = (P(None, *AXES),) + (P(*AXES),) * 4 + (P(),) * 4
    return jax.shard_map(
        shards,
        mesh=mesh,
        in_specs=placed,
        out_specs=(P(None, *AXES), P(*AXES), P()),
        check_vma=False,
    )
```

time: 722 us -> 87.3 us (0.12)
  the two profiles are of different devices: /device:TPU:1 before, /device:TPU:2 now
where the time goes in v1:
time: 87.3 us; the launch traced here: 87 us
  blocking collectives  38.6 us (44%)
  starting transfers between devices  17.6 us (20%)
  waiting for transfers between devices  14.7 us (17%)
  Pallas kernels  10.6 us (12%)
  local copies, waits for them, and re-layouts  4.68 us (5%)
    all_to_all x3, blocking collectives, total_over(): return jnp.sum(lax.all_to_all(copies, axis, 0, 0), axis=0)  38.6 us
    ppermute x6, starting transfers between devices, shift(): return lax.ppermute(value, names[0], moves)  11 us
    pallas_call x4, Pallas kernels, call(): pl.pallas_call(kernel, out_shape=outs, in_specs=[VMEM] * len(inputs), out...  10.6 us
    ppermute x4, waiting for transfers between devices, shift(): return lax.ppermute(value, names, moves)  9.37 us
    ppermute x4, starting transfers between devices, shift(): return lax.ppermute(value, names, moves)  6.57 us
    ppermute x6, waiting for transfers between devices, shift(): return lax.ppermute(value, names[0], moves)  5.29 us
    unnamed x20, local copies, waits for them, and re-layouts  4.62 us
  transfers between devices with their start and end apart: 10, of which 3 were waited for; matrix products, arithmetic and copies ran while one was open for 0% of the time, Pallas kernels for 0%

profile of v1, /device:TPU:2, one launch (start us, length us, event | category | flops | bytes accessed | tf_op | source)
XLA Modules:
  0.0 87.0 jit_solution(2929047378312917659)
XLA Ops:
  0.6 0.0 copy-start
  0.6 1.0 %copy-done = f32[3,8,16,256]{3,2,1,0:T(8,128)S(1)} copy-done((f32[3,8,16,256]{3,2,1,0:T(8,128)S(1)}, f32[3,8,16,256]{3,2,1,0:T(8,128)}, u32[]{:S(2)}) %copy-start) | copy-done | bytes 393240
  1.6 0.0 copy-start.1
  1.6 0.9 %copy-done.1 = f32[8,16,256]{2,1,0:T(8,128)S(1)} copy-done((f32[8,16,256]{2,1,0:T(8,128)S(1)}, f32[8,16,256]{2,1,0:T(8,128)}, u32[]{:S(2)}) %copy-start.1) | copy-done | bytes 131096
  2.5 0.0 copy-start.3
  2.5 0.9 %copy-done.3 = f32[8,16,256]{2,1,0:T(8,128)S(1)} copy-done((f32[8,16,256]{2,1,0:T(8,128)S(1)}, f32[8,16,256]{2,1,0:T(8,128)}, u32[]{:S(2)}) %copy-start.3) | copy-done | bytes 131096
  3.4 0.0 copy-start.4
  3.4 0.9 %copy-done.4 = s32[8,16,256]{2,1,0:T(8,128)S(1)} copy-done((s32[8,16,256]{2,1,0:T(8,128)S(1)}, s32[8,16,256]{2,1,0:T(8,128)}, u32[]{:S(2)}) %copy-start.4) | copy-done | bytes 131096
  4.3 0.0 copy-start.5
  4.3 0.9 %copy-done.5 = f32[8,16,256]{2,1,0:T(8,128)S(1)} copy-done((f32[8,16,256]{2,1,0:T(8,128)S(1)}, f32[8,16,256]{2,1,0:T(8,128)}, u32[]{:S(2)}) %copy-start.5) | copy-done | bytes 131096
  5.2 0.0 copy-start.6
  5.2 0.0 copy-start.7
  5.3 0.5 pack.1
  5.8 2.0 %collective-permute-start = (f32[23,16,256]{2,1,0:T(8,128)S(1)}, f32[23,16,256]{2,1,0:T(8,128)S(1)}, u32[]{:S(2)}, u32[]{:S(2)}) collective-permute-start(f32[23,16,256]{2,1,0:T(8,128)S(1)} %get-tuple-element.17), channel_id=1, source_target_pairs={{0,32},{32,64},{64,96},{96,128},{128,160},{160,192},{192,224},{224... | collective-permute-start | bytes 1130504 | tf_op jit(solution)/shard_map/ppermute | solution.py:387
  7.7 4.0 %collective-permute-start.1 = (f32[23,16,256]{2,1,0:T(8,128)S(1)}, f32[23,16,256]{2,1,0:T(8,128)S(1)}, u32[]{:S(2)}, u32[]{:S(2)}) collective-permute-start(f32[23,16,256]{2,1,0:T(8,128)S(1)} %get-tuple-element.18), channel_id=1, source_target_pairs={{0,224},{32,0},{64,32},{96,64},{128,96},{160,128},{192,160},{224,1... | collective-permute-start | bytes 1130504 | tf_op jit(solution)/shard_map/ppermute | solution.py:387
  11.8 0.0 collective-permute-start.4
  11.8 2.0 %collective-permute-start.5 = (f32[16,128]{1,0:T(8,128)S(1)}, f32[16,128]{1,0:T(8,128)S(1)}, u32[]{:S(2)}, u32[]{:S(2)}) collective-permute-start(f32[16,128]{1,0:T(8,128)S(1)} %get-tuple-element.22), channel_id=1, source_target_pairs={{0,35},{1,32},{2,33},{3,34},{32,67},{33,64},{34,65},{35,66},{64,99... | collective-permute-start | bytes 24584 | tf_op jit(solution)/shard_map/ppermute | solution.py:393
  13.8 3.2 %collective-permute-start.6 = (f32[16,128]{1,0:T(8,128)S(1)}, f32[16,128]{1,0:T(8,128)S(1)}, u32[]{:S(2)}, u32[]{:S(2)}) collective-permute-start(f32[16,128]{1,0:T(8,128)S(1)} %get-tuple-element.23), channel_id=1, source_target_pairs={{0,225},{1,226},{2,227},{3,224},{32,1},{33,2},{34,3},{35,0},{64,33... | collective-permute-start | bytes 24584 | tf_op jit(solution)/shard_map/ppermute | solution.py:393
  17.0 6.1 %collective-permute-done.4.args_9_ = f32[16,128]{1,0:T(8,128)S(1)} collective-permute-done((f32[16,128]{1,0:T(8,128)S(1)}, f32[16,128]{1,0:T(8,128)S(1)}, u32[]{:S(2)}, u32[]{:S(2)}) %collective-permute-start.4) | collective-permute-done | bytes 8224 | tf_op jit(solution)/shard_map/ppermute | solution.py:393
  23.2 0.0 collective-permute-start.2
  23.2 0.0 collective-permute-done.5.args_10_
  23.2 3.2 %collective-permute-start.3 = (f32[2,16,128]{2,1,0:T(8,128)S(1)}, f32[2,16,128]{2,1,0:T(8,128)S(1)}, u32[]{:S(2)}, u32[]{:S(2)}) collective-permute-start(f32[2,16,128]{2,1,0:T(8,128)S(1)} %get-tuple-element.20), channel_id=1, source_target_pairs={{0,3},{1,0},{2,1},{3,2},{4,7},{5,4},{6,5},{7,6},{8,11},{9,8},{10,9... | collective-permute-start | bytes 49160 | tf_op jit(solution)/shard_map/ppermute | solution.py:387
  26.4 0.0 collective-permute-done.6.args_11_
  26.4 1.3 %collective-permute-start.7 = (f32[16,128]{1,0:T(8,128)S(1)}, f32[16,128]{1,0:T(8,128)S(1)}, u32[]{:S(2)}, u32[]{:S(2)}) collective-permute-start(f32[16,128]{1,0:T(8,128)S(1)} %get-tuple-element.24), channel_id=1, source_target_pairs={{0,227},{1,224},{2,225},{3,226},{32,3},{33,0},{34,1},{35,2},{64,35... | collective-permute-start | bytes 24584 | tf_op jit(solution)/shard_map/ppermute | solution.py:393
  27.7 3.2 %collective-permute-done.7.args_12_ = f32[16,128]{1,0:T(8,128)S(1)} collective-permute-done((f32[16,128]{1,0:T(8,128)S(1)}, f32[16,128]{1,0:T(8,128)S(1)}, u32[]{:S(2)}, u32[]{:S(2)}) %collective-permute-start.7) | collective-permute-done | bytes 8224 | tf_op jit(solution)/shard_map/ppermute | solution.py:393
  31.0 0.0 collective-permute-done.2.args_7_
  31.0 0.0 collective-permute-done.3.args_8_
  31.0 0.0 collective-permute-done.args_5_
  31.0 0.0 collective-permute-done.1.args_6_
  31.0 2.6 %edges.1 = (f32[46,8,256]{2,1,0:T(8,128)S(1)}, f32[46,8,256]{2,1,0:T(8,128)S(1)}) custom-call(f32[3,8,16,256]{3,2,1,0:T(8,128)S(1)} %copy-done, f32[8,16,256]{2,1,0:T(8,128)S(1)} %copy-done.3, s32[8,16,256]{2,1,0:T(8,128)S(1)} %copy-done.4, f32[8,16,256]{2,1,0:T(8,128)S(1)} %copy-done.1, f32[8,16,256]{2,1,0:T(8,128)S(1)} %copy-done.5, ...), custom_call_target="tpu_custom_call" | custom-call | tf_op jit(solution)/shard_map/edges/pallas_call | solution.py:407
  33.6 0.0 collective-permute-start.8
  33.6 1.7 %collective-permute-start.9 = (f32[46,8,256]{2,1,0:T(8,128)S(1)}, f32[46,8,256]{2,1,0:T(8,128)S(1)}, u32[]{:S(2)}, u32[]{:S(2)}) collective-permute-start(f32[46,8,256]{2,1,0:T(8,128)S(1)} %get-tuple-element.26), channel_id=1, source_target_pairs={{0,28},{4,0},{8,4},{12,8},{16,12},{20,16},{24,20},{28,24},{1,29},{... | collective-permute-start | bytes 1130504 | tf_op jit(solution)/shard_map/ppermute | solution.py:387
  35.4 5.3 %collective-permute-done.8.args_13_ = f32[46,8,256]{2,1,0:T(8,128)S(1)} collective-permute-done((f32[46,8,256]{2,1,0:T(8,128)S(1)}, f32[46,8,256]{2,1,0:T(8,128)S(1)}, u32[]{:S(2)}, u32[]{:S(2)}) %collective-permute-start.8) | collective-permute-done | bytes 376864 | tf_op jit(solution)/shard_map/ppermute | solution.py:387
  40.6 0.0 collective-permute-done.9.args_14_
  40.6 0.0 copy-done.6
  40.7 0.0 copy-done.7
  40.7 5.3 %main.1 = (f32[10,8,128]{2,1,0:T(8,128)S(1)}, f32[9,8,16,256]{3,2,1,0:T(8,128)S(1)}, f32[8,16,256]{2,1,0:T(8,128)S(1)}, f32[8,16,256]{2,1,0:T(8,128)S(1)}) custom-call(f32[3,8,16,256]{3,2,1,0:T(8,128)S(1)} %copy-done, f32[8,16,256]{2,1,0:T(8,128)S(1)} %copy-done.3, s32[8,16,256]{2,1,0:T(8,128)S(1)} %copy-done.4, f32[8,16,256]{2,1,0:T(8,128)S(1)} %copy-done.1, ...), custom_call_target="tpu_custom_call" | custom-call | tf_op jit(solution)/shard_map/main/pallas_call | solution.py:407
  46.0 12.5 %all_to_all.15 = f32[8,10,8,128]{3,2,1,0:T(8,128)S(1)} all-to-all(f32[8,10,8,128]{3,2,1,0:T(8,128)S(1)} %broadcast_in_dim.6), channel_id=1, replica_groups=mesh['stream'=8,'girth'=8,'prop'=4] {'girth'}, dimensions={0} | all-to-all | bytes 655360 | tf_op jit(solution)/shard_map/all_to_all | solution.py:399
  58.6 0.0 copy-start.2
  58.6 0.0 copy-start.8
  58.6 0.0 copy-start.9
  58.6 8.6 %all_to_all.16 = f32[4,10,8,128]{3,2,1,0:T(8,128)S(1)} all-to-all(f32[4,10,8,128]{3,2,1,0:T(8,128)S(1)} %broadcast_in_dim.7), channel_id=1, replica_groups=mesh['stream'=8,'girth'=8,'prop'=4] {'prop'}, dimensions={0} | all-to-all | bytes 327680 | tf_op jit(solution)/shard_map/all_to_all | solution.py:399
  67.3 17.4 %all_to_all.17 = f32[8,10,8,128]{3,2,1,0:T(8,128)S(1)} all-to-all(f32[8,10,8,128]{3,2,1,0:T(8,128)S(1)} %broadcast_in_dim.8), channel_id=1, replica_groups=mesh['stream'=8,'girth'=8,'prop'=4] {'stream'}, dimensions={0} | all-to-all | bytes 655360 | tf_op jit(solution)/shard_map/all_to_all | solution.py:399
  84.7 0.0 copy-done.2
  84.8 0.0 copy-done.8
  84.8 0.0 copy-done.9
  84.8 2.2 %final.1 = (f32[3,8,16,256]{3,2,1,0:T(8,128)}, f32[8,16,256]{2,1,0:T(8,128)}, f32[3,1024]{1,0:T(4,128)}) custom-call(f32[10,8,128]{2,1,0:T(8,128)S(1)} %reduce_sum.29.total, f32[9,8,16,256]{3,2,1,0:T(8,128)S(1)} %get-tuple-element.28.grads, f32[8,16,256]{2,1,0:T(8,128)S(1)} %copy-done.2, f32[8,16,256]{2,1,0:T(8,128)S(1)} %get-tuple-element.29.r0, ...), custom_call_target="tpu_custom_call" | custom-call | tf_op jit(solution)/shard_map/final/pallas_call | solution.py:407
  (6 shorter events, 0.1 us)
Async XLA Ops:
  0.6 1.0 %copy-start = (f32[3,8,16,256]{3,2,1,0:T(8,128)S(1)}, f32[3,8,16,256]{3,2,1,0:T(8,128)}, u32[]{:S(2)}) copy-start(f32[3,8,16,256]{3,2,1,0:T(8,128)} %args_0_.8) | copy-start | bytes 1179652
  1.6 0.9 %copy-start.1 = (f32[8,16,256]{2,1,0:T(8,128)S(1)}, f32[8,16,256]{2,1,0:T(8,128)}, u32[]{:S(2)}) copy-start(f32[8,16,256]{2,1,0:T(8,128)} %pres.1) | copy-start | bytes 393220
  2.5 0.9 %copy-start.3 = (f32[8,16,256]{2,1,0:T(8,128)S(1)}, f32[8,16,256]{2,1,0:T(8,128)}, u32[]{:S(2)}) copy-start(f32[8,16,256]{2,1,0:T(8,128)} %args_1_.8) | copy-start | bytes 393220
  3.4 0.9 %copy-start.4 = (s32[8,16,256]{2,1,0:T(8,128)S(1)}, s32[8,16,256]{2,1,0:T(8,128)}, u32[]{:S(2)}) copy-start(s32[8,16,256]{2,1,0:T(8,128)} %args_2_.8) | copy-start | bytes 393220
  4.3 0.9 %copy-start.5 = (f32[8,16,256]{2,1,0:T(8,128)S(1)}, f32[8,16,256]{2,1,0:T(8,128)}, u32[]{:S(2)}) copy-start(f32[8,16,256]{2,1,0:T(8,128)} %args_4_.8) | copy-start | bytes 393220
  5.2 35.4 %copy-start.6 = (s32[3,1024]{1,0:T(4,128)S(1)}, s32[3,1024]{1,0:T(4,128)}, u32[]{:S(2)}) copy-start(s32[3,1024]{1,0:T(4,128)} %host.1) | copy-start | bytes 36868
  5.2 35.4 %copy-start.7 = (f32[3,1024]{1,0:T(4,128)S(1)}, f32[3,1024]{1,0:T(4,128)}, u32[]{:S(2)}) copy-start(f32[3,1024]{1,0:T(4,128)} %off.1) | copy-start | bytes 36868
  5.8 25.2 %collective-permute-start = (f32[23,16,256]{2,1,0:T(8,128)S(1)}, f32[23,16,256]{2,1,0:T(8,128)S(1)}, u32[]{:S(2)}, u32[]{:S(2)}) collective-permute-start(f32[23,16,256]{2,1,0:T(8,128)S(1)} %get-tuple-element.17), channel_id=1, source_target_pairs={{0,32},{32,64},{64,96},{96,128},{128,160},{160,192},{192,224},{224... | collective-permute-start | bytes 1130504 | tf_op jit(solution)/shard_map/ppermute | solution.py:387
  7.7 23.2 %collective-permute-start.1 = (f32[23,16,256]{2,1,0:T(8,128)S(1)}, f32[23,16,256]{2,1,0:T(8,128)S(1)}, u32[]{:S(2)}, u32[]{:S(2)}) collective-permute-start(f32[23,16,256]{2,1,0:T(8,128)S(1)} %get-tuple-element.18), channel_id=1, source_target_pairs={{0,224},{32,0},{64,32},{96,64},{128,96},{160,128},{192,160},{224,1... | collective-permute-start | bytes 1130504 | tf_op jit(solution)/shard_map/ppermute | solution.py:387
  11.8 11.4 %collective-permute-start.4 = (f32[16,128]{1,0:T(8,128)S(1)}, f32[16,128]{1,0:T(8,128)S(1)}, u32[]{:S(2)}, u32[]{:S(2)}) collective-permute-start(f32[16,128]{1,0:T(8,128)S(1)} %get-tuple-element.21), channel_id=1, source_target_pairs={{0,33},{1,34},{2,35},{3,32},{32,65},{33,66},{34,67},{35,64},{64,97... | collective-permute-start | bytes 24584 | tf_op jit(solution)/shard_map/ppermute | solution.py:393
  11.8 11.4 %collective-permute-start.5 = (f32[16,128]{1,0:T(8,128)S(1)}, f32[16,128]{1,0:T(8,128)S(1)}, u32[]{:S(2)}, u32[]{:S(2)}) collective-permute-start(f32[16,128]{1,0:T(8,128)S(1)} %get-tuple-element.22), channel_id=1, source_target_pairs={{0,35},{1,32},{2,33},{3,34},{32,67},{33,64},{34,65},{35,66},{64,99... | collective-permute-start | bytes 24584 | tf_op jit(solution)/shard_map/ppermute | solution.py:393
  13.8 12.6 %collective-permute-start.6 = (f32[16,128]{1,0:T(8,128)S(1)}, f32[16,128]{1,0:T(8,128)S(1)}, u32[]{:S(2)}, u32[]{:S(2)}) collective-permute-start(f32[16,128]{1,0:T(8,128)S(1)} %get-tuple-element.23), channel_id=1, source_target_pairs={{0,225},{1,226},{2,227},{3,224},{32,1},{33,2},{34,3},{35,0},{64,33... | collective-permute-start | bytes 24584 | tf_op jit(solution)/shard_map/ppermute | solution.py:393
  23.2 7.8 %collective-permute-start.2 = (f32[2,16,128]{2,1,0:T(8,128)S(1)}, f32[2,16,128]{2,1,0:T(8,128)S(1)}, u32[]{:S(2)}, u32[]{:S(2)}) collective-permute-start(f32[2,16,128]{2,1,0:T(8,128)S(1)} %get-tuple-element.19), channel_id=1, source_target_pairs={{0,1},{1,2},{2,3},{3,0},{4,5},{5,6},{6,7},{7,4},{8,9},{9,10},{10,1... | collective-permute-start | bytes 49160 | tf_op jit(solution)/shard_map/ppermute | solution.py:387
  23.2 7.8 %collective-permute-start.3 = (f32[2,16,128]{2,1,0:T(8,128)S(1)}, f32[2,16,128]{2,1,0:T(8,128)S(1)}, u32[]{:S(2)}, u32[]{:S(2)}) collective-permute-start(f32[2,16,128]{2,1,0:T(8,128)S(1)} %get-tuple-element.20), channel_id=1, source_target_pairs={{0,3},{1,0},{2,1},{3,2},{4,7},{5,4},{6,5},{7,6},{8,11},{9,8},{10,9... | collective-permute-start | bytes 49160 | tf_op jit(solution)/shard_map/ppermute | solution.py:387
  26.4 4.6 %collective-permute-start.7 = (f32[16,128]{1,0:T(8,128)S(1)}, f32[16,128]{1,0:T(8,128)S(1)}, u32[]{:S(2)}, u32[]{:S(2)}) collective-permute-start(f32[16,128]{1,0:T(8,128)S(1)} %get-tuple-element.24), channel_id=1, source_target_pairs={{0,227},{1,224},{2,225},{3,226},{32,3},{33,0},{34,1},{35,2},{64,35... | collective-permute-start | bytes 24584 | tf_op jit(solution)/shard_map/ppermute | solution.py:393
  33.6 7.0 %collective-permute-start.8 = (f32[46,8,256]{2,1,0:T(8,128)S(1)}, f32[46,8,256]{2,1,0:T(8,128)S(1)}, u32[]{:S(2)}, u32[]{:S(2)}) collective-permute-start(f32[46,8,256]{2,1,0:T(8,128)S(1)} %get-tuple-element.25), channel_id=1, source_target_pairs={{0,4},{4,8},{8,12},{12,16},{16,20},{20,24},{24,28},{28,0},{1,5},{5... | collective-permute-start | bytes 1130504 | tf_op jit(solution)/shard_map/ppermute | solution.py:387
  33.6 7.0 %collective-permute-start.9 = (f32[46,8,256]{2,1,0:T(8,128)S(1)}, f32[46,8,256]{2,1,0:T(8,128)S(1)}, u32[]{:S(2)}, u32[]{:S(2)}) collective-permute-start(f32[46,8,256]{2,1,0:T(8,128)S(1)} %get-tuple-element.26), channel_id=1, source_target_pairs={{0,28},{4,0},{8,4},{12,8},{16,12},{20,16},{24,20},{28,24},{1,29},{... | collective-permute-start | bytes 1130504 | tf_op jit(solution)/shard_map/ppermute | solution.py:387
  58.6 26.2 %copy-start.2 = (f32[8,16,256]{2,1,0:T(8,128)S(1)}, f32[8,16,256]{2,1,0:T(8,128)}, u32[]{:S(2)}) copy-start(f32[8,16,256]{2,1,0:T(8,128)} %pres.1) | copy-start | bytes 393220
  58.6 26.2 %copy-start.8 = (f32[3,1024]{1,0:T(4,128)S(1)}, f32[3,1024]{1,0:T(4,128)}, u32[]{:S(2)}) copy-start(f32[3,1024]{1,0:T(4,128)} %motion.1) | copy-start | bytes 36868
  58.6 26.2 %copy-start.9 = (f32[1024]{0:T(1024)S(1)}, f32[1024]{0:T(1024)}, u32[]{:S(2)}) copy-start(f32[1024]{0:T(1024)} %param.17) | copy-start | bytes 12292

commit v2 on v1

v2 whole, which is shorter than its diff:
```python
import jax
import jax.numpy as jnp
from jax import lax
from jax.experimental import pallas as pl
from jax.experimental.pallas import tpu as pltpu
from jax.sharding import Mesh, PartitionSpec as P

DT = 0.1
F32 = jnp.float32

X, Y, Z = 8, 16, 256
YE, ZE = 24, 384
VISC, KEEP, PRES, RELAX = 3, 4, 5, 6
FIELDS = 7
RADIUS = (4, 3, 3, 3, 3, 3, 2)
XLAYERS = [(f, d) for f in range(FIELDS) for d in range(1, RADIUS[f] + 1)]
CORNER = (3, 3, 3, 2, 2, 2, 1)
RELAYED = [(f, d) for f in range(FIELDS) for d in range(1, CORNER[f] + 1)]
YPAIRS = FIELDS * X // 2
YTILES = YPAIRS + 1
RTILES = len(RELAYED) + 2
WINDOW = 3
VMEM = pl.BlockSpec(memory_space=pltpu.VMEM)
PARAMS = pltpu.CompilerParams(vmem_limit_bytes=48 * 1024 * 1024)


def iota(shape, dim):
    return lax.broadcasted_iota(jnp.int32, shape, dim)


def roll(a, shift, axis):
    shift = shift % a.shape[axis]
    return a if shift == 0 else pltpu.roll(a, shift, axis)


def halves(width=Z):
    return [slice(i, i + 128) for i in range(0, width, 128)]


def pack_kernel(
    velocity, visc, solid, pres, relax, own_out, up, down, z_up, z_down, stage, sems
):
    copies = [
        pltpu.make_async_copy(velocity, own_out.at[:3], sems.at[0]),
        pltpu.make_async_copy(visc, own_out.at[VISC], sems.at[1]),
        pltpu.make_async_copy(solid, stage, sems.at[2]),
        pltpu.make_async_copy(pres, own_out.at[PRES], sems.at[3]),
        pltpu.make_async_copy(relax, own_out.at[RELAX], sems.at[4]),
    ]
    for copy in copies:
        copy.start()
    for copy in copies:
        copy.wait()
    own_out[KEEP] = 1.0 - stage[...].astype(F32)
    slot = iota((Y, 128), 1) // 4
    for unit in range(2):
        high = jnp.zeros((Y, 128), F32)
        low = jnp.zeros((Y, 128), F32)
        for j in range(32):
            q = unit * 32 + j
            if q < FIELDS * X:
                f, x = divmod(q, X)
                high = jnp.where(slot == j, roll(own_out[f, x, :, Z - 128 :], 4 * j - 124, 1), high)
                low = jnp.where(slot == j, roll(own_out[f, x, :, :128], 4 * j, 1), low)
        z_up[unit] = high
        z_down[unit] = low
    for i, (f, d) in enumerate(XLAYERS):
        up[i] = own_out[f, X - d]
        down[i] = own_out[f, d - 1]


def position():
    return (
        lax.axis_index("stream"),
        lax.axis_index("gx") * 2 + lax.axis_index("core"),
        lax.axis_index("prop"),
    )


def inside_flags():
    out = []
    for i, n in zip(position(), (8, 8, 4)):
        out.append((i > 0).astype(F32))
        out.append((i < n - 1).astype(F32))
    return out


def third_reader(zm, zp):
    in_zm, in_zp = inside_flags()[4:]
    lane = iota((Y, 128), 1)
    right = (lane < 4).astype(F32) * in_zp
    left = (lane >= 124).astype(F32) * in_zm

    def third(f, x):
        unit, j = divmod(f * X + x, 32)
        return roll(zp[unit], -4 * j, 1) * right + roll(zm[unit], 124 - 4 * j, 1) * left

    return third


def edge_kernel(fields, zm, zp, to_up, to_down):
    third = third_reader(zm, zp)
    low_rows = iota((8, 128), 0) < 4
    slot = iota((8, 128), 1) // 8
    highs = [jnp.zeros((8, 128), F32) for _ in range(2)]
    lows = [jnp.zeros((8, 128), F32) for _ in range(2)]

    def pair(a, b):
        high = jnp.where(low_rows, roll(a[8:], 4, 0), b[8:])
        low = jnp.where(low_rows, a[:8], roll(b[:8], 4, 0))
        return high, low

    for t in range(YPAIRS):
        f, x = divmod(2 * t, X)
        for cut in halves():
            to_up[t, :, cut], to_down[t, :, cut] = pair(fields[f, x, :, cut], fields[f, x + 1, :, cut])
        high, low = pair(third(f, x), third(f, x + 1))
        unit, j = divmod(t, 16)
        highs[unit] = jnp.where(slot == j, roll(high, 8 * j + 4, 1), highs[unit])
        lows[unit] = jnp.where(slot == j, roll(low, 8 * j + 4, 1), lows[unit])
    for unit, cut in enumerate(halves()):
        to_up[YPAIRS, :, cut] = highs[unit]
        to_down[YPAIRS, :, cut] = lows[unit]


def block_kernel(fields, zm, zp, ym, yp, ext, to_up, to_down):
    third = third_reader(zm, zp)
    _, _, in_ym, in_yp, _, _ = inside_flags()
    low_rows = iota((8, 128), 0) < 4
    slot = iota((8, 128), 1) // 8
    lane = iota((8, 128), 1)
    ends = ((lane < 4) | (lane >= 124)).astype(F32)

    def rows(t, cut, odd):
        plus, minus = yp[t, :, cut] * in_yp, ym[t, :, cut] * in_ym
        if odd:
            return jnp.where(low_rows, roll(plus, 4, 0), minus)
        return jnp.where(low_rows, plus, roll(minus, 4, 0))

    for f in range(FIELDS):
        for x in range(X):
            t, odd = divmod(f * X + x, 2)
            ext[f, x, :Y, :Z] = fields[f, x]
            ext[f, x, :Y, Z:] = third(f, x)
            for cut in halves():
                ext[f, x, Y:, cut] = rows(t, cut, odd)
            unit, j = divmod(t, 16)
            packed = rows(YPAIRS, halves()[unit], odd)
            ext[f, x, Y:, Z:] = roll(packed, -8 * j - 4, 1) * ends
    for up, out in ((True, to_up), (False, to_down)):
        units = [jnp.zeros((8, 128), F32) for _ in range(4)]
        for i, (f, d) in enumerate(RELAYED):
            x = X - d if up else d - 1
            out[i] = ext[f, x, Y:, :Z]
            for h in range(3):
                unit, j = divmod(3 * i + h, 16)
                tile = roll(ext[f, x, 8 * h : 8 * h + 8, Z:], 8 * j + 4, 1)
                units[unit] = jnp.where(slot == j, tile, units[unit])
        for unit in range(4):
            out[len(RELAYED) + unit // 2, :, halves()[unit % 2]] = units[unit]


def y_plus(a):
    return roll(a, -1, 0)


def y_minus(a):
    return roll(a, 1, 0)


def z_plus(a):
    return roll(a, -1, 1)


def z_minus(a):
    return roll(a, 1, 1)


def own(a):
    return a[:Y, :Z]


def main_kernel(
    ext, xm, xp, rm, rp, host, off, keep_half, send_half, grads, r0_out, s_out, *scratch
):
    halo, pred, res, img, payload = scratch
    in_xm, in_xp, in_ym, in_yp, in_zm, in_zp = inside_flags()

    lane = iota((8, 128), 1)
    ends = ((lane < 4) | (lane >= 124)).astype(F32)
    for side, (edge, relay, flag) in enumerate(((xm, rm, in_xm), (xp, rp, in_xp))):
        for i, layer in enumerate(XLAYERS):
            halo[side, i, :Y, :Z] = edge[i] * flag
            if layer not in RELAYED:
                halo[side, i, :Y, Z:] = jnp.zeros((Y, 128), F32)
                halo[side, i, Y:] = jnp.zeros((8, ZE), F32)
                continue
            n = RELAYED.index(layer)
            halo[side, i, Y:, :Z] = relay[n] * flag
            for h in range(3):
                unit, j = divmod(3 * n + h, 16)
                packed = relay[len(RELAYED) + unit // 2, :, halves()[unit % 2]]
                halo[side, i, 8 * h : 8 * h + 8, Z:] = roll(packed, -8 * j - 4, 1) * (ends * flag)

    row, col = iota((YE, ZE), 0), iota((YE, ZE), 1)
    in_y = jnp.where(row < Y, 1.0, jnp.where(row < Y + 4, in_yp, in_ym))
    in_z = jnp.where(
        col < Z, 1.0, jnp.where(col < Z + 4, in_zp, jnp.where(col >= ZE - 4, in_zm, 0.0))
    )
    mask = in_y * in_z

    def field(f, x):
        if x < 0:
            return halo[0, XLAYERS.index((f, -x))]
        if x >= X:
            return halo[1, XLAYERS.index((f, x - X + 1))]
        return ext[f, x]

    def in_x(x):
        return in_xm if x < 0 else in_xp if x >= X else 1.0

    for x in range(-3, X + 3):
        speed = [field(d, x) for d in range(3)]
        visc, keep = field(VISC, x), field(KEEP, x)
        for k in range(3 if -3 < x < X + 2 else 1):
            center = speed[k]
            xp_, xm_ = field(k, x + 1), field(k, x - 1)
            yp_, ym_ = y_plus(center), y_minus(center)
            zp_, zm_ = z_plus(center), z_minus(center)
            lap = xp_ + xm_ + yp_ + ym_ + zp_ + zm_ - 6.0 * center
            conv = 0.5 * (
                speed[0] * (xp_ - xm_) + speed[1] * (yp_ - ym_) + speed[2] * (zp_ - zm_)
            )
            pred[k, x + 3] = keep * (center + DT * (visc * lap - conv))

    def residual(x, interior):
        div = 0.5 * (
            pred[0, x + 4]
            - pred[0, x + 2]
            + (y_plus(pred[1, x + 3]) - y_minus(pred[1, x + 3]))
            + (z_plus(pred[2, x + 3]) - z_minus(pred[2, x + 3]))
        )
        center = field(PRES, x)
        xp, xm = field(PRES, x + 1), field(PRES, x - 1)
        yp_, ym_ = y_plus(center), y_minus(center)
        zp_, zm_ = z_plus(center), z_minus(center)
        image = (6.0 + field(RELAX, x)) * center - (xp + xm + yp_ + ym_ + zp_ + zm_)
        value = (-div / DT - image) * (mask * in_x(x))
        res[x + 2] = value
        if interior:
            keep = own(field(KEEP, x))
            for d, (p, m) in enumerate(((xp, xm), (yp_, ym_), (zp_, zm_))):
                grads[d, x] = keep * (own(pred[d, x + 3]) - DT * 0.5 * (own(p) - own(m)))
            r0_out[x] = own(value)

    def image_of(x, interior):
        center = res[x + 2]
        xp, xm = res[x + 3], res[x + 1]
        yp_, ym_ = y_plus(center), y_minus(center)
        zp_, zm_ = z_plus(center), z_minus(center)
        value = (6.0 + field(RELAX, x)) * center - (xp + xm + yp_ + ym_ + zp_ + zm_)
        value = value * (mask * in_x(x))
        img[x + 1] = value
        if interior:
            keep = own(field(KEEP, x)) * (-DT * 0.5)
            for d, (p, m) in enumerate(((xp, xm), (yp_, ym_), (zp_, zm_))):
                grads[3 + d, x] = keep * (own(p) - own(m))
            s_out[x] = own(value)

    for x in (-2, -1, X, X + 1):
        residual(x, False)
    for x in range(X):
        residual(x, True)
    for x in (-1, X):
        image_of(x, False)
    for x in range(X):
        image_of(x, True)
    sums = [jnp.zeros((Y, Z), F32) for _ in range(4)]
    for x in range(X):
        center = img[x + 1]
        xp, xm = img[x + 2], img[x]
        yp_, ym_ = y_plus(center), y_minus(center)
        zp_, zm_ = z_plus(center), z_minus(center)
        nearby = own(xp) + own(xm) + own(yp_) + own(ym_) + own(zp_) + own(zm_)
        s, r = own(center), own(res[x + 2])
        image = (6.0 + own(field(RELAX, x))) * s - nearby
        keep = own(field(KEEP, x)) * (-DT * 0.5)
        for d, (p, m) in enumerate(((xp, xm), (yp_, ym_), (zp_, zm_))):
            grads[6 + d, x] = keep * (own(p) - own(m))
        for i, (a, b) in enumerate(((r, r), (r, s), (s, s), (s, image))):
            sums[i] = sums[i] + a * b
    payload[9] = jnp.zeros((8, 128), F32)
    for i, total in enumerate(sums):
        line = jnp.sum(total[:, :128] + total[:, 128:], axis=0, keepdims=True)
        payload[9, i : i + 1] = line

    first = window_start()
    samples = grads[:, pl.ds(first, WINDOW)].reshape(9 * WINDOW * Y, Z)
    width = 256
    for c in range(host.shape[1] // width):
        cut = slice(c * width, c * width + width)
        z_weights, xy_weights = point_weights(host, off, cut, first)
        parts = lax.dot_general(
            samples,
            z_weights,
            (((1,), (0,)), ((), ())),
            precision=lax.Precision.HIGHEST,
            preferred_element_type=F32,
        ).reshape(9, WINDOW, Y, width)
        for k in range(9):
            total = parts[k, 0] * xy_weights[0]
            for l in range(1, WINDOW):
                total = total + parts[k, l] * xy_weights[l]
            line = jnp.sum(total, axis=0, keepdims=True)
            for half in range(width // 128):
                at = c * (width // 128) + half
                payload[k, at : at + 1] = line[:, half * 128 : half * 128 + 128]
    second = lax.axis_index("core") == 1
    for k in range(5):
        keep_half[k] = jnp.where(second, payload[5 + k], payload[k])
        send_half[k] = jnp.where(second, payload[k], payload[5 + k])


def window_start():
    return jnp.where(lax.axis_index("stream") * X + X == 32, X - WINDOW, 0)


def axis_weights(host, off, d, cut, place):
    low = host[d : d + 1, cut]
    part = off[d : d + 1, cut]
    return jnp.where(place == low, 1.0 - part, 0.0) + jnp.where(place == low + 1, part, 0.0)


def point_weights(host, off, cut, first):
    width = cut.stop - cut.start
    z_place = iota((Z, width), 0) + lax.axis_index("prop") * Z
    y_place = iota((Y, width), 0) + position()[1] * Y
    z_weights = axis_weights(host, off, 2, cut, z_place)
    y_weights = axis_weights(host, off, 1, cut, y_place)
    x_first = lax.axis_index("stream") * X + first
    xy = [y_weights * axis_weights(host, off, 0, cut, x_first + l) for l in range(WINDOW)]
    return z_weights, xy


def final_kernel(
    mine, other, fields, grads, r0, s, host, off, motion, coeff, velocity, pressure, points, force
):
    second = lax.axis_index("core") == 1
    total = [jnp.where(second, other[k], mine[k]) for k in range(5)]
    total += [jnp.where(second, mine[k], other[k]) for k in range(5)]
    lines = total[9]
    rr, rs, ss, st = [jnp.sum(lines[i : i + 1], axis=1, keepdims=True) for i in range(4)]
    alpha = rr / rs
    new = rr - 2.0 * alpha * rs + alpha * alpha * ss
    beta = new / rr
    grow = 1.0 + beta
    curve = grow * grow * rs - 2.0 * grow * alpha * ss + alpha * alpha * st
    alpha2 = new / curve
    c0 = alpha + alpha2 * grow
    c1 = -alpha2 * alpha
    for k in range(3):
        value = total[k] + c0 * total[3 + k] + c1 * total[6 + k]
        for i in range(8):
            points[k : k + 1, i * 128 : i * 128 + 128] = value[i : i + 1]
    slip = points[...] - motion[...]
    speed = jnp.sqrt(jnp.sum(slip * slip, axis=0, keepdims=True) + 1.0)
    force[...] = (-DT * coeff[...] * speed) * slip
    for x in range(X):
        pressure[x] = fields[PRES, x] + c0 * r0[x] + c1 * s[x]
        for k in range(3):
            velocity[k, x] = grads[k, x] + c0 * grads[3 + k, x] + c1 * grads[6 + k, x]
    first = window_start()
    width = 256
    body = jnp.zeros((3 * WINDOW * Y, Z), F32)
    for c in range(host.shape[1] // width):
        cut = slice(c * width, c * width + width)
        z_weights, xy_weights = point_weights(host, off, cut, first)
        scaled = jnp.concatenate(
            [xy_weights[l] * force[k : k + 1, cut] for k in range(3) for l in range(WINDOW)],
            axis=0,
        )
        body = body + lax.dot_general(
            scaled,
            z_weights,
            (((1,), (1,)), ((), ())),
            precision=lax.Precision.HIGHEST,
            preferred_element_type=F32,
        )
    body = body.reshape(3, WINDOW, Y, Z)
    for k in range(3):
        for l in range(WINDOW):
            velocity[k, first + l] = velocity[k, first + l] + body[k, l]


def shift(value, axis, step):
    names = axis if isinstance(axis, tuple) else (axis,)
    n = 1
    for name in names:
        n *= lax.axis_size(name)
    return lax.ppermute(value, axis, [(i, (i + step) % n) for i in range(n)])


def total_over(value, axis, n):
    copies = jnp.broadcast_to(value[None], (n,) + value.shape)
    return jnp.sum(lax.all_to_all(copies, axis, 0, 0), axis=0)


def sds(*shape):
    return jax.ShapeDtypeStruct(shape, F32)


def call(kernel, outs, inputs, scratch=(), name=None, space=None):
    return pl.pallas_call(
        kernel,
        out_shape=outs,
        in_specs=[pl.BlockSpec(memory_space=space or pltpu.VMEM)] * len(inputs),
        out_specs=[VMEM] * len(outs),
        scratch_shapes=scratch,
        compiler_params=PARAMS,
        name=name,
    )(*inputs)


def shards(
    velocity, eddy_visc, solid, pressure_old, relaxation, host_cell, offsets, blade_motion, force_coeff
):
    points = host_cell.shape[1]
    girth = ("gx", "core")
    block, side, unit = sds(X, Y, Z), sds(len(XLAYERS), Y, Z), sds(2, Y, 128)
    fields, up, down, z_up, z_down = call(
        pack_kernel,
        (sds(FIELDS, X, Y, Z), side, side, unit, unit),
        (velocity, eddy_visc, solid, pressure_old, relaxation),
        [pltpu.VMEM((X, Y, Z), jnp.int32), pltpu.SemaphoreType.DMA((5,))],
        name="pack",
        space=pltpu.HBM,
    )
    zm, zp = shift(z_up, "prop", 1), shift(z_down, "prop", -1)
    xm, xp = shift(up, "stream", 1), shift(down, "stream", -1)
    edge = sds(YTILES, 8, Z)
    y_up, y_down = call(edge_kernel, (edge, edge), (fields, zm, zp), name="edges")
    ym, yp = shift(y_up, girth, 1), shift(y_down, girth, -1)
    relay = sds(RTILES, 8, Z)
    ext, r_up, r_down = call(
        block_kernel,
        (sds(FIELDS, X, YE, ZE), relay, relay),
        (fields, zm, zp, ym, yp),
        name="block",
    )
    rm, rp = shift(r_up, "stream", 1), shift(r_down, "stream", -1)
    half = sds(5, 8, 128)
    kept, sent, grads, r0, s = call(
        main_kernel,
        (half, half, sds(9, X, Y, Z), block, block),
        (ext, xm, xp, rm, rp, host_cell, offsets),
        [
            pltpu.VMEM((2, len(XLAYERS), YE, ZE), F32),
            pltpu.VMEM((3, X + 6, YE, ZE), F32),
            pltpu.VMEM((X + 4, YE, ZE), F32),
            pltpu.VMEM((X + 2, YE, ZE), F32),
            pltpu.VMEM((10, 8, 128), F32),
        ],
        name="main",
    )
    mine = kept + shift(sent, "core", 1)
    mine = total_over(mine, ("gx", "prop"), 16)
    mine = total_over(mine, "stream", 8)
    other = shift(mine, "core", 1)
    return call(
        final_kernel,
        (sds(3, X, Y, Z), block, sds(3, points)),
        (
            mine,
            other,
            fields,
            grads,
            r0,
            s,
            host_cell,
            offsets,
            blade_motion,
            force_coeff.reshape(1, points),
        ),
        [pltpu.VMEM((3, points), F32)],
        name="final",
    )


def solution(mesh):
    cut = Mesh(mesh.devices.reshape(8, 4, 2, 4), ("stream", "gx", "core", "prop"))
    cells = ("stream", ("gx", "core"), "prop")
    placed = (P(None, *cells),) + (P(*cells),) * 4 + (P(),) * 4
    return jax.shard_map(
        shards,
        mesh=cut,
        in_specs=placed,
        out_specs=(P(None, *cells), P(*cells), P()),
        check_vma=False,
    )
```

time: 87.3 us -> 73.2 us (0.84)
  the two profiles are of different devices: /device:TPU:2 before, /device:TPU:1 now
where the time goes in v2:
time: 73.2 us; the launch traced here: 73 us
  blocking collectives  27.7 us (38%)
  starting transfers between devices  23.2 us (32%)
  Pallas kernels  9.32 us (13%)
  waiting for transfers between devices  7.38 us (10%)
  local copies, waits for them, and re-layouts  4.66 us (6%)
    all_to_all x2, blocking collectives, total_over(): return jnp.sum(lax.all_to_all(copies, axis, 0, 0), axis=0)  27.7 us
    ppermute x10, starting transfers between devices, shift(): return lax.ppermute(value, axis, [(i, (i + step) % n) for i in range(n)])  23.2 us
    pallas_call x5, Pallas kernels, call(): pl.pallas_call(kernel, out_shape=outs, in_specs=[pl.BlockSpec(memory_spac...  9.32 us
    ppermute x10, waiting for transfers between devices, shift(): return lax.ppermute(value, axis, [(i, (i + step) % n) for i in range(n)])  7.38 us
    unnamed x18, local copies, waits for them, and re-layouts  4.62 us
  transfers between devices with their start and end apart: 10, of which 5 were waited for; matrix products, arithmetic and copies ran while one was open for 0% of the time, Pallas kernels for 1%

profile of v2, /device:TPU:1, one launch (start us, length us, event | category | flops | bytes accessed | tf_op | source)
XLA Modules:
  0.0 73.0 jit_solution(5235236260900889333)
XLA Ops:
  0.6 0.0 copy-start
  0.6 1.0 %copy-done = f32[3,8,16,256]{3,2,1,0:T(8,128)S(1)} copy-done((f32[3,8,16,256]{3,2,1,0:T(8,128)S(1)}, f32[3,8,16,256]{3,2,1,0:T(8,128)}, u32[]{:S(2)}) %copy-start) | copy-done | bytes 393240
  1.6 0.0 copy-start.1
  1.6 0.9 %copy-done.1 = f32[8,16,256]{2,1,0:T(8,128)S(1)} copy-done((f32[8,16,256]{2,1,0:T(8,128)S(1)}, f32[8,16,256]{2,1,0:T(8,128)}, u32[]{:S(2)}) %copy-start.1) | copy-done | bytes 131096
  2.5 0.0 copy-start.2
  2.5 0.9 %copy-done.2 = s32[8,16,256]{2,1,0:T(8,128)S(1)} copy-done((s32[8,16,256]{2,1,0:T(8,128)S(1)}, s32[8,16,256]{2,1,0:T(8,128)}, u32[]{:S(2)}) %copy-start.2) | copy-done | bytes 131096
  3.4 0.0 copy-start.3
  3.4 0.9 %copy-done.3 = f32[8,16,256]{2,1,0:T(8,128)S(1)} copy-done((f32[8,16,256]{2,1,0:T(8,128)S(1)}, f32[8,16,256]{2,1,0:T(8,128)}, u32[]{:S(2)}) %copy-start.3) | copy-done | bytes 131096
  4.3 0.0 copy-start.4
  4.3 0.9 %copy-done.4 = f32[8,16,256]{2,1,0:T(8,128)S(1)} copy-done((f32[8,16,256]{2,1,0:T(8,128)S(1)}, f32[8,16,256]{2,1,0:T(8,128)}, u32[]{:S(2)}) %copy-start.4) | copy-done | bytes 131096
  5.2 0.0 copy-start.5
  5.3 0.0 copy-start.6
  5.3 1.2 %pack.1 = (f32[7,8,16,256]{3,2,1,0:T(8,128)S(1)}, f32[21,16,256]{2,1,0:T(8,128)S(1)}, f32[21,16,256]{2,1,0:T(8,128)S(1)}, f32[2,16,128]{2,1,0:T(8,128)S(1)}, f32[2,16,128]{2,1,0:T(8,128)S(1)}) custom-call(f32[3,8,16,256]{3,2,1,0:T(8,128)S(1)} %copy-done, f32[8,16,256]{2,1,0:T(8,128)S(1)} %copy-done.1, s32[8,16,256]{2,1,0:T(8,128)S(1)} %copy-done.2, ...), custom_call_target="tpu_custom_call" | custom-call | tf_op jit(solution)/shard_map/pack/pallas_call | solution.py:413
  6.5 2.2 %collective-permute-start = (f32[2,16,128]{2,1,0:T(8,128)S(1)}, f32[2,16,128]{2,1,0:T(8,128)S(1)}, u32[]{:S(2)}, u32[]{:S(2)}) collective-permute-start(f32[2,16,128]{2,1,0:T(8,128)S(1)} %get-tuple-element.19), channel_id=1, source_target_pairs={{0,1},{1,2},{2,3},{3,0},{4,5},{5,6},{6,7},{7,4},{8,9},{9,10},{10,1... | collective-permute-start | bytes 49160 | tf_op jit(solution)/shard_map/ppermute | solution.py:400
  8.7 1.5 %collective-permute-start.1 = (f32[2,16,128]{2,1,0:T(8,128)S(1)}, f32[2,16,128]{2,1,0:T(8,128)S(1)}, u32[]{:S(2)}, u32[]{:S(2)}) collective-permute-start(f32[2,16,128]{2,1,0:T(8,128)S(1)} %get-tuple-element.20), channel_id=1, source_target_pairs={{0,3},{1,0},{2,1},{3,2},{4,7},{5,4},{6,5},{7,6},{8,11},{9,8},{10,9... | collective-permute-start | bytes 49160 | tf_op jit(solution)/shard_map/ppermute | solution.py:400
  10.2 1.0 %collective-permute-done.zm = f32[2,16,128]{2,1,0:T(8,128)S(1)} collective-permute-done((f32[2,16,128]{2,1,0:T(8,128)S(1)}, f32[2,16,128]{2,1,0:T(8,128)S(1)}, u32[]{:S(2)}, u32[]{:S(2)}) %collective-permute-start) | collective-permute-done | bytes 16416 | tf_op jit(solution)/shard_map/ppermute | solution.py:400
  11.3 0.0 collective-permute-done.1.zp
  11.3 1.3 %edges.1 = (f32[29,8,256]{2,1,0:T(8,128)S(1)}, f32[29,8,256]{2,1,0:T(8,128)S(1)}) custom-call(f32[7,8,16,256]{3,2,1,0:T(8,128)S(1)} %get-tuple-element.18.fields, f32[2,16,128]{2,1,0:T(8,128)S(1)} %collective-permute-done.zm, f32[2,16,128]{2,1,0:T(8,128)S(1)} %collective-permute-done.1.zp), custom_call_target="tpu_custom_call" | custom-call | tf_op jit(solution)/shard_map/edges/pallas_call | solution.py:413
  12.6 3.2 %collective-permute-start.2 = (f32[29,8,256]{2,1,0:T(8,128)S(1)}, f32[29,8,256]{2,1,0:T(8,128)S(1)}, u32[]{:S(2)}, u32[]{:S(2)}) collective-permute-start(f32[29,8,256]{2,1,0:T(8,128)S(1)} %get-tuple-element.21), channel_id=1, source_target_pairs={{0,4},{4,8},{8,12},{12,16},{16,20},{20,24},{24,28},{28,0},{1,5},{5... | collective-permute-start | bytes 712712 | tf_op jit(solution)/shard_map/ppermute | solution.py:400
  15.8 0.3 collective-permute-start.3
  16.1 1.3 %collective-permute-start.4 = (f32[21,16,256]{2,1,0:T(8,128)S(1)}, f32[21,16,256]{2,1,0:T(8,128)S(1)}, u32[]{:S(2)}, u32[]{:S(2)}) collective-permute-start(f32[21,16,256]{2,1,0:T(8,128)S(1)} %get-tuple-element.24), channel_id=1, source_target_pairs={{0,32},{32,64},{64,96},{96,128},{128,160},{160,192},{192,224},{224... | collective-permute-start | bytes 1032200 | tf_op jit(solution)/shard_map/ppermute | solution.py:400
  17.5 3.9 %collective-permute-start.5 = (f32[21,16,256]{2,1,0:T(8,128)S(1)}, f32[21,16,256]{2,1,0:T(8,128)S(1)}, u32[]{:S(2)}, u32[]{:S(2)}) collective-permute-start(f32[21,16,256]{2,1,0:T(8,128)S(1)} %get-tuple-element.25), channel_id=1, source_target_pairs={{0,224},{32,0},{64,32},{96,64},{128,96},{160,128},{192,160},{224,1... | collective-permute-start | bytes 1032200 | tf_op jit(solution)/shard_map/ppermute | solution.py:400
  21.4 0.0 collective-permute-done.2.ym
  21.4 0.2 collective-permute-done.3.yp
  21.7 0.5 block.1
  22.2 1.7 %collective-permute-start.6 = (f32[18,8,256]{2,1,0:T(8,128)S(1)}, f32[18,8,256]{2,1,0:T(8,128)S(1)}, u32[]{:S(2)}, u32[]{:S(2)}) collective-permute-start(f32[18,8,256]{2,1,0:T(8,128)S(1)} %get-tuple-element.26), channel_id=1, source_target_pairs={{0,32},{32,64},{64,96},{96,128},{128,160},{160,192},{192,224},{224... | collective-permute-start | bytes 442376 | tf_op jit(solution)/shard_map/ppermute | solution.py:400
  23.9 4.0 %collective-permute-start.7 = (f32[18,8,256]{2,1,0:T(8,128)S(1)}, f32[18,8,256]{2,1,0:T(8,128)S(1)}, u32[]{:S(2)}, u32[]{:S(2)}) collective-permute-start(f32[18,8,256]{2,1,0:T(8,128)S(1)} %get-tuple-element.27), channel_id=1, source_target_pairs={{0,224},{32,0},{64,32},{96,64},{128,96},{160,128},{192,160},{224,1... | collective-permute-start | bytes 442376 | tf_op jit(solution)/shard_map/ppermute | solution.py:400
  27.9 0.0 collective-permute-done.4.xm
  27.9 0.0 collective-permute-done.5.xp
  27.9 4.4 %collective-permute-done.6.rm = f32[18,8,256]{2,1,0:T(8,128)S(1)} collective-permute-done((f32[18,8,256]{2,1,0:T(8,128)S(1)}, f32[18,8,256]{2,1,0:T(8,128)S(1)}, u32[]{:S(2)}, u32[]{:S(2)}) %collective-permute-start.6) | collective-permute-done | bytes 147488 | tf_op jit(solution)/shard_map/ppermute | solution.py:400
  32.3 0.0 collective-permute-done.7.rp
  32.3 0.0 copy-done.5
  32.3 0.0 copy-done.6
  32.3 0.0 copy-start.7
  32.3 0.0 copy-start.8
  32.3 4.0 %main.1 = (f32[5,8,128]{2,1,0:T(8,128)S(1)}, f32[5,8,128]{2,1,0:T(8,128)S(1)}, f32[9,8,16,256]{3,2,1,0:T(8,128)S(1)}, f32[8,16,256]{2,1,0:T(8,128)S(1)}, f32[8,16,256]{2,1,0:T(8,128)S(1)}) custom-call(f32[7,8,24,384]{3,2,1,0:T(8,128)S(1)} %get-tuple-element.23.ext, f32[21,16,256]{2,1,0:T(8,128)S(1)} %collective-permute-done.4.xm, ...), custom_call_target="tpu_custom_call" | custom-call | tf_op jit(solution)/shard_map/main/pallas_call | solution.py:413
  36.4 1.4 %collective-permute-start.8 = (f32[5,8,128]{2,1,0:T(8,128)S(1)}, f32[5,8,128]{2,1,0:T(8,128)S(1)}, u32[]{:S(2)}, u32[]{:S(2)}) collective-permute-start(f32[5,8,128]{2,1,0:T(8,128)S(1)} %get-tuple-element.29), channel_id=1, source_target_pairs={{0,4},{4,0},{1,5},{5,1},{2,6},{6,2},{3,7},{7,3},{8,12},{12,8},{9,1... | collective-permute-start | bytes 61448 | tf_op jit(solution)/shard_map/ppermute | solution.py:400
  37.7 0.8 %collective-permute-done.8 = f32[5,8,128]{2,1,0:T(8,128)S(1)} collective-permute-done((f32[5,8,128]{2,1,0:T(8,128)S(1)}, f32[5,8,128]{2,1,0:T(8,128)S(1)}, u32[]{:S(2)}, u32[]{:S(2)}) %collective-permute-start.8) | collective-permute-done | bytes 20512 | tf_op jit(solution)/shard_map/ppermute | solution.py:400
  38.6 13.9 %all_to_all.10 = f32[16,5,8,128]{3,2,1,0:T(8,128)S(1)} all-to-all(f32[16,5,8,128]{3,2,1,0:T(8,128)S(1)} %broadcast_in_dim.4), channel_id=1, replica_groups=mesh['stream'=8,'gx'=4,'core'=2,'prop'=4] {'gx','prop'}, dimensions={0} | all-to-all | bytes 655360 | tf_op jit(solution)/shard_map/all_to_all | solution.py:405
  52.6 13.7 %all_to_all.11 = f32[8,5,8,128]{3,2,1,0:T(8,128)S(1)} all-to-all(f32[8,5,8,128]{3,2,1,0:T(8,128)S(1)} %broadcast_in_dim.5), channel_id=1, replica_groups=mesh['stream'=8,'gx'=4,'core'=2,'prop'=4] {'stream'}, dimensions={0} | all-to-all | bytes 327680 | tf_op jit(solution)/shard_map/all_to_all | solution.py:405
  66.4 3.6 %collective-permute-start.9 = (f32[5,8,128]{2,1,0:T(8,128)S(1)}, f32[5,8,128]{2,1,0:T(8,128)S(1)}, u32[]{:S(2)}, u32[]{:S(2)}) collective-permute-start(f32[5,8,128]{2,1,0:T(8,128)S(1)} %reduce_sum.19.mine), channel_id=1, source_target_pairs={{0,4},{4,0},{1,5},{5,1},{2,6},{6,2},{3,7},{7,3},{8,12},{12,8},{9,1... | collective-permute-start | bytes 61448 | tf_op jit(solution)/shard_map/ppermute | solution.py:400
  69.9 0.8 %collective-permute-done.9.other = f32[5,8,128]{2,1,0:T(8,128)S(1)} collective-permute-done((f32[5,8,128]{2,1,0:T(8,128)S(1)}, f32[5,8,128]{2,1,0:T(8,128)S(1)}, u32[]{:S(2)}, u32[]{:S(2)}) %collective-permute-start.9) | collective-permute-done | bytes 20512 | tf_op jit(solution)/shard_map/ppermute | solution.py:400
  70.8 0.0 copy-done.7
  70.8 0.0 copy-done.8
  70.8 2.2 %final.1 = (f32[3,8,16,256]{3,2,1,0:T(8,128)}, f32[8,16,256]{2,1,0:T(8,128)}, f32[3,1024]{1,0:T(4,128)}) custom-call(f32[5,8,128]{2,1,0:T(8,128)S(1)} %reduce_sum.19.mine, f32[5,8,128]{2,1,0:T(8,128)S(1)} %collective-permute-done.9.other, f32[7,8,16,256]{3,2,1,0:T(8,128)S(1)} %get-tuple-element.18.fields, f32[9,8,16,256]{3,2,1,0:T(8,128)S(1)} %get-tuple-element.30.grads, ...), custom_call_target="tpu_custom_call" | custom-call | tf_op jit(solution)/shard_map/final/pallas_call | solution.py:413
  (5 shorter events, 0.1 us)
Async XLA Ops:
  0.6 1.0 %copy-start = (f32[3,8,16,256]{3,2,1,0:T(8,128)S(1)}, f32[3,8,16,256]{3,2,1,0:T(8,128)}, u32[]{:S(2)}) copy-start(f32[3,8,16,256]{3,2,1,0:T(8,128)} %velocity.1) | copy-start | bytes 1179652
  1.6 0.9 %copy-start.1 = (f32[8,16,256]{2,1,0:T(8,128)S(1)}, f32[8,16,256]{2,1,0:T(8,128)}, u32[]{:S(2)}) copy-start(f32[8,16,256]{2,1,0:T(8,128)} %visc.1) | copy-start | bytes 393220
  2.5 0.9 %copy-start.2 = (s32[8,16,256]{2,1,0:T(8,128)S(1)}, s32[8,16,256]{2,1,0:T(8,128)}, u32[]{:S(2)}) copy-start(s32[8,16,256]{2,1,0:T(8,128)} %solid.1) | copy-start | bytes 393220
  3.4 0.9 %copy-start.3 = (f32[8,16,256]{2,1,0:T(8,128)S(1)}, f32[8,16,256]{2,1,0:T(8,128)}, u32[]{:S(2)}) copy-start(f32[8,16,256]{2,1,0:T(8,128)} %pres.1) | copy-start | bytes 393220
  4.3 0.9 %copy-start.4 = (f32[8,16,256]{2,1,0:T(8,128)S(1)}, f32[8,16,256]{2,1,0:T(8,128)}, u32[]{:S(2)}) copy-start(f32[8,16,256]{2,1,0:T(8,128)} %relax.1) | copy-start | bytes 393220
  5.2 27.1 %copy-start.5 = (s32[3,1024]{1,0:T(4,128)S(1)}, s32[3,1024]{1,0:T(4,128)}, u32[]{:S(2)}) copy-start(s32[3,1024]{1,0:T(4,128)} %host.3) | copy-start | bytes 36868
  5.3 27.1 %copy-start.6 = (f32[3,1024]{1,0:T(4,128)S(1)}, f32[3,1024]{1,0:T(4,128)}, u32[]{:S(2)}) copy-start(f32[3,1024]{1,0:T(4,128)} %off.3) | copy-start | bytes 36868
  6.5 4.8 %collective-permute-start = (f32[2,16,128]{2,1,0:T(8,128)S(1)}, f32[2,16,128]{2,1,0:T(8,128)S(1)}, u32[]{:S(2)}, u32[]{:S(2)}) collective-permute-start(f32[2,16,128]{2,1,0:T(8,128)S(1)} %get-tuple-element.19), channel_id=1, source_target_pairs={{0,1},{1,2},{2,3},{3,0},{4,5},{5,6},{6,7},{7,4},{8,9},{9,10},{10,1... | collective-permute-start | bytes 49160 | tf_op jit(solution)/shard_map/ppermute | solution.py:400
  8.7 2.6 %collective-permute-start.1 = (f32[2,16,128]{2,1,0:T(8,128)S(1)}, f32[2,16,128]{2,1,0:T(8,128)S(1)}, u32[]{:S(2)}, u32[]{:S(2)}) collective-permute-start(f32[2,16,128]{2,1,0:T(8,128)S(1)} %get-tuple-element.20), channel_id=1, source_target_pairs={{0,3},{1,0},{2,1},{3,2},{4,7},{5,4},{6,5},{7,6},{8,11},{9,8},{10,9... | collective-permute-start | bytes 49160 | tf_op jit(solution)/shard_map/ppermute | solution.py:400
  12.6 8.8 %collective-permute-start.2 = (f32[29,8,256]{2,1,0:T(8,128)S(1)}, f32[29,8,256]{2,1,0:T(8,128)S(1)}, u32[]{:S(2)}, u32[]{:S(2)}) collective-permute-start(f32[29,8,256]{2,1,0:T(8,128)S(1)} %get-tuple-element.21), channel_id=1, source_target_pairs={{0,4},{4,8},{8,12},{12,16},{16,20},{20,24},{24,28},{28,0},{1,5},{5... | collective-permute-start | bytes 712712 | tf_op jit(solution)/shard_map/ppermute | solution.py:400
  15.8 5.8 %collective-permute-start.3 = (f32[29,8,256]{2,1,0:T(8,128)S(1)}, f32[29,8,256]{2,1,0:T(8,128)S(1)}, u32[]{:S(2)}, u32[]{:S(2)}) collective-permute-start(f32[29,8,256]{2,1,0:T(8,128)S(1)} %get-tuple-element.22), channel_id=1, source_target_pairs={{0,28},{4,0},{8,4},{12,8},{16,12},{20,16},{24,20},{28,24},{1,29},{... | collective-permute-start | bytes 712712 | tf_op jit(solution)/shard_map/ppermute | solution.py:400
  16.1 11.8 %collective-permute-start.4 = (f32[21,16,256]{2,1,0:T(8,128)S(1)}, f32[21,16,256]{2,1,0:T(8,128)S(1)}, u32[]{:S(2)}, u32[]{:S(2)}) collective-permute-start(f32[21,16,256]{2,1,0:T(8,128)S(1)} %get-tuple-element.24), channel_id=1, source_target_pairs={{0,32},{32,64},{64,96},{96,128},{128,160},{160,192},{192,224},{224... | collective-permute-start | bytes 1032200 | tf_op jit(solution)/shard_map/ppermute | solution.py:400
  17.5 10.5 %collective-permute-start.5 = (f32[21,16,256]{2,1,0:T(8,128)S(1)}, f32[21,16,256]{2,1,0:T(8,128)S(1)}, u32[]{:S(2)}, u32[]{:S(2)}) collective-permute-start(f32[21,16,256]{2,1,0:T(8,128)S(1)} %get-tuple-element.25), channel_id=1, source_target_pairs={{0,224},{32,0},{64,32},{96,64},{128,96},{160,128},{192,160},{224,1... | collective-permute-start | bytes 1032200 | tf_op jit(solution)/shard_map/ppermute | solution.py:400
  22.2 10.1 %collective-permute-start.6 = (f32[18,8,256]{2,1,0:T(8,128)S(1)}, f32[18,8,256]{2,1,0:T(8,128)S(1)}, u32[]{:S(2)}, u32[]{:S(2)}) collective-permute-start(f32[18,8,256]{2,1,0:T(8,128)S(1)} %get-tuple-element.26), channel_id=1, source_target_pairs={{0,32},{32,64},{64,96},{96,128},{128,160},{160,192},{192,224},{224... | collective-permute-start | bytes 442376 | tf_op jit(solution)/shard_map/ppermute | solution.py:400
  23.9 8.4 %collective-permute-start.7 = (f32[18,8,256]{2,1,0:T(8,128)S(1)}, f32[18,8,256]{2,1,0:T(8,128)S(1)}, u32[]{:S(2)}, u32[]{:S(2)}) collective-permute-start(f32[18,8,256]{2,1,0:T(8,128)S(1)} %get-tuple-element.27), channel_id=1, source_target_pairs={{0,224},{32,0},{64,32},{96,64},{128,96},{160,128},{192,160},{224,1... | collective-permute-start | bytes 442376 | tf_op jit(solution)/shard_map/ppermute | solution.py:400
  32.3 38.4 %copy-start.7 = (f32[3,1024]{1,0:T(4,128)S(1)}, f32[3,1024]{1,0:T(4,128)}, u32[]{:S(2)}) copy-start(f32[3,1024]{1,0:T(4,128)} %motion.1) | copy-start | bytes 36868
  32.3 38.4 %copy-start.8 = (f32[1024]{0:T(1024)S(1)}, f32[1024]{0:T(1024)}, u32[]{:S(2)}) copy-start(f32[1024]{0:T(1024)} %param.17) | copy-start | bytes 12292
  36.4 2.2 %collective-permute-start.8 = (f32[5,8,128]{2,1,0:T(8,128)S(1)}, f32[5,8,128]{2,1,0:T(8,128)S(1)}, u32[]{:S(2)}, u32[]{:S(2)}) collective-permute-start(f32[5,8,128]{2,1,0:T(8,128)S(1)} %get-tuple-element.29), channel_id=1, source_target_pairs={{0,4},{4,0},{1,5},{5,1},{2,6},{6,2},{3,7},{7,3},{8,12},{12,8},{9,1... | collective-permute-start | bytes 61448 | tf_op jit(solution)/shard_map/ppermute | solution.py:400
  66.4 4.4 %collective-permute-start.9 = (f32[5,8,128]{2,1,0:T(8,128)S(1)}, f32[5,8,128]{2,1,0:T(8,128)S(1)}, u32[]{:S(2)}, u32[]{:S(2)}) collective-permute-start(f32[5,8,128]{2,1,0:T(8,128)S(1)} %reduce_sum.19.mine), channel_id=1, source_target_pairs={{0,4},{4,0},{1,5},{5,1},{2,6},{6,2},{3,7},{7,3},{8,12},{12,8},{9,1... | collective-permute-start | bytes 61448 | tf_op jit(solution)/shard_map/ppermute | solution.py:400

commit v3 on v2

v3 whole, which is shorter than its diff:
```python
import jax
import jax.numpy as jnp
from jax import lax
from jax.experimental import pallas as pl
from jax.experimental.pallas import tpu as pltpu
from jax.sharding import Mesh, PartitionSpec as P

DT = 0.1
F32 = jnp.float32
BF16 = jnp.bfloat16

X, Y, Z = 8, 16, 256
YE, ZE = 24, 384
VISC, KEEP, PRES, RELAX = 3, 4, 5, 6
FIELDS = 7
RADIUS = (4, 3, 3, 3, 3, 3, 2)
XLAYERS = [(f, d) for f in range(FIELDS) for d in range(1, RADIUS[f] + 1)]
CORNER = (3, 3, 3, 2, 2, 2, 1)
RELAYED = [(f, d) for f in range(FIELDS) for d in range(1, CORNER[f] + 1)]
YPAIRS = FIELDS * X // 2
ZUNITS = -(-FIELDS * X // 32)
RTILES = len(RELAYED) + 2
WINDOW = 3
VMEM = pl.BlockSpec(memory_space=pltpu.VMEM)
MIB = 1024 * 1024


def iota(shape, dim):
    return lax.broadcasted_iota(jnp.int32, shape, dim)


def roll(a, shift, axis):
    shift = shift % a.shape[axis]
    return a if shift == 0 else pltpu.roll(a, shift, axis)


def halves(width=Z):
    return [slice(i, i + 128) for i in range(0, width, 128)]


def load(refs, own_out, stage, sems):
    velocity, visc, solid, pres, relax = refs
    copies = [
        pltpu.make_async_copy(velocity, own_out.at[:3], sems.at[0]),
        pltpu.make_async_copy(visc, own_out.at[VISC], sems.at[1]),
        pltpu.make_async_copy(solid, stage, sems.at[2]),
        pltpu.make_async_copy(pres, own_out.at[PRES], sems.at[3]),
        pltpu.make_async_copy(relax, own_out.at[RELAX], sems.at[4]),
    ]
    for copy in copies:
        copy.start()
    for copy in copies:
        copy.wait()
    own_out[KEEP] = 1.0 - stage[...].astype(F32)


def pack_kernel(*args):
    refs, (fields, y_up, y_down, up, down, stage, sems) = args[:5], args[5:]
    load(refs, fields, stage, sems)
    low_rows = iota((8, Z), 0) < 4
    for t in range(YPAIRS):
        f, x = divmod(2 * t, X)
        a, b = fields[f, x], fields[f, x + 1]
        y_up[t] = jnp.where(low_rows, roll(a[8:], 4, 0), b[8:])
        y_down[t] = jnp.where(low_rows, a[:8], roll(b[:8], 4, 0))
    for i, (f, d) in enumerate(XLAYERS):
        up[i] = fields[f, X - d]
        down[i] = fields[f, d - 1]


def position():
    return (
        lax.axis_index("stream"),
        lax.axis_index("gx") * 2 + lax.axis_index("core"),
        lax.axis_index("prop"),
    )


def inside_flags():
    out = []
    for i, n in zip(position(), (8, 8, 4)):
        out.append((i > 0).astype(F32))
        out.append((i < n - 1).astype(F32))
    return out


def z_pack(tiles, to_up, to_down, slot):
    for unit in range(ZUNITS):
        high = jnp.zeros(slot.shape, F32)
        low = jnp.zeros(slot.shape, F32)
        for j, tile in enumerate(tiles[32 * unit : 32 * unit + 32]):
            high = jnp.where(slot == j, roll(tile[:, Z - 128 :], 4 * j - 124, 1), high)
            low = jnp.where(slot == j, roll(tile[:, :128], 4 * j, 1), low)
        to_up(unit, high)
        to_down(unit, low)


def own_kernel(fields, z_up, z_down):
    tiles = [fields[f, x] for f in range(FIELDS) for x in range(X)]
    z_pack(tiles, z_up.__setitem__, z_down.__setitem__, iota((Y, 128), 1) // 4)


def rows_kernel(own_up, own_down, ym, yp, rows, z_up, z_down):
    _, _, in_ym, in_yp, _, _ = inside_flags()
    low_rows = iota((8, Z), 0) < 4
    for t in range(YPAIRS):
        plus, minus = yp[t] * in_yp, ym[t] * in_ym
        f, x = divmod(2 * t, X)
        rows[f, x] = jnp.where(low_rows, plus, roll(minus, 4, 0))
        rows[f, x + 1] = jnp.where(low_rows, roll(plus, 4, 0), minus)
    for unit in range(ZUNITS):
        z_up[unit, :Y], z_down[unit, :Y] = own_up[unit], own_down[unit]

    def put(out):
        def store(unit, value):
            out[unit, Y:] = value

        return store

    tiles = [rows[f, x] for f in range(FIELDS) for x in range(X)]
    z_pack(tiles, put(z_up), put(z_down), iota((8, 128), 1) // 4)


def third_kernel(rows, zm, zp, third, to_up, to_down):
    in_zm, in_zp = inside_flags()[4:]
    lane = iota((8, 128), 1)
    right = (lane < 4).astype(F32) * in_zp
    left = (lane >= 124).astype(F32) * in_zm
    slot = lane // 8
    for f in range(FIELDS):
        for x in range(X):
            for h in range(3):
                unit, j = divmod(f * X + x, 32)
                cut = slice(8 * h, 8 * h + 8)
                plus, minus = roll(zp[unit, cut], -4 * j, 1), roll(zm[unit, cut], 124 - 4 * j, 1)
                third[f, x, cut] = plus * right + minus * left
    for up, out in ((True, to_up), (False, to_down)):
        units = [jnp.zeros((8, 128), F32) for _ in range(4)]
        for i, (f, d) in enumerate(RELAYED):
            x = X - d if up else d - 1
            out[i] = rows[f, x]
            for h in range(3):
                unit, j = divmod(3 * i + h, 16)
                tile = roll(third[f, x, 8 * h : 8 * h + 8], 8 * j + 4, 1)
                units[unit] = jnp.where(slot == j, tile, units[unit])
        for unit in range(4):
            out[len(RELAYED) + unit // 2, :, halves()[unit % 2]] = units[unit]


def y_plus(a):
    return roll(a, -1, 0)


def y_minus(a):
    return roll(a, 1, 0)


def z_plus(a):
    return roll(a, -1, 1)


def z_minus(a):
    return roll(a, 1, 1)


def own(a):
    return a[:Y, :Z]


def cell_mask():
    _, _, in_ym, in_yp, in_zm, in_zp = inside_flags()
    row, col = iota((YE, ZE), 0), iota((YE, ZE), 1)
    in_y = jnp.where(row < Y, 1.0, jnp.where(row < Y + 4, in_yp, in_ym))
    in_z = jnp.where(
        col < Z, 1.0, jnp.where(col < Z + 4, in_zp, jnp.where(col >= ZE - 4, in_zm, 0.0))
    )
    return in_y * in_z


def beside(get, x):
    center = get(x)
    return [
        (get(x + 1), get(x - 1)),
        (y_plus(center), y_minus(center)),
        (z_plus(center), z_minus(center)),
    ]


def nearby(pairs):
    return sum(p + m for p, m in pairs)


def predicted(field, k, x):
    center = field(k, x)
    pairs = beside(lambda i: field(k, i), x)
    conv = 0.5 * sum(field(d, x) * (p - m) for d, (p, m) in enumerate(pairs))
    lap = nearby(pairs) - 6.0 * center
    return field(KEEP, x) * (center + DT * (field(VISC, x) * lap - conv))


def residual(field, pred, x, mask):
    div = 0.5 * (
        pred(0, x + 1)
        - pred(0, x - 1)
        + (y_plus(pred(1, x)) - y_minus(pred(1, x)))
        + (z_plus(pred(2, x)) - z_minus(pred(2, x)))
    )
    pairs = beside(lambda i: field(PRES, i), x)
    image = (6.0 + field(RELAX, x)) * field(PRES, x) - nearby(pairs)
    return (-div / DT - image) * mask, pairs


def image_of(field, get, x, mask):
    pairs = beside(get, x)
    return ((6.0 + field(RELAX, x)) * get(x) - nearby(pairs)) * mask, pairs


def first_part(field, pred, x, pairs, out, at):
    for d, (p, m) in enumerate(pairs):
        grad = own(p) - own(m)
        out[d, at] = own(field(KEEP, x)) * (own(pred(d, x)) - DT * 0.5 * grad)


def later_part(field, x, pairs, out, start, at):
    keep = own(field(KEEP, x)) * (-DT * 0.5)
    for d, (p, m) in enumerate(pairs):
        out[start + d, at] = keep * (own(p) - own(m))


def extended(fields, rows, third, f, x):
    return jnp.concatenate([jnp.concatenate([fields[f, x], rows[f, x]], axis=0), third[f, x]], axis=1)


def inner_kernel(fields, rows, third, pred_out, res_out, img_out, first_out, second_out):
    def field(f, x):
        return extended(fields, rows, third, f, x)

    def pred(k, x):
        return pred_out[k, x - 1]

    def res(x):
        return res_out[x - 2]

    mask = cell_mask()
    for x in range(1, 7):
        for k in range(3):
            pred_out[k, x - 1] = predicted(field, k, x)
    for x in range(2, 6):
        res_out[x - 2], pairs = residual(field, pred, x, mask)
        first_part(field, pred, x, pairs, first_out, x - 2)
    for x in range(3, 5):
        img_out[x - 3], pairs = image_of(field, res, x, mask)
        later_part(field, x, pairs, second_out, 0, x - 3)


def weight_kernel(host, off, z_high, z_low, xy):
    width = 256
    first = window_start()
    for c in range(host.shape[1] // width):
        cut = slice(c * width, c * width + width)
        place = iota((Z, width), 0) + lax.axis_index("prop") * Z
        weight = axis_weights(host, off, 2, cut, place)
        high = weight.astype(BF16)
        z_high[:, cut] = high
        z_low[:, cut] = (weight - high.astype(F32)).astype(BF16)
        place = iota((Y, width), 0) + position()[1] * Y
        weight = axis_weights(host, off, 1, cut, place)
        x_first = lax.axis_index("stream") * X + first
        for l in range(WINDOW):
            xy[l, :, cut] = weight * axis_weights(host, off, 0, cut, x_first + l)


def product(a, high, low, dims):
    a_high = a.astype(BF16)
    a_low = (a - a_high.astype(F32)).astype(BF16)

    def dot(p, q):
        return lax.dot_general(p, q, (dims, ((), ())), preferred_element_type=F32)

    return dot(a_low, high) + dot(a_high, low) + dot(a_high, high)


def main_kernel(
    fields,
    rows,
    third,
    xm,
    xp,
    rm,
    rp,
    pred_in,
    res_in,
    img_in,
    first_in,
    second_in,
    z_high,
    z_low,
    xy,
    keep_half,
    send_half,
    grads,
    r0_out,
    s_out,
    halo,
    pred_own,
    res_own,
    img_own,
    payload,
):
    in_xm, in_xp = inside_flags()[:2]

    lane = iota((8, 128), 1)
    ends = ((lane < 4) | (lane >= 124)).astype(F32)
    for side, (edge, relay, flag) in enumerate(((xm, rm, in_xm), (xp, rp, in_xp))):
        for i, layer in enumerate(XLAYERS):
            halo[side, i, :Y, :Z] = edge[i] * flag
            if layer not in RELAYED:
                halo[side, i, :Y, Z:] = jnp.zeros((Y, 128), F32)
                halo[side, i, Y:] = jnp.zeros((8, ZE), F32)
                continue
            n = RELAYED.index(layer)
            halo[side, i, Y:, :Z] = relay[n] * flag
            for h in range(3):
                unit, j = divmod(3 * n + h, 16)
                packed = relay[len(RELAYED) + unit // 2, :, halves()[unit % 2]]
                halo[side, i, 8 * h : 8 * h + 8, Z:] = roll(packed, -8 * j - 4, 1) * (ends * flag)

    def field(f, x):
        if x < 0:
            return halo[0, XLAYERS.index((f, -x))]
        if x >= X:
            return halo[1, XLAYERS.index((f, x - X + 1))]
        return extended(fields, rows, third, f, x)

    def pred(k, x):
        return pred_in[k, x - 1] if 1 <= x < 7 else pred_own[k, x + 3]

    def res(x):
        return res_in[x - 2] if 2 <= x < 6 else res_own[x + 2]

    def img(x):
        return img_in[x - 3] if 3 <= x < 5 else img_own[x + 1]

    mask = cell_mask()
    masks = {x: mask * in_xm for x in (-2, -1)}
    masks.update({x: mask * in_xp for x in (X, X + 1)})
    for x in (-3, -2, -1, 0, 7, 8, 9, 10):
        for k in range(3 if -3 < x < X + 2 else 1):
            pred_own[k, x + 3] = predicted(field, k, x)
    for x in range(-2, X + 2):
        if not 2 <= x < 6:
            res_own[x + 2], pairs = residual(field, pred, x, masks.get(x, mask))
            if 0 <= x < X:
                first_part(field, pred, x, pairs, grads, x)
    grads[:3, 2:6] = first_in[...]
    for x in range(-1, X + 1):
        if not 3 <= x < 5:
            img_own[x + 1], pairs = image_of(field, res, x, masks.get(x, mask))
            if 0 <= x < X:
                later_part(field, x, pairs, grads, 3, x)
    grads[3:6, 3:5] = second_in[...]
    sums = [jnp.zeros((Y, Z), F32) for _ in range(4)]
    for x in range(X):
        image, pairs = image_of(field, img, x, 1.0)
        later_part(field, x, pairs, grads, 6, x)
        r, s = own(res(x)), own(img(x))
        r0_out[x], s_out[x] = r, s
        for i, (a, b) in enumerate(((r, r), (r, s), (s, s), (s, own(image)))):
            sums[i] = sums[i] + a * b
    payload[9] = jnp.zeros((8, 128), F32)
    for i, total in enumerate(sums):
        line = jnp.sum(total[:, :128] + total[:, 128:], axis=0, keepdims=True)
        payload[9, i : i + 1] = line

    samples = grads[:, pl.ds(window_start(), WINDOW)].reshape(9 * WINDOW * Y, Z)
    width = 256
    for c in range(z_high.shape[1] // width):
        cut = slice(c * width, c * width + width)
        parts = product(samples, z_high[:, cut], z_low[:, cut], ((1,), (0,)))
        parts = parts.reshape(9, WINDOW, Y, width)
        for k in range(9):
            total = sum(parts[k, l] * xy[l, :, cut] for l in range(WINDOW))
            line = jnp.sum(total, axis=0, keepdims=True)
            for half, piece in enumerate(halves(width)):
                at = c * (width // 128) + half
                payload[k, at : at + 1] = line[:, piece]
    second = lax.axis_index("core") == 1
    for k in range(5):
        keep_half[k] = jnp.where(second, payload[5 + k], payload[k])
        send_half[k] = jnp.where(second, payload[k], payload[5 + k])


def window_start():
    return jnp.where(lax.axis_index("stream") * X + X == 32, X - WINDOW, 0)


def axis_weights(host, off, d, cut, place):
    low = host[d : d + 1, cut]
    part = off[d : d + 1, cut]
    return jnp.where(place == low, 1.0 - part, 0.0) + jnp.where(place == low + 1, part, 0.0)


def final_kernel(
    mine,
    other,
    pres,
    grads,
    r0,
    s,
    z_high,
    z_low,
    xy,
    motion,
    coeff,
    velocity,
    pressure,
    points,
    force,
):
    second = lax.axis_index("core") == 1
    total = [jnp.where(second, other[k], mine[k]) for k in range(5)]
    total += [jnp.where(second, mine[k], other[k]) for k in range(5)]
    lines = total[9]
    rr, rs, ss, st = [jnp.sum(lines[i : i + 1], axis=1, keepdims=True) for i in range(4)]
    alpha = rr / rs
    new = rr - 2.0 * alpha * rs + alpha * alpha * ss
    beta = new / rr
    grow = 1.0 + beta
    curve = grow * grow * rs - 2.0 * grow * alpha * ss + alpha * alpha * st
    alpha2 = new / curve
    c0 = alpha + alpha2 * grow
    c1 = -alpha2 * alpha
    for k in range(3):
        value = total[k] + c0 * total[3 + k] + c1 * total[6 + k]
        for i in range(8):
            points[k : k + 1, i * 128 : i * 128 + 128] = value[i : i + 1]
    slip = points[...] - motion[...]
    speed = jnp.sqrt(jnp.sum(slip * slip, axis=0, keepdims=True) + 1.0)
    force[...] = (-DT * coeff[...] * speed) * slip
    for x in range(X):
        pressure[x] = pres[x] + c0 * r0[x] + c1 * s[x]
        for k in range(3):
            velocity[k, x] = grads[k, x] + c0 * grads[3 + k, x] + c1 * grads[6 + k, x]
    first = window_start()
    width = 256
    body = jnp.zeros((3 * WINDOW * Y, Z), F32)
    for c in range(z_high.shape[1] // width):
        cut = slice(c * width, c * width + width)
        scaled = jnp.concatenate(
            [xy[l, :, cut] * force[k : k + 1, cut] for k in range(3) for l in range(WINDOW)],
            axis=0,
        )
        body = body + product(scaled, z_high[:, cut], z_low[:, cut], ((1,), (1,)))
    body = body.reshape(3, WINDOW, Y, Z)
    for k in range(3):
        for l in range(WINDOW):
            velocity[k, first + l] = velocity[k, first + l] + body[k, l]


def shift(value, axis, step):
    names = axis if isinstance(axis, tuple) else (axis,)
    n = 1
    for name in names:
        n *= lax.axis_size(name)
    return lax.ppermute(value, axis, [(i, (i + step) % n) for i in range(n)])


def total_over(value, axis, n):
    copies = jnp.broadcast_to(value[None], (n,) + value.shape)
    return jnp.sum(lax.all_to_all(copies, axis, 0, 0), axis=0)


def sds(*shape, dtype=F32):
    return jax.ShapeDtypeStruct(shape, dtype)


def call(kernel, outs, inputs, scratch=(), name=None, space=None, limit=16, us=1.0):
    return pl.pallas_call(
        kernel,
        out_shape=outs,
        in_specs=[pl.BlockSpec(memory_space=space or pltpu.VMEM)] * len(inputs),
        out_specs=[VMEM] * len(outs),
        scratch_shapes=scratch,
        compiler_params=pltpu.CompilerParams(vmem_limit_bytes=limit * MIB),
        cost_estimate=pl.CostEstimate(
            flops=0, bytes_accessed=int(us * 3.0e6), transcendentals=0
        ),
        name=name,
    )(*inputs)


def shards(
    velocity, eddy_visc, solid, pressure_old, relaxation, host_cell, offsets, blade_motion, force_coeff
):
    points = host_cell.shape[1]
    girth = ("gx", "core")
    block, side, edge = sds(X, Y, Z), sds(len(XLAYERS), Y, Z), sds(YPAIRS, 8, Z)
    fields, y_up, y_down, up, down = call(
        pack_kernel,
        (sds(FIELDS, X, Y, Z), edge, edge, side, side),
        (velocity, eddy_visc, solid, pressure_old, relaxation),
        [pltpu.VMEM((X, Y, Z), jnp.int32), pltpu.SemaphoreType.DMA((5,))],
        name="pack",
        space=pltpu.HBM,
        limit=56,
    )
    ym, yp = shift(y_up, girth, 1), shift(y_down, girth, -1)
    xm, xp = shift(up, "stream", 1), shift(down, "stream", -1)
    unit, own_unit = sds(ZUNITS, YE, 128), sds(ZUNITS, Y, 128)
    own_up, own_down = call(own_kernel, (own_unit, own_unit), (fields,), name="ownz", us=0.5)
    rows, z_up, z_down = call(
        rows_kernel, (sds(FIELDS, X, 8, Z), unit, unit), (own_up, own_down, ym, yp), name="rows", us=0.1
    )
    zm, zp = shift(z_up, "prop", 1), shift(z_down, "prop", -1)
    relay = sds(RTILES, 8, Z)
    third, r_up, r_down = call(
        third_kernel,
        (sds(FIELDS, X, YE, 128), relay, relay),
        (rows, zm, zp),
        name="third",
        us=0.1,
    )
    wide = sds(Z, points, dtype=BF16)
    weights = call(
        weight_kernel, (wide, wide, sds(WINDOW, Y, points)), (host_cell, offsets), name="weights", us=0.5
    )
    inner = call(
        inner_kernel,
        (
            sds(3, 6, YE, ZE),
            sds(4, YE, ZE),
            sds(2, YE, ZE),
            sds(3, 4, Y, Z),
            sds(3, 2, Y, Z),
        ),
        (fields, rows, third),
        name="inner",
        us=1.5,
    )
    rm, rp = shift(r_up, "stream", 1), shift(r_down, "stream", -1)
    half = sds(5, 8, 128)
    kept, sent, grads, r0, s = call(
        main_kernel,
        (half, half, sds(9, X, Y, Z), block, block),
        (fields, rows, third, xm, xp, rm, rp, *inner, *weights),
        [
            pltpu.VMEM((2, len(XLAYERS), YE, ZE), F32),
            pltpu.VMEM((3, X + 6, YE, ZE), F32),
            pltpu.VMEM((X + 4, YE, ZE), F32),
            pltpu.VMEM((X + 2, YE, ZE), F32),
            pltpu.VMEM((10, 8, 128), F32),
        ],
        name="main",
    )
    mine = kept + shift(sent, "core", 1)
    mine = total_over(mine, ("gx", "prop"), 16)
    mine = total_over(mine, "stream", 8)
    other = shift(mine, "core", 1)
    return call(
        final_kernel,
        (sds(3, X, Y, Z), block, sds(3, points)),
        (
            mine,
            other,
            pressure_old,
            grads,
            r0,
            s,
            *weights,
            blade_motion,
            force_coeff.reshape(1, points),
        ),
        [pltpu.VMEM((3, points), F32)],
        name="final",
    )


def solution(mesh):
    cut = Mesh(mesh.devices.reshape(8, 4, 2, 4), ("stream", "gx", "core", "prop"))
    cells = ("stream", ("gx", "core"), "prop")
    placed = (P(None, *cells),) + (P(*cells),) * 4 + (P(),) * 4
    return jax.shard_map(
        shards,
        mesh=cut,
        in_specs=placed,
        out_specs=(P(None, *cells), P(*cells), P()),
        check_vma=False,
    )
```

time: 73.2 us -> 65.1 us (0.89)
  local copies, waits for them, and re-layouts: 4.66 us -> 1.25 us
  waiting for transfers between devices: 7.38 us -> 4.27 us
  starting transfers between devices: 23.2 us -> 22 us
    unnamed x18 -> x14, local copies, waits for them, and re-layouts: 4.62 us -> 1.21 us
    ppermute x10, waiting for transfers between devices: 7.38 us -> 4.27 us  [shift(): return lax.ppermute(value, axis, [(i, (i + step) % n) for i in range(n)])]
    ppermute x10, starting transfers between devices: 23.2 us -> 22 us  [shift(): return lax.ppermute(value, axis, [(i, (i + step) % n) for i in range(n)])]
    pallas_call x5 -> x8, Pallas kernels: 9.32 us -> 8.75 us  [call(): pl.pallas_call(kernel, out_shape=outs, in_specs=[pl.BlockSpec(memory_spac...]
  transfers between devices with their start and end apart: 10 -> 10, of which waited for: 5 -> 4; matrix products, arithmetic and copies ran while one was open for 0% -> 0% of each run, Pallas kernels for 1% -> 4%
where the time goes in v3:
time: 65.1 us; the launch traced here: 64.8 us
  blocking collectives  27.8 us (43%)
  starting transfers between devices  22 us (34%)
  Pallas kernels  8.75 us (13%)
  waiting for transfers between devices  4.27 us (7%)
  local copies, waits for them, and re-layouts  1.25 us (2%)
  between operations  0.78 us (1%)
    all_to_all x2, blocking collectives, total_over(): return jnp.sum(lax.all_to_all(copies, axis, 0, 0), axis=0)  27.8 us
    ppermute x10, starting transfers between devices, shift(): return lax.ppermute(value, axis, [(i, (i + step) % n) for i in range(n)])  22 us
    pallas_call x8, Pallas kernels, call(): pl.pallas_call(kernel, out_shape=outs, in_specs=[pl.BlockSpec(memory_spac...  8.75 us
    ppermute x10, waiting for transfers between devices, shift(): return lax.ppermute(value, axis, [(i, (i + step) % n) for i in range(n)])  4.27 us
  transfers between devices with their start and end apart: 10, of which 4 were waited for; matrix products, arithmetic and copies ran while one was open for 0% of the time, Pallas kernels for 4%

profile of v3, /device:TPU:1, one launch (start us, length us, event | category | flops | bytes accessed | tf_op | source)
XLA Modules:
  0.0 64.8 jit_solution(12343571804675822204)
XLA Ops:
  0.6 0.0 copy-start.4
  0.6 0.0 copy-start.5
  0.7 2.6 %pack.1 = (f32[7,8,16,256]{3,2,1,0:T(8,128)}, f32[28,8,256]{2,1,0:T(8,128)}, f32[28,8,256]{2,1,0:T(8,128)}, f32[21,16,256]{2,1,0:T(8,128)}, f32[21,16,256]{2,1,0:T(8,128)}) custom-call(f32[3,8,16,256]{3,2,1,0:T(8,128)} %args_0_.4, f32[8,16,256]{2,1,0:T(8,128)} %args_1_.4, s32[8,16,256]{2,1,0:T(8,128)} %args_2_.4, f32[8,16,256]{2,1,0:T(8,128)} %pres.1, ...), custom_call_target="tpu_custom_call" | custom-call | bytes 3000000 | tf_op jit(solution)/shard_map/pack/pallas_call | solution.py:478
  3.2 2.6 %collective-permute-start = (f32[28,8,256]{2,1,0:T(8,128)}, f32[28,8,256]{2,1,0:T(8,128)S(1)}, u32[]{:S(2)}, u32[]{:S(2)}) collective-permute-start(f32[28,8,256]{2,1,0:T(8,128)} %get-tuple-element.32), channel_id=1, source_target_pairs={{0,4},{4,8},{8,12},{12,16},{16,20},{20,24},{24,28},{28,0},{1,5},{5... | collective-permute-start | bytes 688136 | tf_op jit(solution)/shard_map/ppermute | solution.py:465
  5.9 0.7 %collective-permute-start.1 = (f32[28,8,256]{2,1,0:T(8,128)}, f32[28,8,256]{2,1,0:T(8,128)S(1)}, u32[]{:S(2)}, u32[]{:S(2)}) collective-permute-start(f32[28,8,256]{2,1,0:T(8,128)} %get-tuple-element.33), channel_id=1, source_target_pairs={{0,28},{4,0},{8,4},{12,8},{16,12},{20,16},{24,20},{28,24},{1,29},{... | collective-permute-start | bytes 688136 | tf_op jit(solution)/shard_map/ppermute | solution.py:465
  6.5 1.0 %collective-permute-start.4 = (f32[21,16,256]{2,1,0:T(8,128)}, f32[21,16,256]{2,1,0:T(8,128)S(1)}, u32[]{:S(2)}, u32[]{:S(2)}) collective-permute-start(f32[21,16,256]{2,1,0:T(8,128)} %get-tuple-element.38), channel_id=1, source_target_pairs={{0,32},{32,64},{64,96},{96,128},{128,160},{160,192},{192,224},{224... | collective-permute-start | bytes 1032200 | tf_op jit(solution)/shard_map/ppermute | solution.py:465
  7.5 3.9 %collective-permute-start.5 = (f32[21,16,256]{2,1,0:T(8,128)}, f32[21,16,256]{2,1,0:T(8,128)S(1)}, u32[]{:S(2)}, u32[]{:S(2)}) collective-permute-start(f32[21,16,256]{2,1,0:T(8,128)} %get-tuple-element.39), channel_id=1, source_target_pairs={{0,224},{32,0},{64,32},{96,64},{128,96},{160,128},{192,160},{224,1... | collective-permute-start | bytes 1032200 | tf_op jit(solution)/shard_map/ppermute | solution.py:465
  11.4 0.0 copy-start
  11.4 1.2 %copy-done = f32[7,8,16,256]{3,2,1,0:T(8,128)S(1)} copy-done((f32[7,8,16,256]{3,2,1,0:T(8,128)S(1)}, f32[7,8,16,256]{3,2,1,0:T(8,128)}, u32[]{:S(2)}) %copy-start) | copy-done | bytes 917528
  12.6 0.0 copy-start.1
  12.6 0.3 ownz.1
  12.9 0.0 collective-permute-done.ym
  12.9 0.0 collective-permute-done.1.yp
  12.9 0.2 rows.1
  13.1 1.4 %collective-permute-start.2 = (f32[2,24,128]{2,1,0:T(8,128)S(1)}, f32[2,24,128]{2,1,0:T(8,128)S(1)}, u32[]{:S(2)}, u32[]{:S(2)}) collective-permute-start(f32[2,24,128]{2,1,0:T(8,128)S(1)} %get-tuple-element.35), channel_id=1, source_target_pairs={{0,1},{1,2},{2,3},{3,0},{4,5},{5,6},{6,7},{7,4},{8,9},{9,10},{10,1... | collective-permute-start | bytes 73736 | tf_op jit(solution)/shard_map/ppermute | solution.py:465
  14.5 1.5 %collective-permute-start.3 = (f32[2,24,128]{2,1,0:T(8,128)S(1)}, f32[2,24,128]{2,1,0:T(8,128)S(1)}, u32[]{:S(2)}, u32[]{:S(2)}) collective-permute-start(f32[2,24,128]{2,1,0:T(8,128)S(1)} %get-tuple-element.36), channel_id=1, source_target_pairs={{0,3},{1,0},{2,1},{3,2},{4,7},{5,4},{6,5},{7,6},{8,11},{9,8},{10,9... | collective-permute-start | bytes 73736 | tf_op jit(solution)/shard_map/ppermute | solution.py:465
  16.0 1.4 %collective-permute-done.2.zm = f32[2,24,128]{2,1,0:T(8,128)S(1)} collective-permute-done((f32[2,24,128]{2,1,0:T(8,128)S(1)}, f32[2,24,128]{2,1,0:T(8,128)S(1)}, u32[]{:S(2)}, u32[]{:S(2)}) %collective-permute-start.2) | collective-permute-done | bytes 24608 | tf_op jit(solution)/shard_map/ppermute | solution.py:465
  17.5 0.0 collective-permute-done.3.zp
  17.5 0.5 third.1
  18.0 0.6 collective-permute-start.6
  18.6 4.0 %collective-permute-start.7 = (f32[18,8,256]{2,1,0:T(8,128)S(1)}, f32[18,8,256]{2,1,0:T(8,128)S(1)}, u32[]{:S(2)}, u32[]{:S(2)}) collective-permute-start(f32[18,8,256]{2,1,0:T(8,128)S(1)} %get-tuple-element.41), channel_id=1, source_target_pairs={{0,224},{32,0},{64,32},{96,64},{128,96},{160,128},{192,160},{224,1... | collective-permute-start | bytes 442376 | tf_op jit(solution)/shard_map/ppermute | solution.py:465
  22.6 0.0 copy-done.4
  22.6 0.0 copy-done.5
  22.6 0.3 weights.1
  23.0 0.0 copy-done.1
  23.0 0.9 %inner.1 = (f32[3,6,24,384]{3,2,1,0:T(8,128)S(1)}, f32[4,24,384]{2,1,0:T(8,128)S(1)}, f32[2,24,384]{2,1,0:T(8,128)S(1)}, f32[3,4,16,256]{3,2,1,0:T(8,128)S(1)}, f32[3,2,16,256]{3,2,1,0:T(8,128)S(1)}) custom-call(f32[7,8,16,256]{3,2,1,0:T(8,128)S(1)} %copy-done.1, f32[7,8,8,256]{3,2,1,0:T(8,128)S(1)} %get-tuple-element.34.rows, ...), custom_call_target="tpu_custom_call" | custom-call | bytes 4500000 | tf_op jit(solution)/shard_map/inner/pallas_call | solution.py:478
  23.9 0.0 collective-permute-done.4.xm
  24.0 0.0 collective-permute-done.5.xp
  24.0 1.1 %collective-permute-done.6.rm = f32[18,8,256]{2,1,0:T(8,128)S(1)} collective-permute-done((f32[18,8,256]{2,1,0:T(8,128)S(1)}, f32[18,8,256]{2,1,0:T(8,128)S(1)}, u32[]{:S(2)}, u32[]{:S(2)}) %collective-permute-start.6) | collective-permute-done | bytes 147488 | tf_op jit(solution)/shard_map/ppermute | solution.py:465
  25.1 0.0 collective-permute-done.7.rp
  25.1 2.3 %main.1 = (f32[5,8,128]{2,1,0:T(8,128)S(1)}, f32[5,8,128]{2,1,0:T(8,128)S(1)}, f32[9,8,16,256]{3,2,1,0:T(8,128)S(1)}, f32[8,16,256]{2,1,0:T(8,128)S(1)}, f32[8,16,256]{2,1,0:T(8,128)S(1)}) custom-call(f32[7,8,16,256]{3,2,1,0:T(8,128)S(1)} %copy-done.1, f32[7,8,8,256]{3,2,1,0:T(8,128)S(1)} %get-tuple-element.34.rows, ...), custom_call_target="tpu_custom_call" | custom-call | bytes 3000000 | tf_op jit(solution)/shard_map/main/pallas_call | solution.py:478
  27.4 0.0 copy-start.2
  27.4 0.0 copy-start.3
  27.4 0.0 copy-start.6
  27.4 2.7 %collective-permute-start.8 = (f32[5,8,128]{2,1,0:T(8,128)S(1)}, f32[5,8,128]{2,1,0:T(8,128)S(1)}, u32[]{:S(2)}, u32[]{:S(2)}) collective-permute-start(f32[5,8,128]{2,1,0:T(8,128)S(1)} %get-tuple-element.51), channel_id=1, source_target_pairs={{0,4},{4,0},{1,5},{5,1},{2,6},{6,2},{3,7},{7,3},{8,12},{12,8},{9,1... | collective-permute-start | bytes 61448 | tf_op jit(solution)/shard_map/ppermute | solution.py:465
  30.1 0.8 %collective-permute-done.8 = f32[5,8,128]{2,1,0:T(8,128)S(1)} collective-permute-done((f32[5,8,128]{2,1,0:T(8,128)S(1)}, f32[5,8,128]{2,1,0:T(8,128)S(1)}, u32[]{:S(2)}, u32[]{:S(2)}) %collective-permute-start.8) | collective-permute-done | bytes 20512 | tf_op jit(solution)/shard_map/ppermute | solution.py:465
  31.0 13.8 %all_to_all.10 = f32[16,5,8,128]{3,2,1,0:T(8,128)S(1)} all-to-all(f32[16,5,8,128]{3,2,1,0:T(8,128)S(1)} %broadcast_in_dim.4), channel_id=1, replica_groups=mesh['stream'=8,'gx'=4,'core'=2,'prop'=4] {'gx','prop'}, dimensions={0} | all-to-all | bytes 655360 | tf_op jit(solution)/shard_map/all_to_all | solution.py:470
  44.8 14.0 %all_to_all.11 = f32[8,5,8,128]{3,2,1,0:T(8,128)S(1)} all-to-all(f32[8,5,8,128]{3,2,1,0:T(8,128)S(1)} %broadcast_in_dim.5), channel_id=1, replica_groups=mesh['stream'=8,'gx'=4,'core'=2,'prop'=4] {'stream'}, dimensions={0} | all-to-all | bytes 327680 | tf_op jit(solution)/shard_map/all_to_all | solution.py:470
  58.9 3.6 %collective-permute-start.9 = (f32[5,8,128]{2,1,0:T(8,128)S(1)}, f32[5,8,128]{2,1,0:T(8,128)S(1)}, u32[]{:S(2)}, u32[]{:S(2)}) collective-permute-start(f32[5,8,128]{2,1,0:T(8,128)S(1)} %reduce_sum.19.mine), channel_id=1, source_target_pairs={{0,4},{4,0},{1,5},{5,1},{2,6},{6,2},{3,7},{7,3},{8,12},{12,8},{9,1... | collective-permute-start | bytes 61448 | tf_op jit(solution)/shard_map/ppermute | solution.py:465
  62.4 0.8 %collective-permute-done.9.other = f32[5,8,128]{2,1,0:T(8,128)S(1)} collective-permute-done((f32[5,8,128]{2,1,0:T(8,128)S(1)}, f32[5,8,128]{2,1,0:T(8,128)S(1)}, u32[]{:S(2)}, u32[]{:S(2)}) %collective-permute-start.9) | collective-permute-done | bytes 20512 | tf_op jit(solution)/shard_map/ppermute | solution.py:465
  63.3 0.0 copy-done.2
  63.3 0.0 copy-done.3
  63.3 0.0 copy-done.6
  63.3 1.6 %final.1 = (f32[3,8,16,256]{3,2,1,0:T(8,128)}, f32[8,16,256]{2,1,0:T(8,128)}, f32[3,1024]{1,0:T(4,128)}) custom-call(f32[5,8,128]{2,1,0:T(8,128)S(1)} %reduce_sum.19.mine, f32[5,8,128]{2,1,0:T(8,128)S(1)} %collective-permute-done.9.other, f32[8,16,256]{2,1,0:T(8,128)S(1)} %copy-done.2, f32[9,8,16,256]{3,2,1,0:T(8,128)S(1)} %get-tuple-element.52.grads, ...), custom_call_target="tpu_custom_call" | custom-call | bytes 3000000 | tf_op jit(solution)/shard_map/final/pallas_call | solution.py:478
  (5 shorter events, 0.1 us)
Async XLA Ops:
  0.6 22.0 %copy-start.4 = (s32[3,1024]{1,0:T(4,128)S(1)}, s32[3,1024]{1,0:T(4,128)}, u32[]{:S(2)}) copy-start(s32[3,1024]{1,0:T(4,128)} %host.1) | copy-start | bytes 36868
  0.6 22.0 %copy-start.5 = (f32[3,1024]{1,0:T(4,128)S(1)}, f32[3,1024]{1,0:T(4,128)}, u32[]{:S(2)}) copy-start(f32[3,1024]{1,0:T(4,128)} %off.1) | copy-start | bytes 36868
  3.2 9.7 %collective-permute-start = (f32[28,8,256]{2,1,0:T(8,128)}, f32[28,8,256]{2,1,0:T(8,128)S(1)}, u32[]{:S(2)}, u32[]{:S(2)}) collective-permute-start(f32[28,8,256]{2,1,0:T(8,128)} %get-tuple-element.32), channel_id=1, source_target_pairs={{0,4},{4,8},{8,12},{12,16},{16,20},{20,24},{24,28},{28,0},{1,5},{5... | collective-permute-start | bytes 688136 | tf_op jit(solution)/shard_map/ppermute | solution.py:465
  5.9 7.1 %collective-permute-start.1 = (f32[28,8,256]{2,1,0:T(8,128)}, f32[28,8,256]{2,1,0:T(8,128)S(1)}, u32[]{:S(2)}, u32[]{:S(2)}) collective-permute-start(f32[28,8,256]{2,1,0:T(8,128)} %get-tuple-element.33), channel_id=1, source_target_pairs={{0,28},{4,0},{8,4},{12,8},{16,12},{20,16},{24,20},{28,24},{1,29},{... | collective-permute-start | bytes 688136 | tf_op jit(solution)/shard_map/ppermute | solution.py:465
  6.5 17.4 %collective-permute-start.4 = (f32[21,16,256]{2,1,0:T(8,128)}, f32[21,16,256]{2,1,0:T(8,128)S(1)}, u32[]{:S(2)}, u32[]{:S(2)}) collective-permute-start(f32[21,16,256]{2,1,0:T(8,128)} %get-tuple-element.38), channel_id=1, source_target_pairs={{0,32},{32,64},{64,96},{96,128},{128,160},{160,192},{192,224},{224... | collective-permute-start | bytes 1032200 | tf_op jit(solution)/shard_map/ppermute | solution.py:465
  7.5 16.5 %collective-permute-start.5 = (f32[21,16,256]{2,1,0:T(8,128)}, f32[21,16,256]{2,1,0:T(8,128)S(1)}, u32[]{:S(2)}, u32[]{:S(2)}) collective-permute-start(f32[21,16,256]{2,1,0:T(8,128)} %get-tuple-element.39), channel_id=1, source_target_pairs={{0,224},{32,0},{64,32},{96,64},{128,96},{160,128},{192,160},{224,1... | collective-permute-start | bytes 1032200 | tf_op jit(solution)/shard_map/ppermute | solution.py:465
  11.4 1.2 %copy-start = (f32[7,8,16,256]{3,2,1,0:T(8,128)S(1)}, f32[7,8,16,256]{3,2,1,0:T(8,128)}, u32[]{:S(2)}) copy-start(f32[7,8,16,256]{3,2,1,0:T(8,128)} %get-tuple-element.29.fields) | copy-start | bytes 2752516
  12.6 10.4 %copy-start.1 = (f32[7,8,16,256]{3,2,1,0:T(8,128)S(1)}, f32[7,8,16,256]{3,2,1,0:T(8,128)}, u32[]{:S(2)}) copy-start(f32[7,8,16,256]{3,2,1,0:T(8,128)} %get-tuple-element.29.fields) | copy-start | bytes 2752516
  13.1 4.3 %collective-permute-start.2 = (f32[2,24,128]{2,1,0:T(8,128)S(1)}, f32[2,24,128]{2,1,0:T(8,128)S(1)}, u32[]{:S(2)}, u32[]{:S(2)}) collective-permute-start(f32[2,24,128]{2,1,0:T(8,128)S(1)} %get-tuple-element.35), channel_id=1, source_target_pairs={{0,1},{1,2},{2,3},{3,0},{4,5},{5,6},{6,7},{7,4},{8,9},{9,10},{10,1... | collective-permute-start | bytes 73736 | tf_op jit(solution)/shard_map/ppermute | solution.py:465
  14.5 3.0 %collective-permute-start.3 = (f32[2,24,128]{2,1,0:T(8,128)S(1)}, f32[2,24,128]{2,1,0:T(8,128)S(1)}, u32[]{:S(2)}, u32[]{:S(2)}) collective-permute-start(f32[2,24,128]{2,1,0:T(8,128)S(1)} %get-tuple-element.36), channel_id=1, source_target_pairs={{0,3},{1,0},{2,1},{3,2},{4,7},{5,4},{6,5},{7,6},{8,11},{9,8},{10,9... | collective-permute-start | bytes 73736 | tf_op jit(solution)/shard_map/ppermute | solution.py:465
  18.0 7.1 %collective-permute-start.6 = (f32[18,8,256]{2,1,0:T(8,128)S(1)}, f32[18,8,256]{2,1,0:T(8,128)S(1)}, u32[]{:S(2)}, u32[]{:S(2)}) collective-permute-start(f32[18,8,256]{2,1,0:T(8,128)S(1)} %get-tuple-element.40), channel_id=1, source_target_pairs={{0,32},{32,64},{64,96},{96,128},{128,160},{160,192},{192,224},{224... | collective-permute-start | bytes 442376 | tf_op jit(solution)/shard_map/ppermute | solution.py:465
  18.6 6.5 %collective-permute-start.7 = (f32[18,8,256]{2,1,0:T(8,128)S(1)}, f32[18,8,256]{2,1,0:T(8,128)S(1)}, u32[]{:S(2)}, u32[]{:S(2)}) collective-permute-start(f32[18,8,256]{2,1,0:T(8,128)S(1)} %get-tuple-element.41), channel_id=1, source_target_pairs={{0,224},{32,0},{64,32},{96,64},{128,96},{160,128},{192,160},{224,1... | collective-permute-start | bytes 442376 | tf_op jit(solution)/shard_map/ppermute | solution.py:465
  27.4 35.9 %copy-start.2 = (f32[8,16,256]{2,1,0:T(8,128)S(1)}, f32[8,16,256]{2,1,0:T(8,128)}, u32[]{:S(2)}) copy-start(f32[8,16,256]{2,1,0:T(8,128)} %pres.1) | copy-start | bytes 393220
  27.4 35.9 %copy-start.3 = (f32[3,1024]{1,0:T(4,128)S(1)}, f32[3,1024]{1,0:T(4,128)}, u32[]{:S(2)}) copy-start(f32[3,1024]{1,0:T(4,128)} %motion.1) | copy-start | bytes 36868
  27.4 35.8 %copy-start.6 = (f32[1024]{0:T(1024)S(1)}, f32[1024]{0:T(1024)}, u32[]{:S(2)}) copy-start(f32[1024]{0:T(1024)} %param.17) | copy-start | bytes 12292
  27.4 3.6 %collective-permute-start.8 = (f32[5,8,128]{2,1,0:T(8,128)S(1)}, f32[5,8,128]{2,1,0:T(8,128)S(1)}, u32[]{:S(2)}, u32[]{:S(2)}) collective-permute-start(f32[5,8,128]{2,1,0:T(8,128)S(1)} %get-tuple-element.51), channel_id=1, source_target_pairs={{0,4},{4,0},{1,5},{5,1},{2,6},{6,2},{3,7},{7,3},{8,12},{12,8},{9,1... | collective-permute-start | bytes 61448 | tf_op jit(solution)/shard_map/ppermute | solution.py:465
  58.9 4.4 %collective-permute-start.9 = (f32[5,8,128]{2,1,0:T(8,128)S(1)}, f32[5,8,128]{2,1,0:T(8,128)S(1)}, u32[]{:S(2)}, u32[]{:S(2)}) collective-permute-start(f32[5,8,128]{2,1,0:T(8,128)S(1)} %reduce_sum.19.mine), channel_id=1, source_target_pairs={{0,4},{4,0},{1,5},{5,1},{2,6},{6,2},{3,7},{7,3},{8,12},{12,8},{9,1... | collective-permute-start | bytes 61448 | tf_op jit(solution)/shard_map/ppermute | solution.py:465

commit v4 on v3

--- a/solution.py
+++ b/solution.py
@@ -17,9 +17,11 @@
 XLAYERS = [(f, d) for f in range(FIELDS) for d in range(1, RADIUS[f] + 1)]
 CORNER = (3, 3, 3, 2, 2, 2, 1)
 RELAYED = [(f, d) for f in range(FIELDS) for d in range(1, CORNER[f] + 1)]
+SHARED = [(f, d) for f, d in RELAYED if d < CORNER[f]]
 YPAIRS = FIELDS * X // 2
 ZUNITS = -(-FIELDS * X // 32)
-RTILES = len(RELAYED) + 2
+SHARED += [(f, d) for f, d in RELAYED if CORNER[f] == 1]
+RTILES = len(SHARED) + 2
 WINDOW = 3
 VMEM = pl.BlockSpec(memory_space=pltpu.VMEM)
 MIB = 1024 * 1024
@@ -64,8 +66,7 @@
         y_up[t] = jnp.where(low_rows, roll(a[8:], 4, 0), b[8:])
         y_down[t] = jnp.where(low_rows, a[:8], roll(b[:8], 4, 0))
     for i, (f, d) in enumerate(XLAYERS):
-        up[i] = fields[f, X - d]
-        down[i] = fields[f, d - 1]
+        up[i], down[i] = fields[f, X - d], fields[f, d - 1]
 
 
 def position():
@@ -104,29 +105,27 @@
     _, _, in_ym, in_yp, _, _ = inside_flags()
     low_rows = iota((8, Z), 0) < 4
     for t in range(YPAIRS):
-        plus, minus = yp[t] * in_yp, ym[t] * in_ym
+        minus, plus = ym[t], yp[t]
+        plus, minus = plus * in_yp, minus * in_ym
         f, x = divmod(2 * t, X)
         rows[f, x] = jnp.where(low_rows, plus, roll(minus, 4, 0))
         rows[f, x + 1] = jnp.where(low_rows, roll(plus, 4, 0), minus)
+    tiles = [rows[f, x] for f in range(FIELDS) for x in range(X)]
+    ups, downs = {}, {}
+    z_pack(tiles, ups.__setitem__, downs.__setitem__, iota((8, 128), 1) // 4)
     for unit in range(ZUNITS):
         z_up[unit, :Y], z_down[unit, :Y] = own_up[unit], own_down[unit]
-
-    def put(out):
-        def store(unit, value):
-            out[unit, Y:] = value
-
-        return store
-
-    tiles = [rows[f, x] for f in range(FIELDS) for x in range(X)]
-    z_pack(tiles, put(z_up), put(z_down), iota((8, 128), 1) // 4)
-
-
-def third_kernel(rows, zm, zp, third, to_up, to_down):
+        z_up[unit, Y:], z_down[unit, Y:] = ups[unit], downs[unit]
+
+
+def third_kernel(rows, zm, zp, third, r_up, r_down):
     in_zm, in_zp = inside_flags()[4:]
     lane = iota((8, 128), 1)
     right = (lane < 4).astype(F32) * in_zp
     left = (lane >= 124).astype(F32) * in_zm
     slot = lane // 8
+    row = iota((8, Z), 0)
+    outer_rows = (row < 2) | (row >= 6)
     for f in range(FIELDS):
         for x in range(X):
             for h in range(3):
@@ -134,17 +133,25 @@
                 cut = slice(8 * h, 8 * h + 8)
                 plus, minus = roll(zp[unit, cut], -4 * j, 1), roll(zm[unit, cut], 124 - 4 * j, 1)
                 third[f, x, cut] = plus * right + minus * left
+    to_up, to_down = {}, {}
     for up, out in ((True, to_up), (False, to_down)):
         units = [jnp.zeros((8, 128), F32) for _ in range(4)]
         for i, (f, d) in enumerate(RELAYED):
             x = X - d if up else d - 1
-            out[i] = rows[f, x]
+            if (f, d) in SHARED:
+                tile = rows[f, x]
+                if d + 1 == CORNER[f]:
+                    after = rows[f, x - 1 if up else x + 1]
+                    tile = jnp.where(outer_rows, tile, roll(after, 4, 0))
+                out[SHARED.index((f, d))] = tile
             for h in range(3):
                 unit, j = divmod(3 * i + h, 16)
                 tile = roll(third[f, x, 8 * h : 8 * h + 8], 8 * j + 4, 1)
                 units[unit] = jnp.where(slot == j, tile, units[unit])
-        for unit in range(4):
-            out[len(RELAYED) + unit // 2, :, halves()[unit % 2]] = units[unit]
+        for unit in range(0, 4, 2):
+            out[len(SHARED) + unit // 2] = jnp.concatenate(units[unit : unit + 2], axis=1)
+    for t in range(RTILES):
+        r_up[t], r_down[t] = to_up[t], to_down[t]
 
 
 def y_plus(a):
@@ -319,10 +326,14 @@
                 halo[side, i, Y:] = jnp.zeros((8, ZE), F32)
                 continue
             n = RELAYED.index(layer)
-            halo[side, i, Y:, :Z] = relay[n] * flag
+            if layer in SHARED:
+                tile = relay[SHARED.index(layer)]
+            else:
+                tile = roll(relay[SHARED.index((layer[0], layer[1] - 1))], 4, 0)
+            halo[side, i, Y:, :Z] = tile * flag
             for h in range(3):
                 unit, j = divmod(3 * n + h, 16)
-                packed = relay[len(RELAYED) + unit // 2, :, halves()[unit % 2]]
+                packed = relay[len(SHARED) + unit // 2, :, halves()[unit % 2]]
                 halo[side, i, 8 * h : 8 * h + 8, Z:] = roll(packed, -8 * j - 4, 1) * (ends * flag)
 
     def field(f, x):
@@ -457,12 +468,14 @@
             velocity[k, first + l] = velocity[k, first + l] + body[k, l]
 
 
-def shift(value, axis, step):
-    names = axis if isinstance(axis, tuple) else (axis,)
-    n = 1
-    for name in names:
-        n *= lax.axis_size(name)
-    return lax.ppermute(value, axis, [(i, (i + step) % n) for i in range(n)])
+def exchange(up, down, axis, n):
+    before = lax.ppermute(up, axis, [(i, (i + 1) % n) for i in range(n)])
+    after = lax.ppermute(down, axis, [(i, (i - 1) % n) for i in range(n)])
+    return before, after
+
+
+def swap_cores(value):
+    return lax.ppermute(value, "core", [(0, 1), (1, 0)])
 
 
 def total_over(value, axis, n):
@@ -495,28 +508,31 @@
     points = host_cell.shape[1]
     girth = ("gx", "core")
     block, side, edge = sds(X, Y, Z), sds(len(XLAYERS), Y, Z), sds(YPAIRS, 8, Z)
-    fields, y_up, y_down, up, down = call(
+    fields, y_up, y_down, x_up, x_down = call(
         pack_kernel,
         (sds(FIELDS, X, Y, Z), edge, edge, side, side),
-        (velocity, eddy_visc, solid, pressure_old, relaxation),
+        [
+            pltpu.with_memory_space_constraint(a, pltpu.HBM)
+            for a in (velocity, eddy_visc, solid, pressure_old, relaxation)
+        ],
         [pltpu.VMEM((X, Y, Z), jnp.int32), pltpu.SemaphoreType.DMA((5,))],
         name="pack",
         space=pltpu.HBM,
-        limit=56,
-    )
-    ym, yp = shift(y_up, girth, 1), shift(y_down, girth, -1)
-    xm, xp = shift(up, "stream", 1), shift(down, "stream", -1)
+        limit=24,
+    )
+    from_y = exchange(y_up, y_down, girth, 8)
+    from_x = exchange(x_up, x_down, "stream", 8)
     unit, own_unit = sds(ZUNITS, YE, 128), sds(ZUNITS, Y, 128)
     own_up, own_down = call(own_kernel, (own_unit, own_unit), (fields,), name="ownz", us=0.5)
     rows, z_up, z_down = call(
-        rows_kernel, (sds(FIELDS, X, 8, Z), unit, unit), (own_up, own_down, ym, yp), name="rows", us=0.1
-    )
-    zm, zp = shift(z_up, "prop", 1), shift(z_down, "prop", -1)
+        rows_kernel, (sds(FIELDS, X, 8, Z), unit, unit), (own_up, own_down, *from_y), name="rows", us=0.1
+    )
+    from_z = exchange(z_up, z_down, "prop", 4)
     relay = sds(RTILES, 8, Z)
     third, r_up, r_down = call(
         third_kernel,
         (sds(FIELDS, X, YE, 128), relay, relay),
-        (rows, zm, zp),
+        (rows, *from_z),
         name="third",
         us=0.1,
     )
@@ -537,12 +553,12 @@
         name="inner",
         us=1.5,
     )
-    rm, rp = shift(r_up, "stream", 1), shift(r_down, "stream", -1)
+    from_r = exchange(r_up, r_down, "stream", 8)
     half = sds(5, 8, 128)
     kept, sent, grads, r0, s = call(
         main_kernel,
         (half, half, sds(9, X, Y, Z), block, block),
-        (fields, rows, third, xm, xp, rm, rp, *inner, *weights),
+        (fields, rows, third, *from_x, *from_r, *inner, *weights),
         [
             pltpu.VMEM((2, len(XLAYERS), YE, ZE), F32),
             pltpu.VMEM((3, X + 6, YE, ZE), F32),
@@ -552,10 +568,10 @@
         ],
         name="main",
     )
-    mine = kept + shift(sent, "core", 1)
+    mine = kept + swap_cores(sent)
     mine = total_over(mine, ("gx", "prop"), 16)
     mine = total_over(mine, "stream", 8)
-    other = shift(mine, "core", 1)
+    other = swap_cores(mine)
     return call(
         final_kernel,
         (sds(3, X, Y, Z), block, sds(3, points)),

time: 65.1 us -> 62.2 us (0.955)
  Pallas kernels: 8.75 us -> 7.48 us
  local copies, waits for them, and re-layouts: 1.25 us -> 0.07 us
    pallas_call x8, Pallas kernels: 8.75 us -> 7.48 us  [call(): pl.pallas_call(kernel, out_shape=outs, in_specs=[pl.BlockSpec(memory_spac...]
    unnamed x14 -> x10, local copies, waits for them, and re-layouts: 1.21 us -> 0.03 us
where the time goes in v4:
time: 62.2 us; the launch traced here: 62.1 us
  blocking collectives  27.8 us (45%)
  starting transfers between devices  22.1 us (36%)
  Pallas kernels  7.48 us (12%)
  waiting for transfers between devices  3.74 us (6%)
  between operations  0.77 us (1%)
    all_to_all x2, blocking collectives, total_over(): return jnp.sum(lax.all_to_all(copies, axis, 0, 0), axis=0)  27.8 us
    ppermute x4, starting transfers between devices, exchange(): after = lax.ppermute(down, axis, [(i, (i - 1) % n) for i in range(n)])  10.2 us
    pallas_call x8, Pallas kernels, call(): pl.pallas_call(kernel, out_shape=outs, in_specs=[pl.BlockSpec(memory_spac...  7.48 us
    ppermute x4, starting transfers between devices, exchange(): before = lax.ppermute(up, axis, [(i, (i + 1) % n) for i in range(n)])  6.53 us
    ppermute x2, starting transfers between devices, swap_cores(): return lax.ppermute(value, 'core', [(0, 1), (1, 0)])  5.43 us
    ppermute x4, waiting for transfers between devices, exchange(): before = lax.ppermute(up, axis, [(i, (i + 1) % n) for i in range(n)])  2.02 us
    ppermute x2, waiting for transfers between devices, swap_cores(): return lax.ppermute(value, 'core', [(0, 1), (1, 0)])  1.69 us
  transfers between devices with their start and end apart: 10, of which 4 were waited for; matrix products, arithmetic and copies ran while one was open for 0% of the time, Pallas kernels for 4%

profile of v4, /device:TPU:1, one launch (start us, length us, event | category | flops | bytes accessed | tf_op | source)
XLA Modules:
  0.0 62.1 jit_solution(233816018909211872)
XLA Ops:
  0.6 1.3 %pack.1 = (f32[7,8,16,256]{3,2,1,0:T(8,128)S(1)}, f32[28,8,256]{2,1,0:T(8,128)S(1)}, f32[28,8,256]{2,1,0:T(8,128)S(1)}, f32[21,16,256]{2,1,0:T(8,128)S(1)}, f32[21,16,256]{2,1,0:T(8,128)S(1)}) custom-call(f32[3,8,16,256]{3,2,1,0:T(8,128)} %args_0_.4, f32[8,16,256]{2,1,0:T(8,128)} %args_1_.4, s32[8,16,256]{2,1,0:T(8,128)} %args_2_.4, f32[8,16,256]{2,1,0:T(8,128)} %pres.1, ...), custom_call_target="tpu_custom_call" | custom-call | bytes 3000000 | tf_op jit(solution)/shard_map/pack/pallas_call | solution.py:491
  1.9 0.0 copy-start.2
  1.9 0.0 copy-start.3
  2.0 2.6 %collective-permute-start = (f32[28,8,256]{2,1,0:T(8,128)S(1)}, f32[28,8,256]{2,1,0:T(8,128)S(1)}, u32[]{:S(2)}, u32[]{:S(2)}) collective-permute-start(f32[28,8,256]{2,1,0:T(8,128)S(1)} %get-tuple-element.32), channel_id=1, source_target_pairs={{0,4},{4,8},{8,12},{12,16},{16,20},{20,24},{24,28},{28,0},{1,5},{5... | collective-permute-start | bytes 688136 | tf_op jit(solution)/shard_map/ppermute | solution.py:472
  4.6 0.7 %collective-permute-start.1 = (f32[28,8,256]{2,1,0:T(8,128)S(1)}, f32[28,8,256]{2,1,0:T(8,128)S(1)}, u32[]{:S(2)}, u32[]{:S(2)}) collective-permute-start(f32[28,8,256]{2,1,0:T(8,128)S(1)} %get-tuple-element.33), channel_id=1, source_target_pairs={{0,28},{4,0},{8,4},{12,8},{16,12},{20,16},{24,20},{28,24},{1,29},{... | collective-permute-start | bytes 688136 | tf_op jit(solution)/shard_map/ppermute | solution.py:473
  5.2 1.0 %collective-permute-start.4 = (f32[21,16,256]{2,1,0:T(8,128)S(1)}, f32[21,16,256]{2,1,0:T(8,128)S(1)}, u32[]{:S(2)}, u32[]{:S(2)}) collective-permute-start(f32[21,16,256]{2,1,0:T(8,128)S(1)} %get-tuple-element.38), channel_id=1, source_target_pairs={{0,32},{32,64},{64,96},{96,128},{128,160},{160,192},{192,224},{224... | collective-permute-start | bytes 1032200 | tf_op jit(solution)/shard_map/ppermute | solution.py:472
  6.2 3.9 %collective-permute-start.5 = (f32[21,16,256]{2,1,0:T(8,128)S(1)}, f32[21,16,256]{2,1,0:T(8,128)S(1)}, u32[]{:S(2)}, u32[]{:S(2)}) collective-permute-start(f32[21,16,256]{2,1,0:T(8,128)S(1)} %get-tuple-element.39), channel_id=1, source_target_pairs={{0,224},{32,0},{64,32},{96,64},{128,96},{160,128},{192,160},{224,1... | collective-permute-start | bytes 1032200 | tf_op jit(solution)/shard_map/ppermute | solution.py:473
  10.2 0.3 ownz.1
  10.5 0.0 collective-permute-done.ym
  10.5 0.0 collective-permute-done.1.yp
  10.5 0.2 rows.1
  10.7 1.4 %collective-permute-start.2 = (f32[2,24,128]{2,1,0:T(8,128)S(1)}, f32[2,24,128]{2,1,0:T(8,128)S(1)}, u32[]{:S(2)}, u32[]{:S(2)}) collective-permute-start(f32[2,24,128]{2,1,0:T(8,128)S(1)} %get-tuple-element.35), channel_id=1, source_target_pairs={{0,1},{1,2},{2,3},{3,0},{4,5},{5,6},{6,7},{7,4},{8,9},{9,10},{10,1... | collective-permute-start | bytes 73736 | tf_op jit(solution)/shard_map/ppermute | solution.py:472
  12.1 1.5 %collective-permute-start.3 = (f32[2,24,128]{2,1,0:T(8,128)S(1)}, f32[2,24,128]{2,1,0:T(8,128)S(1)}, u32[]{:S(2)}, u32[]{:S(2)}) collective-permute-start(f32[2,24,128]{2,1,0:T(8,128)S(1)} %get-tuple-element.36), channel_id=1, source_target_pairs={{0,3},{1,0},{2,1},{3,2},{4,7},{5,4},{6,5},{7,6},{8,11},{9,8},{10,9... | collective-permute-start | bytes 73736 | tf_op jit(solution)/shard_map/ppermute | solution.py:473
  13.6 1.4 %collective-permute-done.2.zm = f32[2,24,128]{2,1,0:T(8,128)S(1)} collective-permute-done((f32[2,24,128]{2,1,0:T(8,128)S(1)}, f32[2,24,128]{2,1,0:T(8,128)S(1)}, u32[]{:S(2)}, u32[]{:S(2)}) %collective-permute-start.2) | collective-permute-done | bytes 24608 | tf_op jit(solution)/shard_map/ppermute | solution.py:472
  15.0 0.0 collective-permute-done.3.zp
  15.0 0.5 third.1
  15.6 1.6 %collective-permute-start.6 = (f32[12,8,256]{2,1,0:T(8,128)S(1)}, f32[12,8,256]{2,1,0:T(8,128)S(1)}, u32[]{:S(2)}, u32[]{:S(2)}) collective-permute-start(f32[12,8,256]{2,1,0:T(8,128)S(1)} %get-tuple-element.40), channel_id=1, source_target_pairs={{0,32},{32,64},{64,96},{96,128},{128,160},{160,192},{192,224},{224... | collective-permute-start | bytes 294920 | tf_op jit(solution)/shard_map/ppermute | solution.py:472
  17.1 4.0 %collective-permute-start.7 = (f32[12,8,256]{2,1,0:T(8,128)S(1)}, f32[12,8,256]{2,1,0:T(8,128)S(1)}, u32[]{:S(2)}, u32[]{:S(2)}) collective-permute-start(f32[12,8,256]{2,1,0:T(8,128)S(1)} %get-tuple-element.41), channel_id=1, source_target_pairs={{0,224},{32,0},{64,32},{96,64},{128,96},{160,128},{192,160},{224,1... | collective-permute-start | bytes 294920 | tf_op jit(solution)/shard_map/ppermute | solution.py:473
  21.2 0.0 copy-done.2
  21.2 0.0 copy-done.3
  21.2 0.3 weights.1
  21.5 0.9 %inner.1 = (f32[3,6,24,384]{3,2,1,0:T(8,128)S(1)}, f32[4,24,384]{2,1,0:T(8,128)S(1)}, f32[2,24,384]{2,1,0:T(8,128)S(1)}, f32[3,4,16,256]{3,2,1,0:T(8,128)S(1)}, f32[3,2,16,256]{3,2,1,0:T(8,128)S(1)}) custom-call(f32[7,8,16,256]{3,2,1,0:T(8,128)S(1)} %get-tuple-element.29.fields, f32[7,8,8,256]{3,2,1,0:T(8,128)S(1)} %get-tuple-element.34.rows, ...), custom_call_target="tpu_custom_call" | custom-call | bytes 4500000 | tf_op jit(solution)/shard_map/inner/pallas_call | solution.py:491
  22.5 0.0 collective-permute-done.4.xm
  22.5 0.0 collective-permute-done.5.xp
  22.5 0.6 collective-permute-done.6.rm
  23.1 0.0 collective-permute-done.7.rp
  23.1 2.3 %main.1 = (f32[5,8,128]{2,1,0:T(8,128)S(1)}, f32[5,8,128]{2,1,0:T(8,128)S(1)}, f32[9,8,16,256]{3,2,1,0:T(8,128)S(1)}, f32[8,16,256]{2,1,0:T(8,128)S(1)}, f32[8,16,256]{2,1,0:T(8,128)S(1)}) custom-call(f32[7,8,16,256]{3,2,1,0:T(8,128)S(1)} %get-tuple-element.29.fields, f32[7,8,8,256]{3,2,1,0:T(8,128)S(1)} %get-tuple-element.34.rows, ...), custom_call_target="tpu_custom_call" | custom-call | bytes 3000000 | tf_op jit(solution)/shard_map/main/pallas_call | solution.py:491
  25.4 0.0 copy-start
  25.4 0.0 copy-start.1
  25.4 0.0 copy-start.4
  25.4 1.9 %collective-permute-start.8 = (f32[5,8,128]{2,1,0:T(8,128)S(1)}, f32[5,8,128]{2,1,0:T(8,128)S(1)}, u32[]{:S(2)}, u32[]{:S(2)}) collective-permute-start(f32[5,8,128]{2,1,0:T(8,128)S(1)} %get-tuple-element.51), channel_id=1, source_target_pairs={{0,4},{4,0},{1,5},{5,1},{2,6},{6,2},{3,7},{7,3},{8,12},{12,8},{9,1... | collective-permute-start | bytes 61448 | tf_op jit(solution)/shard_map/ppermute | solution.py:478
  27.3 0.8 %collective-permute-done.8 = f32[5,8,128]{2,1,0:T(8,128)S(1)} collective-permute-done((f32[5,8,128]{2,1,0:T(8,128)S(1)}, f32[5,8,128]{2,1,0:T(8,128)S(1)}, u32[]{:S(2)}, u32[]{:S(2)}) %collective-permute-start.8) | collective-permute-done | bytes 20512 | tf_op jit(solution)/shard_map/ppermute | solution.py:478
  28.2 14.0 %all_to_all.10 = f32[16,5,8,128]{3,2,1,0:T(8,128)S(1)} all-to-all(f32[16,5,8,128]{3,2,1,0:T(8,128)S(1)} %broadcast_in_dim.4), channel_id=1, replica_groups=mesh['stream'=8,'gx'=4,'core'=2,'prop'=4] {'gx','prop'}, dimensions={0} | all-to-all | bytes 655360 | tf_op jit(solution)/shard_map/all_to_all | solution.py:483
  42.2 13.9 %all_to_all.11 = f32[8,5,8,128]{3,2,1,0:T(8,128)S(1)} all-to-all(f32[8,5,8,128]{3,2,1,0:T(8,128)S(1)} %broadcast_in_dim.5), channel_id=1, replica_groups=mesh['stream'=8,'gx'=4,'core'=2,'prop'=4] {'stream'}, dimensions={0} | all-to-all | bytes 327680 | tf_op jit(solution)/shard_map/all_to_all | solution.py:483
  56.1 3.6 %collective-permute-start.9 = (f32[5,8,128]{2,1,0:T(8,128)S(1)}, f32[5,8,128]{2,1,0:T(8,128)S(1)}, u32[]{:S(2)}, u32[]{:S(2)}) collective-permute-start(f32[5,8,128]{2,1,0:T(8,128)S(1)} %reduce_sum.19.mine), channel_id=1, source_target_pairs={{0,4},{4,0},{1,5},{5,1},{2,6},{6,2},{3,7},{7,3},{8,12},{12,8},{9,1... | collective-permute-start | bytes 61448 | tf_op jit(solution)/shard_map/ppermute | solution.py:478
  59.6 0.8 %collective-permute-done.9.other = f32[5,8,128]{2,1,0:T(8,128)S(1)} collective-permute-done((f32[5,8,128]{2,1,0:T(8,128)S(1)}, f32[5,8,128]{2,1,0:T(8,128)S(1)}, u32[]{:S(2)}, u32[]{:S(2)}) %collective-permute-start.9) | collective-permute-done | bytes 20512 | tf_op jit(solution)/shard_map/ppermute | solution.py:478
  60.5 0.0 copy-done
  60.5 0.0 copy-done.1
  60.5 0.0 copy-done.4
  60.5 1.6 %final.1 = (f32[3,8,16,256]{3,2,1,0:T(8,128)}, f32[8,16,256]{2,1,0:T(8,128)}, f32[3,1024]{1,0:T(4,128)}) custom-call(f32[5,8,128]{2,1,0:T(8,128)S(1)} %reduce_sum.19.mine, f32[5,8,128]{2,1,0:T(8,128)S(1)} %collective-permute-done.9.other, f32[8,16,256]{2,1,0:T(8,128)S(1)} %copy-done, f32[9,8,16,256]{3,2,1,0:T(8,128)S(1)} %get-tuple-element.52.grads, ...), custom_call_target="tpu_custom_call" | custom-call | bytes 3000000 | tf_op jit(solution)/shard_map/final/pallas_call | solution.py:491
  (5 shorter events, 0.1 us)
Async XLA Ops:
  1.9 19.2 %copy-start.2 = (s32[3,1024]{1,0:T(4,128)S(1)}, s32[3,1024]{1,0:T(4,128)}, u32[]{:S(2)}) copy-start(s32[3,1024]{1,0:T(4,128)} %host.1) | copy-start | bytes 36868
  1.9 19.2 %copy-start.3 = (f32[3,1024]{1,0:T(4,128)S(1)}, f32[3,1024]{1,0:T(4,128)}, u32[]{:S(2)}) copy-start(f32[3,1024]{1,0:T(4,128)} %off.1) | copy-start | bytes 36868
  2.0 8.5 %collective-permute-start = (f32[28,8,256]{2,1,0:T(8,128)S(1)}, f32[28,8,256]{2,1,0:T(8,128)S(1)}, u32[]{:S(2)}, u32[]{:S(2)}) collective-permute-start(f32[28,8,256]{2,1,0:T(8,128)S(1)} %get-tuple-element.32), channel_id=1, source_target_pairs={{0,4},{4,8},{8,12},{12,16},{16,20},{20,24},{24,28},{28,0},{1,5},{5... | collective-permute-start | bytes 688136 | tf_op jit(solution)/shard_map/ppermute | solution.py:472
  4.6 5.9 %collective-permute-start.1 = (f32[28,8,256]{2,1,0:T(8,128)S(1)}, f32[28,8,256]{2,1,0:T(8,128)S(1)}, u32[]{:S(2)}, u32[]{:S(2)}) collective-permute-start(f32[28,8,256]{2,1,0:T(8,128)S(1)} %get-tuple-element.33), channel_id=1, source_target_pairs={{0,28},{4,0},{8,4},{12,8},{16,12},{20,16},{24,20},{28,24},{1,29},{... | collective-permute-start | bytes 688136 | tf_op jit(solution)/shard_map/ppermute | solution.py:473
  5.2 17.2 %collective-permute-start.4 = (f32[21,16,256]{2,1,0:T(8,128)S(1)}, f32[21,16,256]{2,1,0:T(8,128)S(1)}, u32[]{:S(2)}, u32[]{:S(2)}) collective-permute-start(f32[21,16,256]{2,1,0:T(8,128)S(1)} %get-tuple-element.38), channel_id=1, source_target_pairs={{0,32},{32,64},{64,96},{96,128},{128,160},{160,192},{192,224},{224... | collective-permute-start | bytes 1032200 | tf_op jit(solution)/shard_map/ppermute | solution.py:472
  6.2 16.3 %collective-permute-start.5 = (f32[21,16,256]{2,1,0:T(8,128)S(1)}, f32[21,16,256]{2,1,0:T(8,128)S(1)}, u32[]{:S(2)}, u32[]{:S(2)}) collective-permute-start(f32[21,16,256]{2,1,0:T(8,128)S(1)} %get-tuple-element.39), channel_id=1, source_target_pairs={{0,224},{32,0},{64,32},{96,64},{128,96},{160,128},{192,160},{224,1... | collective-permute-start | bytes 1032200 | tf_op jit(solution)/shard_map/ppermute | solution.py:473
  10.7 4.3 %collective-permute-start.2 = (f32[2,24,128]{2,1,0:T(8,128)S(1)}, f32[2,24,128]{2,1,0:T(8,128)S(1)}, u32[]{:S(2)}, u32[]{:S(2)}) collective-permute-start(f32[2,24,128]{2,1,0:T(8,128)S(1)} %get-tuple-element.35), channel_id=1, source_target_pairs={{0,1},{1,2},{2,3},{3,0},{4,5},{5,6},{6,7},{7,4},{8,9},{9,10},{10,1... | collective-permute-start | bytes 73736 | tf_op jit(solution)/shard_map/ppermute | solution.py:472
  12.1 3.0 %collective-permute-start.3 = (f32[2,24,128]{2,1,0:T(8,128)S(1)}, f32[2,24,128]{2,1,0:T(8,128)S(1)}, u32[]{:S(2)}, u32[]{:S(2)}) collective-permute-start(f32[2,24,128]{2,1,0:T(8,128)S(1)} %get-tuple-element.36), channel_id=1, source_target_pairs={{0,3},{1,0},{2,1},{3,2},{4,7},{5,4},{6,5},{7,6},{8,11},{9,8},{10,9... | collective-permute-start | bytes 73736 | tf_op jit(solution)/shard_map/ppermute | solution.py:473
  15.6 7.5 %collective-permute-start.6 = (f32[12,8,256]{2,1,0:T(8,128)S(1)}, f32[12,8,256]{2,1,0:T(8,128)S(1)}, u32[]{:S(2)}, u32[]{:S(2)}) collective-permute-start(f32[12,8,256]{2,1,0:T(8,128)S(1)} %get-tuple-element.40), channel_id=1, source_target_pairs={{0,32},{32,64},{64,96},{96,128},{128,160},{160,192},{192,224},{224... | collective-permute-start | bytes 294920 | tf_op jit(solution)/shard_map/ppermute | solution.py:472
  17.1 5.9 %collective-permute-start.7 = (f32[12,8,256]{2,1,0:T(8,128)S(1)}, f32[12,8,256]{2,1,0:T(8,128)S(1)}, u32[]{:S(2)}, u32[]{:S(2)}) collective-permute-start(f32[12,8,256]{2,1,0:T(8,128)S(1)} %get-tuple-element.41), channel_id=1, source_target_pairs={{0,224},{32,0},{64,32},{96,64},{128,96},{160,128},{192,160},{224,1... | collective-permute-start | bytes 294920 | tf_op jit(solution)/shard_map/ppermute | solution.py:473
  25.4 35.1 %copy-start = (f32[8,16,256]{2,1,0:T(8,128)S(1)}, f32[8,16,256]{2,1,0:T(8,128)}, u32[]{:S(2)}) copy-start(f32[8,16,256]{2,1,0:T(8,128)} %pres.1) | copy-start | bytes 393220
  25.4 35.1 %copy-start.1 = (f32[3,1024]{1,0:T(4,128)S(1)}, f32[3,1024]{1,0:T(4,128)}, u32[]{:S(2)}) copy-start(f32[3,1024]{1,0:T(4,128)} %motion.1) | copy-start | bytes 36868
  25.4 35.1 %copy-start.4 = (f32[1024]{0:T(1024)S(1)}, f32[1024]{0:T(1024)}, u32[]{:S(2)}) copy-start(f32[1024]{0:T(1024)} %param.17) | copy-start | bytes 12292
  25.4 2.7 %collective-permute-start.8 = (f32[5,8,128]{2,1,0:T(8,128)S(1)}, f32[5,8,128]{2,1,0:T(8,128)S(1)}, u32[]{:S(2)}, u32[]{:S(2)}) collective-permute-start(f32[5,8,128]{2,1,0:T(8,128)S(1)} %get-tuple-element.51), channel_id=1, source_target_pairs={{0,4},{4,0},{1,5},{5,1},{2,6},{6,2},{3,7},{7,3},{8,12},{12,8},{9,1... | collective-permute-start | bytes 61448 | tf_op jit(solution)/shard_map/ppermute | solution.py:478
  56.1 4.4 %collective-permute-start.9 = (f32[5,8,128]{2,1,0:T(8,128)S(1)}, f32[5,8,128]{2,1,0:T(8,128)S(1)}, u32[]{:S(2)}, u32[]{:S(2)}) collective-permute-start(f32[5,8,128]{2,1,0:T(8,128)S(1)} %reduce_sum.19.mine), channel_id=1, source_target_pairs={{0,4},{4,0},{1,5},{5,1},{2,6},{6,2},{3,7},{7,3},{8,12},{12,8},{9,1... | collective-permute-start | bytes 61448 | tf_op jit(solution)/shard_map/ppermute | solution.py:478

commit v5 on v4

--- a/solution.py
+++ b/solution.py
@@ -474,6 +474,11 @@
     return before, after
 
 
+def pairs_sum(value, axis, pairs):
+    moves = [(a, b) for a, b in pairs] + [(b, a) for a, b in pairs]
+    return value + lax.ppermute(value, axis, moves)
+
+
 def swap_cores(value):
     return lax.ppermute(value, "core", [(0, 1), (1, 0)])
 
@@ -570,8 +575,12 @@
     )
     mine = kept + swap_cores(sent)
     mine = total_over(mine, ("gx", "prop"), 16)
-    mine = total_over(mine, "stream", 8)
-    other = swap_cores(mine)
+    mine = pairs_sum(mine, "stream", [(0, 1), (2, 3), (4, 5), (6, 7)])
+    mine = pairs_sum(mine, "stream", [(1, 2), (3, 4), (5, 6), (7, 0)])
+    across = (3, 6, 5, 0, 7, 2, 1, 4)
+    both = [(2 * i + c, 2 * across[i] + 1 - c) for i in range(8) for c in range(2)]
+    other = swap_cores(mine) + lax.ppermute(mine, ("stream", "core"), both)
+    mine = mine + lax.ppermute(mine, "stream", list(enumerate(across)))
     return call(
         final_kernel,
         (sds(3, X, Y, Z), block, sds(3, points)),

time: 62.2 us -> 61.9 us (level); the launches traced: 62.1 us -> 60.9 us
  blocking collectives: 27.8 us -> 14 us
  starting transfers between devices: 22.1 us -> 30.5 us
  waiting for transfers between devices: 3.74 us -> 8.04 us
    all_to_all x2 -> x1, blocking collectives: 27.8 us -> 14 us  [total_over(): return jnp.sum(lax.all_to_all(copies, axis, 0, 0), axis=0)]
    ppermute x0 -> x4, starting transfers between devices: none -> 11.6 us  [the longest x1 4.43 us: shards(): other = swap_cores(mine) + lax.ppermute(mine, ('stream', 'core'), both)]
    ppermute x0 -> x4, waiting for transfers between devices: none -> 5.15 us  [the longest x2 3.79 us: pairs_sum(): return value + lax.ppermute(value, axis, moves)]
    ppermute x2, starting transfers between devices: 5.43 us -> 2.18 us  [swap_cores(): return lax.ppermute(value, 'core', [(0, 1), (1, 0)])]
    ppermute x2, waiting for transfers between devices: 1.69 us -> 0.85 us  [swap_cores(): return lax.ppermute(value, 'core', [(0, 1), (1, 0)])]
  transfers between devices with their start and end apart: 10 -> 14, of which waited for: 4 -> 6; matrix products, arithmetic and copies ran while one was open for 0% -> 0% of each run, Pallas kernels for 4% -> 4%
where the time goes in v5:
time: 61.9 us; the launch traced here: 60.9 us
  starting transfers between devices  30.5 us (49%)
  blocking collectives  14 us (23%)
  waiting for transfers between devices  8.04 us (13%)
  Pallas kernels  7.49 us (12%)
  between operations  0.79 us (1%)
    all_to_all x1, blocking collectives, total_over(): return jnp.sum(lax.all_to_all(copies, axis, 0, 0), axis=0)  14 us
    ppermute x4, starting transfers between devices, exchange(): after = lax.ppermute(down, axis, [(i, (i - 1) % n) for i in range(n)])  10.2 us
    pallas_call x8, Pallas kernels, call(): pl.pallas_call(kernel, out_shape=outs, in_specs=[pl.BlockSpec(memory_spac...  7.49 us
    ppermute x4, starting transfers between devices, exchange(): before = lax.ppermute(up, axis, [(i, (i + 1) % n) for i in range(n)])  6.53 us
    ppermute x1, starting transfers between devices, shards(): other = swap_cores(mine) + lax.ppermute(mine, ('stream', 'core'), both)  4.43 us
    ppermute x1, starting transfers between devices, shards(): mine = mine + lax.ppermute(mine, 'stream', list(enumerate(across)))  4.22 us
    ppermute x2, waiting for transfers between devices, pairs_sum(): return value + lax.ppermute(value, axis, moves)  3.79 us
    ppermute x2, starting transfers between devices, pairs_sum(): return value + lax.ppermute(value, axis, moves)  2.96 us
  transfers between devices with their start and end apart: 14, of which 6 were waited for; matrix products, arithmetic and copies ran while one was open for 0% of the time, Pallas kernels for 4%

profile of v5, /device:TPU:1, one launch (start us, length us, event | category | flops | bytes accessed | tf_op | source)
XLA Modules:
  0.0 60.9 jit_solution(8549839868976415140)
XLA Ops:
  0.6 1.3 %pack.1 = (f32[7,8,16,256]{3,2,1,0:T(8,128)S(1)}, f32[28,8,256]{2,1,0:T(8,128)S(1)}, f32[28,8,256]{2,1,0:T(8,128)S(1)}, f32[21,16,256]{2,1,0:T(8,128)S(1)}, f32[21,16,256]{2,1,0:T(8,128)S(1)}) custom-call(f32[3,8,16,256]{3,2,1,0:T(8,128)} %args_0_.4, f32[8,16,256]{2,1,0:T(8,128)} %args_1_.4, s32[8,16,256]{2,1,0:T(8,128)} %args_2_.4, f32[8,16,256]{2,1,0:T(8,128)} %pres.1, ...), custom_call_target="tpu_custom_call" | custom-call | bytes 3000000 | tf_op jit(solution)/shard_map/pack/pallas_call | solution.py:496
  1.9 0.0 copy-start.2
  1.9 0.0 copy-start.3
  2.0 2.6 %collective-permute-start = (f32[28,8,256]{2,1,0:T(8,128)S(1)}, f32[28,8,256]{2,1,0:T(8,128)S(1)}, u32[]{:S(2)}, u32[]{:S(2)}) collective-permute-start(f32[28,8,256]{2,1,0:T(8,128)S(1)} %get-tuple-element.32), channel_id=1, source_target_pairs={{0,4},{4,8},{8,12},{12,16},{16,20},{20,24},{24,28},{28,0},{1,5},{5... | collective-permute-start | bytes 688136 | tf_op jit(solution)/shard_map/ppermute | solution.py:472
  4.6 0.7 %collective-permute-start.1 = (f32[28,8,256]{2,1,0:T(8,128)S(1)}, f32[28,8,256]{2,1,0:T(8,128)S(1)}, u32[]{:S(2)}, u32[]{:S(2)}) collective-permute-start(f32[28,8,256]{2,1,0:T(8,128)S(1)} %get-tuple-element.33), channel_id=1, source_target_pairs={{0,28},{4,0},{8,4},{12,8},{16,12},{20,16},{24,20},{28,24},{1,29},{... | collective-permute-start | bytes 688136 | tf_op jit(solution)/shard_map/ppermute | solution.py:473
  5.2 1.0 %collective-permute-start.4 = (f32[21,16,256]{2,1,0:T(8,128)S(1)}, f32[21,16,256]{2,1,0:T(8,128)S(1)}, u32[]{:S(2)}, u32[]{:S(2)}) collective-permute-start(f32[21,16,256]{2,1,0:T(8,128)S(1)} %get-tuple-element.38), channel_id=1, source_target_pairs={{0,32},{32,64},{64,96},{96,128},{128,160},{160,192},{192,224},{224... | collective-permute-start | bytes 1032200 | tf_op jit(solution)/shard_map/ppermute | solution.py:472
  6.2 3.9 %collective-permute-start.5 = (f32[21,16,256]{2,1,0:T(8,128)S(1)}, f32[21,16,256]{2,1,0:T(8,128)S(1)}, u32[]{:S(2)}, u32[]{:S(2)}) collective-permute-start(f32[21,16,256]{2,1,0:T(8,128)S(1)} %get-tuple-element.39), channel_id=1, source_target_pairs={{0,224},{32,0},{64,32},{96,64},{128,96},{160,128},{192,160},{224,1... | collective-permute-start | bytes 1032200 | tf_op jit(solution)/shard_map/ppermute | solution.py:473
  10.2 0.3 ownz.1
  10.5 0.0 collective-permute-done.ym
  10.5 0.0 collective-permute-done.1.yp
  10.5 0.2 rows.1
  10.7 1.4 %collective-permute-start.2 = (f32[2,24,128]{2,1,0:T(8,128)S(1)}, f32[2,24,128]{2,1,0:T(8,128)S(1)}, u32[]{:S(2)}, u32[]{:S(2)}) collective-permute-start(f32[2,24,128]{2,1,0:T(8,128)S(1)} %get-tuple-element.35), channel_id=1, source_target_pairs={{0,1},{1,2},{2,3},{3,0},{4,5},{5,6},{6,7},{7,4},{8,9},{9,10},{10,1... | collective-permute-start | bytes 73736 | tf_op jit(solution)/shard_map/ppermute | solution.py:472
  12.1 1.5 %collective-permute-start.3 = (f32[2,24,128]{2,1,0:T(8,128)S(1)}, f32[2,24,128]{2,1,0:T(8,128)S(1)}, u32[]{:S(2)}, u32[]{:S(2)}) collective-permute-start(f32[2,24,128]{2,1,0:T(8,128)S(1)} %get-tuple-element.36), channel_id=1, source_target_pairs={{0,3},{1,0},{2,1},{3,2},{4,7},{5,4},{6,5},{7,6},{8,11},{9,8},{10,9... | collective-permute-start | bytes 73736 | tf_op jit(solution)/shard_map/ppermute | solution.py:473
  13.6 1.4 %collective-permute-done.2.zm = f32[2,24,128]{2,1,0:T(8,128)S(1)} collective-permute-done((f32[2,24,128]{2,1,0:T(8,128)S(1)}, f32[2,24,128]{2,1,0:T(8,128)S(1)}, u32[]{:S(2)}, u32[]{:S(2)}) %collective-permute-start.2) | collective-permute-done | bytes 24608 | tf_op jit(solution)/shard_map/ppermute | solution.py:472
  15.0 0.0 collective-permute-done.3.zp
  15.0 0.5 third.1
  15.6 1.6 %collective-permute-start.6 = (f32[12,8,256]{2,1,0:T(8,128)S(1)}, f32[12,8,256]{2,1,0:T(8,128)S(1)}, u32[]{:S(2)}, u32[]{:S(2)}) collective-permute-start(f32[12,8,256]{2,1,0:T(8,128)S(1)} %get-tuple-element.40), channel_id=1, source_target_pairs={{0,32},{32,64},{64,96},{96,128},{128,160},{160,192},{192,224},{224... | collective-permute-start | bytes 294920 | tf_op jit(solution)/shard_map/ppermute | solution.py:472
  17.1 4.0 %collective-permute-start.7 = (f32[12,8,256]{2,1,0:T(8,128)S(1)}, f32[12,8,256]{2,1,0:T(8,128)S(1)}, u32[]{:S(2)}, u32[]{:S(2)}) collective-permute-start(f32[12,8,256]{2,1,0:T(8,128)S(1)} %get-tuple-element.41), channel_id=1, source_target_pairs={{0,224},{32,0},{64,32},{96,64},{128,96},{160,128},{192,160},{224,1... | collective-permute-start | bytes 294920 | tf_op jit(solution)/shard_map/ppermute | solution.py:473
  21.2 0.0 copy-done.2
  21.2 0.0 copy-done.3
  21.2 0.3 weights.1
  21.5 0.9 %inner.1 = (f32[3,6,24,384]{3,2,1,0:T(8,128)S(1)}, f32[4,24,384]{2,1,0:T(8,128)S(1)}, f32[2,24,384]{2,1,0:T(8,128)S(1)}, f32[3,4,16,256]{3,2,1,0:T(8,128)S(1)}, f32[3,2,16,256]{3,2,1,0:T(8,128)S(1)}) custom-call(f32[7,8,16,256]{3,2,1,0:T(8,128)S(1)} %get-tuple-element.29.fields, f32[7,8,8,256]{3,2,1,0:T(8,128)S(1)} %get-tuple-element.34.rows, ...), custom_call_target="tpu_custom_call" | custom-call | bytes 4500000 | tf_op jit(solution)/shard_map/inner/pallas_call | solution.py:496
  22.5 0.0 collective-permute-done.4.xm
  22.5 0.0 collective-permute-done.5.xp
  22.5 0.6 collective-permute-done.6.rm
  23.1 0.0 collective-permute-done.7.rp
  23.1 2.3 %main.1 = (f32[5,8,128]{2,1,0:T(8,128)S(1)}, f32[5,8,128]{2,1,0:T(8,128)S(1)}, f32[9,8,16,256]{3,2,1,0:T(8,128)S(1)}, f32[8,16,256]{2,1,0:T(8,128)S(1)}, f32[8,16,256]{2,1,0:T(8,128)S(1)}) custom-call(f32[7,8,16,256]{3,2,1,0:T(8,128)S(1)} %get-tuple-element.29.fields, f32[7,8,8,256]{3,2,1,0:T(8,128)S(1)} %get-tuple-element.34.rows, ...), custom_call_target="tpu_custom_call" | custom-call | bytes 3000000 | tf_op jit(solution)/shard_map/main/pallas_call | solution.py:496
  25.4 0.0 copy-start
  25.4 0.0 copy-start.1
  25.4 0.0 copy-start.4
  25.4 1.9 %collective-permute-start.8 = (f32[5,8,128]{2,1,0:T(8,128)S(1)}, f32[5,8,128]{2,1,0:T(8,128)S(1)}, u32[]{:S(2)}, u32[]{:S(2)}) collective-permute-start(f32[5,8,128]{2,1,0:T(8,128)S(1)} %get-tuple-element.51), channel_id=1, source_target_pairs={{0,4},{4,0},{1,5},{5,1},{2,6},{6,2},{3,7},{7,3},{8,12},{12,8},{9,1... | collective-permute-start | bytes 61448 | tf_op jit(solution)/shard_map/ppermute | solution.py:483
  27.3 0.8 %collective-permute-done.8 = f32[5,8,128]{2,1,0:T(8,128)S(1)} collective-permute-done((f32[5,8,128]{2,1,0:T(8,128)S(1)}, f32[5,8,128]{2,1,0:T(8,128)S(1)}, u32[]{:S(2)}, u32[]{:S(2)}) %collective-permute-start.8) | collective-permute-done | bytes 20512 | tf_op jit(solution)/shard_map/ppermute | solution.py:483
  28.2 14.0 %all_to_all.5 = f32[16,5,8,128]{3,2,1,0:T(8,128)S(1)} all-to-all(f32[16,5,8,128]{3,2,1,0:T(8,128)S(1)} %broadcast_in_dim.2), channel_id=1, replica_groups=mesh['stream'=8,'gx'=4,'core'=2,'prop'=4] {'gx','prop'}, dimensions={0} | all-to-all | bytes 655360 | tf_op jit(solution)/shard_map/all_to_all | solution.py:488
  42.1 0.1 collective-permute-start.9
  42.2 2.6 %collective-permute-done.9 = f32[5,8,128]{2,1,0:T(8,128)S(1)} collective-permute-done((f32[5,8,128]{2,1,0:T(8,128)S(1)}, f32[5,8,128]{2,1,0:T(8,128)S(1)}, u32[]{:S(2)}, u32[]{:S(2)}) %collective-permute-start.9) | collective-permute-done | bytes 20512 | tf_op jit(solution)/shard_map/ppermute | solution.py:479
  44.9 2.9 %collective-permute-start.10 = (f32[5,8,128]{2,1,0:T(8,128)S(1)}, f32[5,8,128]{2,1,0:T(8,128)S(1)}, u32[]{:S(2)}, u32[]{:S(2)}) collective-permute-start(f32[5,8,128]{2,1,0:T(8,128)S(1)} %add.16), channel_id=1, source_target_pairs={{32,64},{96,128},{160,192},{224,0},{64,32},{128,96},{192,160},{0,2... | collective-permute-start | bytes 61448 | tf_op jit(solution)/shard_map/ppermute | solution.py:479
  47.7 1.2 %collective-permute-done.10 = f32[5,8,128]{2,1,0:T(8,128)S(1)} collective-permute-done((f32[5,8,128]{2,1,0:T(8,128)S(1)}, f32[5,8,128]{2,1,0:T(8,128)S(1)}, u32[]{:S(2)}, u32[]{:S(2)}) %collective-permute-start.10) | collective-permute-done | bytes 20512 | tf_op jit(solution)/shard_map/ppermute | solution.py:479
  48.9 4.2 %collective-permute-start.11 = (f32[5,8,128]{2,1,0:T(8,128)S(1)}, f32[5,8,128]{2,1,0:T(8,128)S(1)}, u32[]{:S(2)}, u32[]{:S(2)}) collective-permute-start(f32[5,8,128]{2,1,0:T(8,128)S(1)} %add.17), channel_id=1, source_target_pairs={{0,96},{32,192},{64,160},{96,0},{128,224},{160,64},{192,32},{224,1... | collective-permute-start | bytes 61448 | tf_op jit(solution)/shard_map/ppermute | solution.py:583
  53.1 4.4 %collective-permute-start.13 = (f32[5,8,128]{2,1,0:T(8,128)S(1)}, f32[5,8,128]{2,1,0:T(8,128)S(1)}, u32[]{:S(2)}, u32[]{:S(2)}) collective-permute-start(f32[5,8,128]{2,1,0:T(8,128)S(1)} %add.17), channel_id=1, source_target_pairs={{0,100},{4,96},{32,196},{36,192},{64,164},{68,160},{96,4},{100,0},... | collective-permute-start | bytes 61448 | tf_op jit(solution)/shard_map/ppermute | solution.py:582
  57.6 0.3 collective-permute-start.12
  57.9 0.0 collective-permute-done.11
  57.9 1.4 %collective-permute-done.13 = f32[5,8,128]{2,1,0:T(8,128)S(1)} collective-permute-done((f32[5,8,128]{2,1,0:T(8,128)S(1)}, f32[5,8,128]{2,1,0:T(8,128)S(1)}, u32[]{:S(2)}, u32[]{:S(2)}) %collective-permute-start.13) | collective-permute-done | bytes 20512 | tf_op jit(solution)/shard_map/ppermute | solution.py:582
  59.2 0.0 collective-permute-done.12
  59.2 0.0 copy-done
  59.2 0.0 copy-done.1
  59.3 0.0 copy-done.4
  59.3 1.6 %final.1 = (f32[3,8,16,256]{3,2,1,0:T(8,128)}, f32[8,16,256]{2,1,0:T(8,128)}, f32[3,1024]{1,0:T(4,128)}) custom-call(f32[5,8,128]{2,1,0:T(8,128)S(1)} %add.18.mine, f32[5,8,128]{2,1,0:T(8,128)S(1)} %add.19.other, f32[8,16,256]{2,1,0:T(8,128)S(1)} %copy-done, f32[9,8,16,256]{3,2,1,0:T(8,128)S(1)} %get-tuple-element.52.grads, ...), custom_call_target="tpu_custom_call" | custom-call | bytes 3000000 | tf_op jit(solution)/shard_map/final/pallas_call | solution.py:496
  (7 shorter events, 0.1 us)
Async XLA Ops:
  1.9 19.2 %copy-start.2 = (s32[3,1024]{1,0:T(4,128)S(1)}, s32[3,1024]{1,0:T(4,128)}, u32[]{:S(2)}) copy-start(s32[3,1024]{1,0:T(4,128)} %host.1) | copy-start | bytes 36868
  1.9 19.2 %copy-start.3 = (f32[3,1024]{1,0:T(4,128)S(1)}, f32[3,1024]{1,0:T(4,128)}, u32[]{:S(2)}) copy-start(f32[3,1024]{1,0:T(4,128)} %off.1) | copy-start | bytes 36868
  2.0 8.5 %collective-permute-start = (f32[28,8,256]{2,1,0:T(8,128)S(1)}, f32[28,8,256]{2,1,0:T(8,128)S(1)}, u32[]{:S(2)}, u32[]{:S(2)}) collective-permute-start(f32[28,8,256]{2,1,0:T(8,128)S(1)} %get-tuple-element.32), channel_id=1, source_target_pairs={{0,4},{4,8},{8,12},{12,16},{16,20},{20,24},{24,28},{28,0},{1,5},{5... | collective-permute-start | bytes 688136 | tf_op jit(solution)/shard_map/ppermute | solution.py:472
  4.6 5.9 %collective-permute-start.1 = (f32[28,8,256]{2,1,0:T(8,128)S(1)}, f32[28,8,256]{2,1,0:T(8,128)S(1)}, u32[]{:S(2)}, u32[]{:S(2)}) collective-permute-start(f32[28,8,256]{2,1,0:T(8,128)S(1)} %get-tuple-element.33), channel_id=1, source_target_pairs={{0,28},{4,0},{8,4},{12,8},{16,12},{20,16},{24,20},{28,24},{1,29},{... | collective-permute-start | bytes 688136 | tf_op jit(solution)/shard_map/ppermute | solution.py:473
  5.2 17.2 %collective-permute-start.4 = (f32[21,16,256]{2,1,0:T(8,128)S(1)}, f32[21,16,256]{2,1,0:T(8,128)S(1)}, u32[]{:S(2)}, u32[]{:S(2)}) collective-permute-start(f32[21,16,256]{2,1,0:T(8,128)S(1)} %get-tuple-element.38), channel_id=1, source_target_pairs={{0,32},{32,64},{64,96},{96,128},{128,160},{160,192},{192,224},{224... | collective-permute-start | bytes 1032200 | tf_op jit(solution)/shard_map/ppermute | solution.py:472
  6.2 16.3 %collective-permute-start.5 = (f32[21,16,256]{2,1,0:T(8,128)S(1)}, f32[21,16,256]{2,1,0:T(8,128)S(1)}, u32[]{:S(2)}, u32[]{:S(2)}) collective-permute-start(f32[21,16,256]{2,1,0:T(8,128)S(1)} %get-tuple-element.39), channel_id=1, source_target_pairs={{0,224},{32,0},{64,32},{96,64},{128,96},{160,128},{192,160},{224,1... | collective-permute-start | bytes 1032200 | tf_op jit(solution)/shard_map/ppermute | solution.py:473
  10.7 4.3 %collective-permute-start.2 = (f32[2,24,128]{2,1,0:T(8,128)S(1)}, f32[2,24,128]{2,1,0:T(8,128)S(1)}, u32[]{:S(2)}, u32[]{:S(2)}) collective-permute-start(f32[2,24,128]{2,1,0:T(8,128)S(1)} %get-tuple-element.35), channel_id=1, source_target_pairs={{0,1},{1,2},{2,3},{3,0},{4,5},{5,6},{6,7},{7,4},{8,9},{9,10},{10,1... | collective-permute-start | bytes 73736 | tf_op jit(solution)/shard_map/ppermute | solution.py:472
  12.1 3.0 %collective-permute-start.3 = (f32[2,24,128]{2,1,0:T(8,128)S(1)}, f32[2,24,128]{2,1,0:T(8,128)S(1)}, u32[]{:S(2)}, u32[]{:S(2)}) collective-permute-start(f32[2,24,128]{2,1,0:T(8,128)S(1)} %get-tuple-element.36), channel_id=1, source_target_pairs={{0,3},{1,0},{2,1},{3,2},{4,7},{5,4},{6,5},{7,6},{8,11},{9,8},{10,9... | collective-permute-start | bytes 73736 | tf_op jit(solution)/shard_map/ppermute | solution.py:473
  15.6 7.5 %collective-permute-start.6 = (f32[12,8,256]{2,1,0:T(8,128)S(1)}, f32[12,8,256]{2,1,0:T(8,128)S(1)}, u32[]{:S(2)}, u32[]{:S(2)}) collective-permute-start(f32[12,8,256]{2,1,0:T(8,128)S(1)} %get-tuple-element.40), channel_id=1, source_target_pairs={{0,32},{32,64},{64,96},{96,128},{128,160},{160,192},{192,224},{224... | collective-permute-start | bytes 294920 | tf_op jit(solution)/shard_map/ppermute | solution.py:472
  17.1 5.9 %collective-permute-start.7 = (f32[12,8,256]{2,1,0:T(8,128)S(1)}, f32[12,8,256]{2,1,0:T(8,128)S(1)}, u32[]{:S(2)}, u32[]{:S(2)}) collective-permute-start(f32[12,8,256]{2,1,0:T(8,128)S(1)} %get-tuple-element.41), channel_id=1, source_target_pairs={{0,224},{32,0},{64,32},{96,64},{128,96},{160,128},{192,160},{224,1... | collective-permute-start | bytes 294920 | tf_op jit(solution)/shard_map/ppermute | solution.py:473
  25.4 33.9 %copy-start = (f32[8,16,256]{2,1,0:T(8,128)S(1)}, f32[8,16,256]{2,1,0:T(8,128)}, u32[]{:S(2)}) copy-start(f32[8,16,256]{2,1,0:T(8,128)} %pres.1) | copy-start | bytes 393220
  25.4 33.9 %copy-start.1 = (f32[3,1024]{1,0:T(4,128)S(1)}, f32[3,1024]{1,0:T(4,128)}, u32[]{:S(2)}) copy-start(f32[3,1024]{1,0:T(4,128)} %motion.1) | copy-start | bytes 36868
  25.4 33.9 %copy-start.4 = (f32[1024]{0:T(1024)S(1)}, f32[1024]{0:T(1024)}, u32[]{:S(2)}) copy-start(f32[1024]{0:T(1024)} %param.17) | copy-start | bytes 12292
  25.4 2.7 %collective-permute-start.8 = (f32[5,8,128]{2,1,0:T(8,128)S(1)}, f32[5,8,128]{2,1,0:T(8,128)S(1)}, u32[]{:S(2)}, u32[]{:S(2)}) collective-permute-start(f32[5,8,128]{2,1,0:T(8,128)S(1)} %get-tuple-element.51), channel_id=1, source_target_pairs={{0,4},{4,0},{1,5},{5,1},{2,6},{6,2},{3,7},{7,3},{8,12},{12,8},{9,1... | collective-permute-start | bytes 61448 | tf_op jit(solution)/shard_map/ppermute | solution.py:483
  42.1 2.7 %collective-permute-start.9 = (f32[5,8,128]{2,1,0:T(8,128)S(1)}, f32[5,8,128]{2,1,0:T(8,128)S(1)}, u32[]{:S(2)}, u32[]{:S(2)}) collective-permute-start(f32[5,8,128]{2,1,0:T(8,128)S(1)} %reduce_sum.9), channel_id=1, source_target_pairs={{0,32},{64,96},{128,160},{192,224},{32,0},{96,64},{160,128},{224,1... | collective-permute-start | bytes 61448 | tf_op jit(solution)/shard_map/ppermute | solution.py:479
  44.9 4.0 %collective-permute-start.10 = (f32[5,8,128]{2,1,0:T(8,128)S(1)}, f32[5,8,128]{2,1,0:T(8,128)S(1)}, u32[]{:S(2)}, u32[]{:S(2)}) collective-permute-start(f32[5,8,128]{2,1,0:T(8,128)S(1)} %add.16), channel_id=1, source_target_pairs={{32,64},{96,128},{160,192},{224,0},{64,32},{128,96},{192,160},{0,2... | collective-permute-start | bytes 61448 | tf_op jit(solution)/shard_map/ppermute | solution.py:479
  48.9 9.0 %collective-permute-start.11 = (f32[5,8,128]{2,1,0:T(8,128)S(1)}, f32[5,8,128]{2,1,0:T(8,128)S(1)}, u32[]{:S(2)}, u32[]{:S(2)}) collective-permute-start(f32[5,8,128]{2,1,0:T(8,128)S(1)} %add.17), channel_id=1, source_target_pairs={{0,96},{32,192},{64,160},{96,0},{128,224},{160,64},{192,32},{224,1... | collective-permute-start | bytes 61448 | tf_op jit(solution)/shard_map/ppermute | solution.py:583
  53.1 6.1 %collective-permute-start.13 = (f32[5,8,128]{2,1,0:T(8,128)S(1)}, f32[5,8,128]{2,1,0:T(8,128)S(1)}, u32[]{:S(2)}, u32[]{:S(2)}) collective-permute-start(f32[5,8,128]{2,1,0:T(8,128)S(1)} %add.17), channel_id=1, source_target_pairs={{0,100},{4,96},{32,196},{36,192},{64,164},{68,160},{96,4},{100,0},... | collective-permute-start | bytes 61448 | tf_op jit(solution)/shard_map/ppermute | solution.py:582
  57.6 1.7 %collective-permute-start.12 = (f32[5,8,128]{2,1,0:T(8,128)S(1)}, f32[5,8,128]{2,1,0:T(8,128)S(1)}, u32[]{:S(2)}, u32[]{:S(2)}) collective-permute-start(f32[5,8,128]{2,1,0:T(8,128)S(1)} %add.17), channel_id=1, source_target_pairs={{0,4},{4,0},{1,5},{5,1},{2,6},{6,2},{3,7},{7,3},{8,12},{12,8},{9,1... | collective-permute-start | bytes 61448 | tf_op jit(solution)/shard_map/ppermute | solution.py:483

commit v6 on v5

--- a/solution.py
+++ b/solution.py
@@ -18,6 +18,7 @@
 CORNER = (3, 3, 3, 2, 2, 2, 1)
 RELAYED = [(f, d) for f in range(FIELDS) for d in range(1, CORNER[f] + 1)]
 SHARED = [(f, d) for f, d in RELAYED if d < CORNER[f]]
+GIVEN = {(f, x) for f, d in RELAYED for x in (d - 1, X - d)}
 YPAIRS = FIELDS * X // 2
 ZUNITS = -(-FIELDS * X // 32)
 SHARED += [(f, d) for f, d in RELAYED if CORNER[f] == 1]
@@ -51,22 +52,26 @@
     ]
     for copy in copies:
         copy.start()
-    for copy in copies:
-        copy.wait()
-    own_out[KEEP] = 1.0 - stage[...].astype(F32)
+    return {f: [copy] for f, copy in zip((0, VISC, KEEP, PRES, RELAX), copies)}
 
 
 def pack_kernel(*args):
     refs, (fields, y_up, y_down, up, down, stage, sems) = args[:5], args[5:]
-    load(refs, fields, stage, sems)
+    copies = load(refs, fields, stage, sems)
     low_rows = iota((8, Z), 0) < 4
-    for t in range(YPAIRS):
-        f, x = divmod(2 * t, X)
-        a, b = fields[f, x], fields[f, x + 1]
-        y_up[t] = jnp.where(low_rows, roll(a[8:], 4, 0), b[8:])
-        y_down[t] = jnp.where(low_rows, a[:8], roll(b[:8], 4, 0))
-    for i, (f, d) in enumerate(XLAYERS):
-        up[i], down[i] = fields[f, X - d], fields[f, d - 1]
+    for f in (VISC, PRES, RELAX, KEEP, 0, 1, 2):
+        for copy in copies.get(f, ()):
+            copy.wait()
+        if f == KEEP:
+            fields[KEEP] = 1.0 - stage[...].astype(F32)
+        for x in range(0, X, 2):
+            t = (f * X + x) // 2
+            a, b = fields[f, x], fields[f, x + 1]
+            y_up[t] = jnp.where(low_rows, roll(a[8:], 4, 0), b[8:])
+            y_down[t] = jnp.where(low_rows, a[:8], roll(b[:8], 4, 0))
+        for d in range(1, RADIUS[f] + 1):
+            i = XLAYERS.index((f, d))
+            up[i], down[i] = fields[f, X - d], fields[f, d - 1]
 
 
 def position():
@@ -118,21 +123,31 @@
         z_up[unit, Y:], z_down[unit, Y:] = ups[unit], downs[unit]
 
 
-def third_kernel(rows, zm, zp, third, r_up, r_down):
+def z_halos(zm, zp, third, given):
     in_zm, in_zp = inside_flags()[4:]
     lane = iota((8, 128), 1)
     right = (lane < 4).astype(F32) * in_zp
     left = (lane >= 124).astype(F32) * in_zm
-    slot = lane // 8
-    row = iota((8, Z), 0)
-    outer_rows = (row < 2) | (row >= 6)
     for f in range(FIELDS):
         for x in range(X):
+            if ((f, x) in GIVEN) != given:
+                continue
+            unit, j = divmod(f * X + x, 32)
             for h in range(3):
-                unit, j = divmod(f * X + x, 32)
                 cut = slice(8 * h, 8 * h + 8)
                 plus, minus = roll(zp[unit, cut], -4 * j, 1), roll(zm[unit, cut], 124 - 4 * j, 1)
                 third[f, x, cut] = plus * right + minus * left
+
+
+def rest_kernel(zm, zp, third):
+    z_halos(zm, zp, third, False)
+
+
+def third_kernel(rows, zm, zp, third, r_up, r_down):
+    z_halos(zm, zp, third, True)
+    slot = iota((8, 128), 1) // 8
+    row = iota((8, Z), 0)
+    outer_rows = (row < 2) | (row >= 6)
     to_up, to_down = {}, {}
     for up, out in ((True, to_up), (False, to_down)):
         units = [jnp.zeros((8, 128), F32) for _ in range(4)]
@@ -234,13 +249,14 @@
         out[start + d, at] = keep * (own(p) - own(m))
 
 
-def extended(fields, rows, third, f, x):
-    return jnp.concatenate([jnp.concatenate([fields[f, x], rows[f, x]], axis=0), third[f, x]], axis=1)
-
-
-def inner_kernel(fields, rows, third, pred_out, res_out, img_out, first_out, second_out):
+def extended(fields, rows, third, rest, f, x):
+    z_tile = third[f, x] if (f, x) in GIVEN else rest[f, x]
+    return jnp.concatenate([jnp.concatenate([fields[f, x], rows[f, x]], axis=0), z_tile], axis=1)
+
+
+def inner_kernel(fields, rows, third, rest, pred_out, res_out, img_out, first_out, second_out):
     def field(f, x):
-        return extended(fields, rows, third, f, x)
+        return extended(fields, rows, third, rest, f, x)
 
     def pred(k, x):
         return pred_out[k, x - 1]
@@ -291,6 +307,7 @@
     fields,
     rows,
     third,
+    rest,
     xm,
     xp,
     rm,
@@ -341,7 +358,7 @@
             return halo[0, XLAYERS.index((f, -x))]
         if x >= X:
             return halo[1, XLAYERS.index((f, x - X + 1))]
-        return extended(fields, rows, third, f, x)
+        return extended(fields, rows, third, rest, f, x)
 
     def pred(k, x):
         return pred_in[k, x - 1] if 1 <= x < 7 else pred_own[k, x + 3]
@@ -545,6 +562,7 @@
     weights = call(
         weight_kernel, (wide, wide, sds(WINDOW, Y, points)), (host_cell, offsets), name="weights", us=0.5
     )
+    rest = call(rest_kernel, (sds(FIELDS, X, YE, 128),), from_z, name="rest", us=0.3)[0]
     inner = call(
         inner_kernel,
         (
@@ -554,7 +572,7 @@
             sds(3, 4, Y, Z),
             sds(3, 2, Y, Z),
         ),
-        (fields, rows, third),
+        (fields, rows, third, rest),
         name="inner",
         us=1.5,
     )
@@ -563,7 +581,7 @@
     kept, sent, grads, r0, s = call(
         main_kernel,
         (half, half, sds(9, X, Y, Z), block, block),
-        (fields, rows, third, *from_x, *from_r, *inner, *weights),
+        (fields, rows, third, rest, *from_x, *from_r, *inner, *weights),
         [
             pltpu.VMEM((2, len(XLAYERS), YE, ZE), F32),
             pltpu.VMEM((3, X + 6, YE, ZE), F32),

time: 61.9 us -> 61.7 us (level)
    pallas_call x8 -> x9, Pallas kernels: 7.49 us -> 7.41 us  [call(): pl.pallas_call(kernel, out_shape=outs, in_specs=[pl.BlockSpec(memory_spac...]
where the time goes in v6:
time: 61.7 us; the launch traced here: 60.6 us
  starting transfers between devices  30.5 us (49%)
  blocking collectives  14 us (23%)
  waiting for transfers between devices  7.85 us (13%)
  Pallas kernels  7.41 us (12%)
  between operations  0.8 us (1%)
    all_to_all x1, blocking collectives, total_over(): return jnp.sum(lax.all_to_all(copies, axis, 0, 0), axis=0)  14 us
    ppermute x4, starting transfers between devices, exchange(): after = lax.ppermute(down, axis, [(i, (i - 1) % n) for i in range(n)])  10.2 us
    pallas_call x9, Pallas kernels, call(): pl.pallas_call(kernel, out_shape=outs, in_specs=[pl.BlockSpec(memory_spac...  7.41 us
    ppermute x4, starting transfers between devices, exchange(): before = lax.ppermute(up, axis, [(i, (i + 1) % n) for i in range(n)])  6.53 us
    ppermute x1, starting transfers between devices, shards(): other = swap_cores(mine) + lax.ppermute(mine, ('stream', 'core'), both)  4.43 us
    ppermute x1, starting transfers between devices, shards(): mine = mine + lax.ppermute(mine, 'stream', list(enumerate(across)))  4.21 us
    ppermute x2, waiting for transfers between devices, pairs_sum(): return value + lax.ppermute(value, axis, moves)  3.79 us
    ppermute x2, starting transfers between devices, pairs_sum(): return value + lax.ppermute(value, axis, moves)  2.96 us
  transfers between devices with their start and end apart: 14, of which 6 were waited for; matrix products, arithmetic and copies ran while one was open for 0% of the time, Pallas kernels for 4%

profile of v6, /device:TPU:1, one launch (start us, length us, event | category | flops | bytes accessed | tf_op | source)
XLA Modules:
  0.0 60.6 jit_solution(17336302286137221824)
XLA Ops:
  0.6 1.3 %pack.1 = (f32[7,8,16,256]{3,2,1,0:T(8,128)S(1)}, f32[28,8,256]{2,1,0:T(8,128)S(1)}, f32[28,8,256]{2,1,0:T(8,128)S(1)}, f32[21,16,256]{2,1,0:T(8,128)S(1)}, f32[21,16,256]{2,1,0:T(8,128)S(1)}) custom-call(f32[3,8,16,256]{3,2,1,0:T(8,128)} %args_0_.4, f32[8,16,256]{2,1,0:T(8,128)} %args_1_.4, s32[8,16,256]{2,1,0:T(8,128)} %args_2_.4, f32[8,16,256]{2,1,0:T(8,128)} %pres.1, ...), custom_call_target="tpu_custom_call" | custom-call | bytes 3000000 | tf_op jit(solution)/shard_map/pack/pallas_call | solution.py:513
  1.9 0.0 copy-start.2
  1.9 0.0 copy-start.3
  1.9 2.6 %collective-permute-start = (f32[28,8,256]{2,1,0:T(8,128)S(1)}, f32[28,8,256]{2,1,0:T(8,128)S(1)}, u32[]{:S(2)}, u32[]{:S(2)}) collective-permute-start(f32[28,8,256]{2,1,0:T(8,128)S(1)} %get-tuple-element.32), channel_id=1, source_target_pairs={{0,4},{4,8},{8,12},{12,16},{16,20},{20,24},{24,28},{28,0},{1,5},{5... | collective-permute-start | bytes 688136 | tf_op jit(solution)/shard_map/ppermute | solution.py:489
  4.6 0.7 %collective-permute-start.1 = (f32[28,8,256]{2,1,0:T(8,128)S(1)}, f32[28,8,256]{2,1,0:T(8,128)S(1)}, u32[]{:S(2)}, u32[]{:S(2)}) collective-permute-start(f32[28,8,256]{2,1,0:T(8,128)S(1)} %get-tuple-element.33), channel_id=1, source_target_pairs={{0,28},{4,0},{8,4},{12,8},{16,12},{20,16},{24,20},{28,24},{1,29},{... | collective-permute-start | bytes 688136 | tf_op jit(solution)/shard_map/ppermute | solution.py:490
  5.2 1.0 %collective-permute-start.4 = (f32[21,16,256]{2,1,0:T(8,128)S(1)}, f32[21,16,256]{2,1,0:T(8,128)S(1)}, u32[]{:S(2)}, u32[]{:S(2)}) collective-permute-start(f32[21,16,256]{2,1,0:T(8,128)S(1)} %get-tuple-element.38), channel_id=1, source_target_pairs={{0,32},{32,64},{64,96},{96,128},{128,160},{160,192},{192,224},{224... | collective-permute-start | bytes 1032200 | tf_op jit(solution)/shard_map/ppermute | solution.py:489
  6.2 3.9 %collective-permute-start.5 = (f32[21,16,256]{2,1,0:T(8,128)S(1)}, f32[21,16,256]{2,1,0:T(8,128)S(1)}, u32[]{:S(2)}, u32[]{:S(2)}) collective-permute-start(f32[21,16,256]{2,1,0:T(8,128)S(1)} %get-tuple-element.39), channel_id=1, source_target_pairs={{0,224},{32,0},{64,32},{96,64},{128,96},{160,128},{192,160},{224,1... | collective-permute-start | bytes 1032200 | tf_op jit(solution)/shard_map/ppermute | solution.py:490
  10.1 0.3 ownz.1
  10.4 0.0 collective-permute-done.ym
  10.4 0.0 collective-permute-done.1.yp
  10.5 0.2 rows.1
  10.7 1.4 %collective-permute-start.2 = (f32[2,24,128]{2,1,0:T(8,128)S(1)}, f32[2,24,128]{2,1,0:T(8,128)S(1)}, u32[]{:S(2)}, u32[]{:S(2)}) collective-permute-start(f32[2,24,128]{2,1,0:T(8,128)S(1)} %get-tuple-element.35), channel_id=1, source_target_pairs={{0,1},{1,2},{2,3},{3,0},{4,5},{5,6},{6,7},{7,4},{8,9},{9,10},{10,1... | collective-permute-start | bytes 73736 | tf_op jit(solution)/shard_map/ppermute | solution.py:489
  12.0 1.5 %collective-permute-start.3 = (f32[2,24,128]{2,1,0:T(8,128)S(1)}, f32[2,24,128]{2,1,0:T(8,128)S(1)}, u32[]{:S(2)}, u32[]{:S(2)}) collective-permute-start(f32[2,24,128]{2,1,0:T(8,128)S(1)} %get-tuple-element.36), channel_id=1, source_target_pairs={{0,3},{1,0},{2,1},{3,2},{4,7},{5,4},{6,5},{7,6},{8,11},{9,8},{10,9... | collective-permute-start | bytes 73736 | tf_op jit(solution)/shard_map/ppermute | solution.py:490
  13.6 1.4 %collective-permute-done.2.zm = f32[2,24,128]{2,1,0:T(8,128)S(1)} collective-permute-done((f32[2,24,128]{2,1,0:T(8,128)S(1)}, f32[2,24,128]{2,1,0:T(8,128)S(1)}, u32[]{:S(2)}, u32[]{:S(2)}) %collective-permute-start.2) | collective-permute-done | bytes 24608 | tf_op jit(solution)/shard_map/ppermute | solution.py:489
  15.0 0.0 collective-permute-done.3.zp
  15.0 0.4 third.1
  15.4 1.6 %collective-permute-start.6 = (f32[12,8,256]{2,1,0:T(8,128)S(1)}, f32[12,8,256]{2,1,0:T(8,128)S(1)}, u32[]{:S(2)}, u32[]{:S(2)}) collective-permute-start(f32[12,8,256]{2,1,0:T(8,128)S(1)} %get-tuple-element.40), channel_id=1, source_target_pairs={{0,32},{32,64},{64,96},{96,128},{128,160},{160,192},{192,224},{224... | collective-permute-start | bytes 294920 | tf_op jit(solution)/shard_map/ppermute | solution.py:489
  17.0 4.0 %collective-permute-start.7 = (f32[12,8,256]{2,1,0:T(8,128)S(1)}, f32[12,8,256]{2,1,0:T(8,128)S(1)}, u32[]{:S(2)}, u32[]{:S(2)}) collective-permute-start(f32[12,8,256]{2,1,0:T(8,128)S(1)} %get-tuple-element.41), channel_id=1, source_target_pairs={{0,224},{32,0},{64,32},{96,64},{128,96},{160,128},{192,160},{224,1... | collective-permute-start | bytes 294920 | tf_op jit(solution)/shard_map/ppermute | solution.py:490
  21.0 0.0 copy-done.2
  21.0 0.0 copy-done.3
  21.0 0.3 weights.1
  21.3 0.2 rest.1
  21.6 0.9 %inner.1 = (f32[3,6,24,384]{3,2,1,0:T(8,128)S(1)}, f32[4,24,384]{2,1,0:T(8,128)S(1)}, f32[2,24,384]{2,1,0:T(8,128)S(1)}, f32[3,4,16,256]{3,2,1,0:T(8,128)S(1)}, f32[3,2,16,256]{3,2,1,0:T(8,128)S(1)}) custom-call(f32[7,8,16,256]{3,2,1,0:T(8,128)S(1)} %get-tuple-element.29.fields, f32[7,8,8,256]{3,2,1,0:T(8,128)S(1)} %get-tuple-element.34.rows, ...), custom_call_target="tpu_custom_call" | custom-call | bytes 4500000 | tf_op jit(solution)/shard_map/inner/pallas_call | solution.py:513
  22.5 0.0 collective-permute-done.4.xm
  22.5 0.0 collective-permute-done.5.xp
  22.5 0.4 collective-permute-done.6.rm
  22.9 0.0 collective-permute-done.7.rp
  22.9 2.2 %main.1 = (f32[5,8,128]{2,1,0:T(8,128)S(1)}, f32[5,8,128]{2,1,0:T(8,128)S(1)}, f32[9,8,16,256]{3,2,1,0:T(8,128)S(1)}, f32[8,16,256]{2,1,0:T(8,128)S(1)}, f32[8,16,256]{2,1,0:T(8,128)S(1)}) custom-call(f32[7,8,16,256]{3,2,1,0:T(8,128)S(1)} %get-tuple-element.29.fields, f32[7,8,8,256]{3,2,1,0:T(8,128)S(1)} %get-tuple-element.34.rows, ...), custom_call_target="tpu_custom_call" | custom-call | bytes 3000000 | tf_op jit(solution)/shard_map/main/pallas_call | solution.py:513
  25.1 0.0 copy-start
  25.1 0.0 copy-start.1
  25.1 0.0 copy-start.4
  25.2 1.9 %collective-permute-start.8 = (f32[5,8,128]{2,1,0:T(8,128)S(1)}, f32[5,8,128]{2,1,0:T(8,128)S(1)}, u32[]{:S(2)}, u32[]{:S(2)}) collective-permute-start(f32[5,8,128]{2,1,0:T(8,128)S(1)} %get-tuple-element.51), channel_id=1, source_target_pairs={{0,4},{4,0},{1,5},{5,1},{2,6},{6,2},{3,7},{7,3},{8,12},{12,8},{9,1... | collective-permute-start | bytes 61448 | tf_op jit(solution)/shard_map/ppermute | solution.py:500
  27.1 0.8 %collective-permute-done.8 = f32[5,8,128]{2,1,0:T(8,128)S(1)} collective-permute-done((f32[5,8,128]{2,1,0:T(8,128)S(1)}, f32[5,8,128]{2,1,0:T(8,128)S(1)}, u32[]{:S(2)}, u32[]{:S(2)}) %collective-permute-start.8) | collective-permute-done | bytes 20512 | tf_op jit(solution)/shard_map/ppermute | solution.py:500
  27.9 14.0 %all_to_all.5 = f32[16,5,8,128]{3,2,1,0:T(8,128)S(1)} all-to-all(f32[16,5,8,128]{3,2,1,0:T(8,128)S(1)} %broadcast_in_dim.2), channel_id=1, replica_groups=mesh['stream'=8,'gx'=4,'core'=2,'prop'=4] {'gx','prop'}, dimensions={0} | all-to-all | bytes 655360 | tf_op jit(solution)/shard_map/all_to_all | solution.py:505
  41.9 0.1 collective-permute-start.9
  42.0 2.6 %collective-permute-done.9 = f32[5,8,128]{2,1,0:T(8,128)S(1)} collective-permute-done((f32[5,8,128]{2,1,0:T(8,128)S(1)}, f32[5,8,128]{2,1,0:T(8,128)S(1)}, u32[]{:S(2)}, u32[]{:S(2)}) %collective-permute-start.9) | collective-permute-done | bytes 20512 | tf_op jit(solution)/shard_map/ppermute | solution.py:496
  44.6 2.9 %collective-permute-start.10 = (f32[5,8,128]{2,1,0:T(8,128)S(1)}, f32[5,8,128]{2,1,0:T(8,128)S(1)}, u32[]{:S(2)}, u32[]{:S(2)}) collective-permute-start(f32[5,8,128]{2,1,0:T(8,128)S(1)} %add.16), channel_id=1, source_target_pairs={{32,64},{96,128},{160,192},{224,0},{64,32},{128,96},{192,160},{0,2... | collective-permute-start | bytes 61448 | tf_op jit(solution)/shard_map/ppermute | solution.py:496
  47.5 1.2 %collective-permute-done.10 = f32[5,8,128]{2,1,0:T(8,128)S(1)} collective-permute-done((f32[5,8,128]{2,1,0:T(8,128)S(1)}, f32[5,8,128]{2,1,0:T(8,128)S(1)}, u32[]{:S(2)}, u32[]{:S(2)}) %collective-permute-start.10) | collective-permute-done | bytes 20512 | tf_op jit(solution)/shard_map/ppermute | solution.py:496
  48.7 4.2 %collective-permute-start.11 = (f32[5,8,128]{2,1,0:T(8,128)S(1)}, f32[5,8,128]{2,1,0:T(8,128)S(1)}, u32[]{:S(2)}, u32[]{:S(2)}) collective-permute-start(f32[5,8,128]{2,1,0:T(8,128)S(1)} %add.17), channel_id=1, source_target_pairs={{0,96},{32,192},{64,160},{96,0},{128,224},{160,64},{192,32},{224,1... | collective-permute-start | bytes 61448 | tf_op jit(solution)/shard_map/ppermute | solution.py:601
  52.9 4.4 %collective-permute-start.13 = (f32[5,8,128]{2,1,0:T(8,128)S(1)}, f32[5,8,128]{2,1,0:T(8,128)S(1)}, u32[]{:S(2)}, u32[]{:S(2)}) collective-permute-start(f32[5,8,128]{2,1,0:T(8,128)S(1)} %add.17), channel_id=1, source_target_pairs={{0,100},{4,96},{32,196},{36,192},{64,164},{68,160},{96,4},{100,0},... | collective-permute-start | bytes 61448 | tf_op jit(solution)/shard_map/ppermute | solution.py:600
  57.3 0.3 collective-permute-start.12
  57.6 0.0 collective-permute-done.11
  57.6 1.4 %collective-permute-done.13 = f32[5,8,128]{2,1,0:T(8,128)S(1)} collective-permute-done((f32[5,8,128]{2,1,0:T(8,128)S(1)}, f32[5,8,128]{2,1,0:T(8,128)S(1)}, u32[]{:S(2)}, u32[]{:S(2)}) %collective-permute-start.13) | collective-permute-done | bytes 20512 | tf_op jit(solution)/shard_map/ppermute | solution.py:600
  59.0 0.0 collective-permute-done.12
  59.0 0.0 copy-done
  59.0 0.0 copy-done.1
  59.0 0.0 copy-done.4
  59.0 1.6 %final.1 = (f32[3,8,16,256]{3,2,1,0:T(8,128)}, f32[8,16,256]{2,1,0:T(8,128)}, f32[3,1024]{1,0:T(4,128)}) custom-call(f32[5,8,128]{2,1,0:T(8,128)S(1)} %add.18.mine, f32[5,8,128]{2,1,0:T(8,128)S(1)} %add.19.other, f32[8,16,256]{2,1,0:T(8,128)S(1)} %copy-done, f32[9,8,16,256]{3,2,1,0:T(8,128)S(1)} %get-tuple-element.52.grads, ...), custom_call_target="tpu_custom_call" | custom-call | bytes 3000000 | tf_op jit(solution)/shard_map/final/pallas_call | solution.py:513
  (7 shorter events, 0.1 us)
Async XLA Ops:
  1.9 19.1 %copy-start.2 = (s32[3,1024]{1,0:T(4,128)S(1)}, s32[3,1024]{1,0:T(4,128)}, u32[]{:S(2)}) copy-start(s32[3,1024]{1,0:T(4,128)} %host.1) | copy-start | bytes 36868
  1.9 19.1 %copy-start.3 = (f32[3,1024]{1,0:T(4,128)S(1)}, f32[3,1024]{1,0:T(4,128)}, u32[]{:S(2)}) copy-start(f32[3,1024]{1,0:T(4,128)} %off.1) | copy-start | bytes 36868
  1.9 8.5 %collective-permute-start = (f32[28,8,256]{2,1,0:T(8,128)S(1)}, f32[28,8,256]{2,1,0:T(8,128)S(1)}, u32[]{:S(2)}, u32[]{:S(2)}) collective-permute-start(f32[28,8,256]{2,1,0:T(8,128)S(1)} %get-tuple-element.32), channel_id=1, source_target_pairs={{0,4},{4,8},{8,12},{12,16},{16,20},{20,24},{24,28},{28,0},{1,5},{5... | collective-permute-start | bytes 688136 | tf_op jit(solution)/shard_map/ppermute | solution.py:489
  4.6 5.9 %collective-permute-start.1 = (f32[28,8,256]{2,1,0:T(8,128)S(1)}, f32[28,8,256]{2,1,0:T(8,128)S(1)}, u32[]{:S(2)}, u32[]{:S(2)}) collective-permute-start(f32[28,8,256]{2,1,0:T(8,128)S(1)} %get-tuple-element.33), channel_id=1, source_target_pairs={{0,28},{4,0},{8,4},{12,8},{16,12},{20,16},{24,20},{28,24},{1,29},{... | collective-permute-start | bytes 688136 | tf_op jit(solution)/shard_map/ppermute | solution.py:490
  5.2 17.3 %collective-permute-start.4 = (f32[21,16,256]{2,1,0:T(8,128)S(1)}, f32[21,16,256]{2,1,0:T(8,128)S(1)}, u32[]{:S(2)}, u32[]{:S(2)}) collective-permute-start(f32[21,16,256]{2,1,0:T(8,128)S(1)} %get-tuple-element.38), channel_id=1, source_target_pairs={{0,32},{32,64},{64,96},{96,128},{128,160},{160,192},{192,224},{224... | collective-permute-start | bytes 1032200 | tf_op jit(solution)/shard_map/ppermute | solution.py:489
  6.2 16.3 %collective-permute-start.5 = (f32[21,16,256]{2,1,0:T(8,128)S(1)}, f32[21,16,256]{2,1,0:T(8,128)S(1)}, u32[]{:S(2)}, u32[]{:S(2)}) collective-permute-start(f32[21,16,256]{2,1,0:T(8,128)S(1)} %get-tuple-element.39), channel_id=1, source_target_pairs={{0,224},{32,0},{64,32},{96,64},{128,96},{160,128},{192,160},{224,1... | collective-permute-start | bytes 1032200 | tf_op jit(solution)/shard_map/ppermute | solution.py:490
  10.7 4.3 %collective-permute-start.2 = (f32[2,24,128]{2,1,0:T(8,128)S(1)}, f32[2,24,128]{2,1,0:T(8,128)S(1)}, u32[]{:S(2)}, u32[]{:S(2)}) collective-permute-start(f32[2,24,128]{2,1,0:T(8,128)S(1)} %get-tuple-element.35), channel_id=1, source_target_pairs={{0,1},{1,2},{2,3},{3,0},{4,5},{5,6},{6,7},{7,4},{8,9},{9,10},{10,1... | collective-permute-start | bytes 73736 | tf_op jit(solution)/shard_map/ppermute | solution.py:489
  12.0 3.0 %collective-permute-start.3 = (f32[2,24,128]{2,1,0:T(8,128)S(1)}, f32[2,24,128]{2,1,0:T(8,128)S(1)}, u32[]{:S(2)}, u32[]{:S(2)}) collective-permute-start(f32[2,24,128]{2,1,0:T(8,128)S(1)} %get-tuple-element.36), channel_id=1, source_target_pairs={{0,3},{1,0},{2,1},{3,2},{4,7},{5,4},{6,5},{7,6},{8,11},{9,8},{10,9... | collective-permute-start | bytes 73736 | tf_op jit(solution)/shard_map/ppermute | solution.py:490
  15.4 7.5 %collective-permute-start.6 = (f32[12,8,256]{2,1,0:T(8,128)S(1)}, f32[12,8,256]{2,1,0:T(8,128)S(1)}, u32[]{:S(2)}, u32[]{:S(2)}) collective-permute-start(f32[12,8,256]{2,1,0:T(8,128)S(1)} %get-tuple-element.40), channel_id=1, source_target_pairs={{0,32},{32,64},{64,96},{96,128},{128,160},{160,192},{192,224},{224... | collective-permute-start | bytes 294920 | tf_op jit(solution)/shard_map/ppermute | solution.py:489
  17.0 5.9 %collective-permute-start.7 = (f32[12,8,256]{2,1,0:T(8,128)S(1)}, f32[12,8,256]{2,1,0:T(8,128)S(1)}, u32[]{:S(2)}, u32[]{:S(2)}) collective-permute-start(f32[12,8,256]{2,1,0:T(8,128)S(1)} %get-tuple-element.41), channel_id=1, source_target_pairs={{0,224},{32,0},{64,32},{96,64},{128,96},{160,128},{192,160},{224,1... | collective-permute-start | bytes 294920 | tf_op jit(solution)/shard_map/ppermute | solution.py:490
  25.1 33.9 %copy-start = (f32[8,16,256]{2,1,0:T(8,128)S(1)}, f32[8,16,256]{2,1,0:T(8,128)}, u32[]{:S(2)}) copy-start(f32[8,16,256]{2,1,0:T(8,128)} %pres.1) | copy-start | bytes 393220
  25.1 33.9 %copy-start.1 = (f32[3,1024]{1,0:T(4,128)S(1)}, f32[3,1024]{1,0:T(4,128)}, u32[]{:S(2)}) copy-start(f32[3,1024]{1,0:T(4,128)} %motion.1) | copy-start | bytes 36868
  25.1 33.9 %copy-start.4 = (f32[1024]{0:T(1024)S(1)}, f32[1024]{0:T(1024)}, u32[]{:S(2)}) copy-start(f32[1024]{0:T(1024)} %param.17) | copy-start | bytes 12292
  25.2 2.7 %collective-permute-start.8 = (f32[5,8,128]{2,1,0:T(8,128)S(1)}, f32[5,8,128]{2,1,0:T(8,128)S(1)}, u32[]{:S(2)}, u32[]{:S(2)}) collective-permute-start(f32[5,8,128]{2,1,0:T(8,128)S(1)} %get-tuple-element.51), channel_id=1, source_target_pairs={{0,4},{4,0},{1,5},{5,1},{2,6},{6,2},{3,7},{7,3},{8,12},{12,8},{9,1... | collective-permute-start | bytes 61448 | tf_op jit(solution)/shard_map/ppermute | solution.py:500
  41.9 2.7 %collective-permute-start.9 = (f32[5,8,128]{2,1,0:T(8,128)S(1)}, f32[5,8,128]{2,1,0:T(8,128)S(1)}, u32[]{:S(2)}, u32[]{:S(2)}) collective-permute-start(f32[5,8,128]{2,1,0:T(8,128)S(1)} %reduce_sum.9), channel_id=1, source_target_pairs={{0,32},{64,96},{128,160},{192,224},{32,0},{96,64},{160,128},{224,1... | collective-permute-start | bytes 61448 | tf_op jit(solution)/shard_map/ppermute | solution.py:496
  44.6 4.0 %collective-permute-start.10 = (f32[5,8,128]{2,1,0:T(8,128)S(1)}, f32[5,8,128]{2,1,0:T(8,128)S(1)}, u32[]{:S(2)}, u32[]{:S(2)}) collective-permute-start(f32[5,8,128]{2,1,0:T(8,128)S(1)} %add.16), channel_id=1, source_target_pairs={{32,64},{96,128},{160,192},{224,0},{64,32},{128,96},{192,160},{0,2... | collective-permute-start | bytes 61448 | tf_op jit(solution)/shard_map/ppermute | solution.py:496
  48.7 8.9 %collective-permute-start.11 = (f32[5,8,128]{2,1,0:T(8,128)S(1)}, f32[5,8,128]{2,1,0:T(8,128)S(1)}, u32[]{:S(2)}, u32[]{:S(2)}) collective-permute-start(f32[5,8,128]{2,1,0:T(8,128)S(1)} %add.17), channel_id=1, source_target_pairs={{0,96},{32,192},{64,160},{96,0},{128,224},{160,64},{192,32},{224,1... | collective-permute-start | bytes 61448 | tf_op jit(solution)/shard_map/ppermute | solution.py:601
  52.9 6.1 %collective-permute-start.13 = (f32[5,8,128]{2,1,0:T(8,128)S(1)}, f32[5,8,128]{2,1,0:T(8,128)S(1)}, u32[]{:S(2)}, u32[]{:S(2)}) collective-permute-start(f32[5,8,128]{2,1,0:T(8,128)S(1)} %add.17), channel_id=1, source_target_pairs={{0,100},{4,96},{32,196},{36,192},{64,164},{68,160},{96,4},{100,0},... | collective-permute-start | bytes 61448 | tf_op jit(solution)/shard_map/ppermute | solution.py:600
  57.3 1.7 %collective-permute-start.12 = (f32[5,8,128]{2,1,0:T(8,128)S(1)}, f32[5,8,128]{2,1,0:T(8,128)S(1)}, u32[]{:S(2)}, u32[]{:S(2)}) collective-permute-start(f32[5,8,128]{2,1,0:T(8,128)S(1)} %add.17), channel_id=1, source_target_pairs={{0,4},{4,0},{1,5},{5,1},{2,6},{6,2},{3,7},{7,3},{8,12},{12,8},{9,1... | collective-permute-start | bytes 61448 | tf_op jit(solution)/shard_map/ppermute | solution.py:500

commit v7 on v6

--- a/solution.py
+++ b/solution.py
@@ -21,7 +21,6 @@
 GIVEN = {(f, x) for f, d in RELAYED for x in (d - 1, X - d)}
 YPAIRS = FIELDS * X // 2
 ZUNITS = -(-FIELDS * X // 32)
-SHARED += [(f, d) for f, d in RELAYED if CORNER[f] == 1]
 RTILES = len(SHARED) + 2
 WINDOW = 3
 VMEM = pl.BlockSpec(memory_space=pltpu.VMEM)
@@ -158,6 +157,8 @@
                 if d + 1 == CORNER[f]:
                     after = rows[f, x - 1 if up else x + 1]
                     tile = jnp.where(outer_rows, tile, roll(after, 4, 0))
+                if (f, d) == SHARED[0]:
+                    tile = jnp.where((row == 3) | (row == 4), roll(rows[RELAX, x], 4, 0), tile)
                 out[SHARED.index((f, d))] = tile
             for h in range(3):
                 unit, j = divmod(3 * i + h, 16)
@@ -346,7 +347,8 @@
             if layer in SHARED:
                 tile = relay[SHARED.index(layer)]
             else:
-                tile = roll(relay[SHARED.index((layer[0], layer[1] - 1))], 4, 0)
+                host = SHARED[0] if layer[0] == RELAX else (layer[0], layer[1] - 1)
+                tile = roll(relay[SHARED.index(host)], 4, 0)
             halo[side, i, Y:, :Z] = tile * flag
             for h in range(3):
                 unit, j = divmod(3 * n + h, 16)

time: 61.7 us -> 61.5 us (level)
  no operation moved by 1% of the time
where the time goes in v7:
time: 61.5 us; the launch traced here: 60.5 us
  starting transfers between devices  30.5 us (50%)
  blocking collectives  13.9 us (23%)
  waiting for transfers between devices  7.76 us (13%)
  Pallas kernels  7.41 us (12%)
  between operations  0.8 us (1%)
    all_to_all x1, blocking collectives, total_over(): return jnp.sum(lax.all_to_all(copies, axis, 0, 0), axis=0)  13.9 us
    ppermute x4, starting transfers between devices, exchange(): after = lax.ppermute(down, axis, [(i, (i - 1) % n) for i in range(n)])  10.2 us
    pallas_call x9, Pallas kernels, call(): pl.pallas_call(kernel, out_shape=outs, in_specs=[pl.BlockSpec(memory_spac...  7.41 us
    ppermute x4, starting transfers between devices, exchange(): before = lax.ppermute(up, axis, [(i, (i + 1) % n) for i in range(n)])  6.53 us
    ppermute x1, starting transfers between devices, shards(): other = swap_cores(mine) + lax.ppermute(mine, ('stream', 'core'), both)  4.43 us
    ppermute x1, starting transfers between devices, shards(): mine = mine + lax.ppermute(mine, 'stream', list(enumerate(across)))  4.23 us
    ppermute x2, waiting for transfers between devices, pairs_sum(): return value + lax.ppermute(value, axis, moves)  3.79 us
    ppermute x2, starting transfers between devices, pairs_sum(): return value + lax.ppermute(value, axis, moves)  2.96 us
  transfers between devices with their start and end apart: 14, of which 6 were waited for; matrix products, arithmetic and copies ran while one was open for 0% of the time, Pallas kernels for 4%

profile of v7, /device:TPU:1, one launch (start us, length us, event | category | flops | bytes accessed | tf_op | source)
XLA Modules:
  0.0 60.5 jit_solution(13479576771906848592)
XLA Ops:
  0.6 1.3 %pack.1 = (f32[7,8,16,256]{3,2,1,0:T(8,128)S(1)}, f32[28,8,256]{2,1,0:T(8,128)S(1)}, f32[28,8,256]{2,1,0:T(8,128)S(1)}, f32[21,16,256]{2,1,0:T(8,128)S(1)}, f32[21,16,256]{2,1,0:T(8,128)S(1)}) custom-call(f32[3,8,16,256]{3,2,1,0:T(8,128)} %args_0_.4, f32[8,16,256]{2,1,0:T(8,128)} %args_1_.4, s32[8,16,256]{2,1,0:T(8,128)} %args_2_.4, f32[8,16,256]{2,1,0:T(8,128)} %pres.1, ...), custom_call_target="tpu_custom_call" | custom-call | bytes 3000000 | tf_op jit(solution)/shard_map/pack/pallas_call | solution.py:515
  1.9 0.0 copy-start.2
  1.9 0.0 copy-start.3
  1.9 2.6 %collective-permute-start = (f32[28,8,256]{2,1,0:T(8,128)S(1)}, f32[28,8,256]{2,1,0:T(8,128)S(1)}, u32[]{:S(2)}, u32[]{:S(2)}) collective-permute-start(f32[28,8,256]{2,1,0:T(8,128)S(1)} %get-tuple-element.32), channel_id=1, source_target_pairs={{0,4},{4,8},{8,12},{12,16},{16,20},{20,24},{24,28},{28,0},{1,5},{5... | collective-permute-start | bytes 688136 | tf_op jit(solution)/shard_map/ppermute | solution.py:491
  4.6 0.7 %collective-permute-start.1 = (f32[28,8,256]{2,1,0:T(8,128)S(1)}, f32[28,8,256]{2,1,0:T(8,128)S(1)}, u32[]{:S(2)}, u32[]{:S(2)}) collective-permute-start(f32[28,8,256]{2,1,0:T(8,128)S(1)} %get-tuple-element.33), channel_id=1, source_target_pairs={{0,28},{4,0},{8,4},{12,8},{16,12},{20,16},{24,20},{28,24},{1,29},{... | collective-permute-start | bytes 688136 | tf_op jit(solution)/shard_map/ppermute | solution.py:492
  5.2 1.0 %collective-permute-start.4 = (f32[21,16,256]{2,1,0:T(8,128)S(1)}, f32[21,16,256]{2,1,0:T(8,128)S(1)}, u32[]{:S(2)}, u32[]{:S(2)}) collective-permute-start(f32[21,16,256]{2,1,0:T(8,128)S(1)} %get-tuple-element.38), channel_id=1, source_target_pairs={{0,32},{32,64},{64,96},{96,128},{128,160},{160,192},{192,224},{224... | collective-permute-start | bytes 1032200 | tf_op jit(solution)/shard_map/ppermute | solution.py:491
  6.2 3.9 %collective-permute-start.5 = (f32[21,16,256]{2,1,0:T(8,128)S(1)}, f32[21,16,256]{2,1,0:T(8,128)S(1)}, u32[]{:S(2)}, u32[]{:S(2)}) collective-permute-start(f32[21,16,256]{2,1,0:T(8,128)S(1)} %get-tuple-element.39), channel_id=1, source_target_pairs={{0,224},{32,0},{64,32},{96,64},{128,96},{160,128},{192,160},{224,1... | collective-permute-start | bytes 1032200 | tf_op jit(solution)/shard_map/ppermute | solution.py:492
  10.1 0.3 ownz.1
  10.4 0.0 collective-permute-done.ym
  10.4 0.0 collective-permute-done.1.yp
  10.5 0.2 rows.1
  10.7 1.4 %collective-permute-start.2 = (f32[2,24,128]{2,1,0:T(8,128)S(1)}, f32[2,24,128]{2,1,0:T(8,128)S(1)}, u32[]{:S(2)}, u32[]{:S(2)}) collective-permute-start(f32[2,24,128]{2,1,0:T(8,128)S(1)} %get-tuple-element.35), channel_id=1, source_target_pairs={{0,1},{1,2},{2,3},{3,0},{4,5},{5,6},{6,7},{7,4},{8,9},{9,10},{10,1... | collective-permute-start | bytes 73736 | tf_op jit(solution)/shard_map/ppermute | solution.py:491
  12.0 1.5 %collective-permute-start.3 = (f32[2,24,128]{2,1,0:T(8,128)S(1)}, f32[2,24,128]{2,1,0:T(8,128)S(1)}, u32[]{:S(2)}, u32[]{:S(2)}) collective-permute-start(f32[2,24,128]{2,1,0:T(8,128)S(1)} %get-tuple-element.36), channel_id=1, source_target_pairs={{0,3},{1,0},{2,1},{3,2},{4,7},{5,4},{6,5},{7,6},{8,11},{9,8},{10,9... | collective-permute-start | bytes 73736 | tf_op jit(solution)/shard_map/ppermute | solution.py:492
  13.6 1.4 %collective-permute-done.2.zm = f32[2,24,128]{2,1,0:T(8,128)S(1)} collective-permute-done((f32[2,24,128]{2,1,0:T(8,128)S(1)}, f32[2,24,128]{2,1,0:T(8,128)S(1)}, u32[]{:S(2)}, u32[]{:S(2)}) %collective-permute-start.2) | collective-permute-done | bytes 24608 | tf_op jit(solution)/shard_map/ppermute | solution.py:491
  15.0 0.0 collective-permute-done.3.zp
  15.0 0.4 third.1
  15.4 1.6 %collective-permute-start.6 = (f32[11,8,256]{2,1,0:T(8,128)S(1)}, f32[11,8,256]{2,1,0:T(8,128)S(1)}, u32[]{:S(2)}, u32[]{:S(2)}) collective-permute-start(f32[11,8,256]{2,1,0:T(8,128)S(1)} %get-tuple-element.40), channel_id=1, source_target_pairs={{0,32},{32,64},{64,96},{96,128},{128,160},{160,192},{192,224},{224... | collective-permute-start | bytes 270344 | tf_op jit(solution)/shard_map/ppermute | solution.py:491
  17.0 4.0 %collective-permute-start.7 = (f32[11,8,256]{2,1,0:T(8,128)S(1)}, f32[11,8,256]{2,1,0:T(8,128)S(1)}, u32[]{:S(2)}, u32[]{:S(2)}) collective-permute-start(f32[11,8,256]{2,1,0:T(8,128)S(1)} %get-tuple-element.41), channel_id=1, source_target_pairs={{0,224},{32,0},{64,32},{96,64},{128,96},{160,128},{192,160},{224,1... | collective-permute-start | bytes 270344 | tf_op jit(solution)/shard_map/ppermute | solution.py:492
  21.0 0.0 copy-done.2
  21.0 0.0 copy-done.3
  21.0 0.3 weights.1
  21.3 0.2 rest.1
  21.6 0.9 %inner.1 = (f32[3,6,24,384]{3,2,1,0:T(8,128)S(1)}, f32[4,24,384]{2,1,0:T(8,128)S(1)}, f32[2,24,384]{2,1,0:T(8,128)S(1)}, f32[3,4,16,256]{3,2,1,0:T(8,128)S(1)}, f32[3,2,16,256]{3,2,1,0:T(8,128)S(1)}) custom-call(f32[7,8,16,256]{3,2,1,0:T(8,128)S(1)} %get-tuple-element.29.fields, f32[7,8,8,256]{3,2,1,0:T(8,128)S(1)} %get-tuple-element.34.rows, ...), custom_call_target="tpu_custom_call" | custom-call | bytes 4500000 | tf_op jit(solution)/shard_map/inner/pallas_call | solution.py:515
  22.5 0.0 collective-permute-done.4.xm
  22.5 0.0 collective-permute-done.5.xp
  22.5 0.3 collective-permute-done.6.rm
  22.8 0.0 collective-permute-done.7.rp
  22.8 2.2 %main.1 = (f32[5,8,128]{2,1,0:T(8,128)S(1)}, f32[5,8,128]{2,1,0:T(8,128)S(1)}, f32[9,8,16,256]{3,2,1,0:T(8,128)S(1)}, f32[8,16,256]{2,1,0:T(8,128)S(1)}, f32[8,16,256]{2,1,0:T(8,128)S(1)}) custom-call(f32[7,8,16,256]{3,2,1,0:T(8,128)S(1)} %get-tuple-element.29.fields, f32[7,8,8,256]{3,2,1,0:T(8,128)S(1)} %get-tuple-element.34.rows, ...), custom_call_target="tpu_custom_call" | custom-call | bytes 3000000 | tf_op jit(solution)/shard_map/main/pallas_call | solution.py:515
  25.0 0.0 copy-start
  25.0 0.0 copy-start.1
  25.1 0.0 copy-start.4
  25.1 1.9 %collective-permute-start.8 = (f32[5,8,128]{2,1,0:T(8,128)S(1)}, f32[5,8,128]{2,1,0:T(8,128)S(1)}, u32[]{:S(2)}, u32[]{:S(2)}) collective-permute-start(f32[5,8,128]{2,1,0:T(8,128)S(1)} %get-tuple-element.51), channel_id=1, source_target_pairs={{0,4},{4,0},{1,5},{5,1},{2,6},{6,2},{3,7},{7,3},{8,12},{12,8},{9,1... | collective-permute-start | bytes 61448 | tf_op jit(solution)/shard_map/ppermute | solution.py:502
  27.0 0.8 %collective-permute-done.8 = f32[5,8,128]{2,1,0:T(8,128)S(1)} collective-permute-done((f32[5,8,128]{2,1,0:T(8,128)S(1)}, f32[5,8,128]{2,1,0:T(8,128)S(1)}, u32[]{:S(2)}, u32[]{:S(2)}) %collective-permute-start.8) | collective-permute-done | bytes 20512 | tf_op jit(solution)/shard_map/ppermute | solution.py:502
  27.9 13.9 %all_to_all.5 = f32[16,5,8,128]{3,2,1,0:T(8,128)S(1)} all-to-all(f32[16,5,8,128]{3,2,1,0:T(8,128)S(1)} %broadcast_in_dim.2), channel_id=1, replica_groups=mesh['stream'=8,'gx'=4,'core'=2,'prop'=4] {'gx','prop'}, dimensions={0} | all-to-all | bytes 655360 | tf_op jit(solution)/shard_map/all_to_all | solution.py:507
  41.7 0.1 collective-permute-start.9
  41.8 2.6 %collective-permute-done.9 = f32[5,8,128]{2,1,0:T(8,128)S(1)} collective-permute-done((f32[5,8,128]{2,1,0:T(8,128)S(1)}, f32[5,8,128]{2,1,0:T(8,128)S(1)}, u32[]{:S(2)}, u32[]{:S(2)}) %collective-permute-start.9) | collective-permute-done | bytes 20512 | tf_op jit(solution)/shard_map/ppermute | solution.py:498
  44.5 2.9 %collective-permute-start.10 = (f32[5,8,128]{2,1,0:T(8,128)S(1)}, f32[5,8,128]{2,1,0:T(8,128)S(1)}, u32[]{:S(2)}, u32[]{:S(2)}) collective-permute-start(f32[5,8,128]{2,1,0:T(8,128)S(1)} %add.16), channel_id=1, source_target_pairs={{32,64},{96,128},{160,192},{224,0},{64,32},{128,96},{192,160},{0,2... | collective-permute-start | bytes 61448 | tf_op jit(solution)/shard_map/ppermute | solution.py:498
  47.3 1.2 %collective-permute-done.10 = f32[5,8,128]{2,1,0:T(8,128)S(1)} collective-permute-done((f32[5,8,128]{2,1,0:T(8,128)S(1)}, f32[5,8,128]{2,1,0:T(8,128)S(1)}, u32[]{:S(2)}, u32[]{:S(2)}) %collective-permute-start.10) | collective-permute-done | bytes 20512 | tf_op jit(solution)/shard_map/ppermute | solution.py:498
  48.5 4.2 %collective-permute-start.11 = (f32[5,8,128]{2,1,0:T(8,128)S(1)}, f32[5,8,128]{2,1,0:T(8,128)S(1)}, u32[]{:S(2)}, u32[]{:S(2)}) collective-permute-start(f32[5,8,128]{2,1,0:T(8,128)S(1)} %add.17), channel_id=1, source_target_pairs={{0,96},{32,192},{64,160},{96,0},{128,224},{160,64},{192,32},{224,1... | collective-permute-start | bytes 61448 | tf_op jit(solution)/shard_map/ppermute | solution.py:603
  52.7 4.4 %collective-permute-start.13 = (f32[5,8,128]{2,1,0:T(8,128)S(1)}, f32[5,8,128]{2,1,0:T(8,128)S(1)}, u32[]{:S(2)}, u32[]{:S(2)}) collective-permute-start(f32[5,8,128]{2,1,0:T(8,128)S(1)} %add.17), channel_id=1, source_target_pairs={{0,100},{4,96},{32,196},{36,192},{64,164},{68,160},{96,4},{100,0},... | collective-permute-start | bytes 61448 | tf_op jit(solution)/shard_map/ppermute | solution.py:602
  57.2 0.3 collective-permute-start.12
  57.5 0.0 collective-permute-done.11
  57.5 1.4 %collective-permute-done.13 = f32[5,8,128]{2,1,0:T(8,128)S(1)} collective-permute-done((f32[5,8,128]{2,1,0:T(8,128)S(1)}, f32[5,8,128]{2,1,0:T(8,128)S(1)}, u32[]{:S(2)}, u32[]{:S(2)}) %collective-permute-start.13) | collective-permute-done | bytes 20512 | tf_op jit(solution)/shard_map/ppermute | solution.py:602
  58.8 0.0 collective-permute-done.12
  58.8 0.0 copy-done
  58.9 0.0 copy-done.1
  58.9 0.0 copy-done.4
  58.9 1.6 %final.1 = (f32[3,8,16,256]{3,2,1,0:T(8,128)}, f32[8,16,256]{2,1,0:T(8,128)}, f32[3,1024]{1,0:T(4,128)}) custom-call(f32[5,8,128]{2,1,0:T(8,128)S(1)} %add.18.mine, f32[5,8,128]{2,1,0:T(8,128)S(1)} %add.19.other, f32[8,16,256]{2,1,0:T(8,128)S(1)} %copy-done, f32[9,8,16,256]{3,2,1,0:T(8,128)S(1)} %get-tuple-element.52.grads, ...), custom_call_target="tpu_custom_call" | custom-call | bytes 3000000 | tf_op jit(solution)/shard_map/final/pallas_call | solution.py:515
  (7 shorter events, 0.1 us)
Async XLA Ops:
  1.9 19.1 %copy-start.2 = (s32[3,1024]{1,0:T(4,128)S(1)}, s32[3,1024]{1,0:T(4,128)}, u32[]{:S(2)}) copy-start(s32[3,1024]{1,0:T(4,128)} %host.1) | copy-start | bytes 36868
  1.9 19.1 %copy-start.3 = (f32[3,1024]{1,0:T(4,128)S(1)}, f32[3,1024]{1,0:T(4,128)}, u32[]{:S(2)}) copy-start(f32[3,1024]{1,0:T(4,128)} %off.1) | copy-start | bytes 36868
  1.9 8.5 %collective-permute-start = (f32[28,8,256]{2,1,0:T(8,128)S(1)}, f32[28,8,256]{2,1,0:T(8,128)S(1)}, u32[]{:S(2)}, u32[]{:S(2)}) collective-permute-start(f32[28,8,256]{2,1,0:T(8,128)S(1)} %get-tuple-element.32), channel_id=1, source_target_pairs={{0,4},{4,8},{8,12},{12,16},{16,20},{20,24},{24,28},{28,0},{1,5},{5... | collective-permute-start | bytes 688136 | tf_op jit(solution)/shard_map/ppermute | solution.py:491
  4.6 5.9 %collective-permute-start.1 = (f32[28,8,256]{2,1,0:T(8,128)S(1)}, f32[28,8,256]{2,1,0:T(8,128)S(1)}, u32[]{:S(2)}, u32[]{:S(2)}) collective-permute-start(f32[28,8,256]{2,1,0:T(8,128)S(1)} %get-tuple-element.33), channel_id=1, source_target_pairs={{0,28},{4,0},{8,4},{12,8},{16,12},{20,16},{24,20},{28,24},{1,29},{... | collective-permute-start | bytes 688136 | tf_op jit(solution)/shard_map/ppermute | solution.py:492
  5.2 17.3 %collective-permute-start.4 = (f32[21,16,256]{2,1,0:T(8,128)S(1)}, f32[21,16,256]{2,1,0:T(8,128)S(1)}, u32[]{:S(2)}, u32[]{:S(2)}) collective-permute-start(f32[21,16,256]{2,1,0:T(8,128)S(1)} %get-tuple-element.38), channel_id=1, source_target_pairs={{0,32},{32,64},{64,96},{96,128},{128,160},{160,192},{192,224},{224... | collective-permute-start | bytes 1032200 | tf_op jit(solution)/shard_map/ppermute | solution.py:491
  6.2 16.3 %collective-permute-start.5 = (f32[21,16,256]{2,1,0:T(8,128)S(1)}, f32[21,16,256]{2,1,0:T(8,128)S(1)}, u32[]{:S(2)}, u32[]{:S(2)}) collective-permute-start(f32[21,16,256]{2,1,0:T(8,128)S(1)} %get-tuple-element.39), channel_id=1, source_target_pairs={{0,224},{32,0},{64,32},{96,64},{128,96},{160,128},{192,160},{224,1... | collective-permute-start | bytes 1032200 | tf_op jit(solution)/shard_map/ppermute | solution.py:492
  10.7 4.3 %collective-permute-start.2 = (f32[2,24,128]{2,1,0:T(8,128)S(1)}, f32[2,24,128]{2,1,0:T(8,128)S(1)}, u32[]{:S(2)}, u32[]{:S(2)}) collective-permute-start(f32[2,24,128]{2,1,0:T(8,128)S(1)} %get-tuple-element.35), channel_id=1, source_target_pairs={{0,1},{1,2},{2,3},{3,0},{4,5},{5,6},{6,7},{7,4},{8,9},{9,10},{10,1... | collective-permute-start | bytes 73736 | tf_op jit(solution)/shard_map/ppermute | solution.py:491
  12.0 3.0 %collective-permute-start.3 = (f32[2,24,128]{2,1,0:T(8,128)S(1)}, f32[2,24,128]{2,1,0:T(8,128)S(1)}, u32[]{:S(2)}, u32[]{:S(2)}) collective-permute-start(f32[2,24,128]{2,1,0:T(8,128)S(1)} %get-tuple-element.36), channel_id=1, source_target_pairs={{0,3},{1,0},{2,1},{3,2},{4,7},{5,4},{6,5},{7,6},{8,11},{9,8},{10,9... | collective-permute-start | bytes 73736 | tf_op jit(solution)/shard_map/ppermute | solution.py:492
  15.4 7.4 %collective-permute-start.6 = (f32[11,8,256]{2,1,0:T(8,128)S(1)}, f32[11,8,256]{2,1,0:T(8,128)S(1)}, u32[]{:S(2)}, u32[]{:S(2)}) collective-permute-start(f32[11,8,256]{2,1,0:T(8,128)S(1)} %get-tuple-element.40), channel_id=1, source_target_pairs={{0,32},{32,64},{64,96},{96,128},{128,160},{160,192},{192,224},{224... | collective-permute-start | bytes 270344 | tf_op jit(solution)/shard_map/ppermute | solution.py:491
  17.0 5.9 %collective-permute-start.7 = (f32[11,8,256]{2,1,0:T(8,128)S(1)}, f32[11,8,256]{2,1,0:T(8,128)S(1)}, u32[]{:S(2)}, u32[]{:S(2)}) collective-permute-start(f32[11,8,256]{2,1,0:T(8,128)S(1)} %get-tuple-element.41), channel_id=1, source_target_pairs={{0,224},{32,0},{64,32},{96,64},{128,96},{160,128},{192,160},{224,1... | collective-permute-start | bytes 270344 | tf_op jit(solution)/shard_map/ppermute | solution.py:492
  25.0 33.8 %copy-start = (f32[8,16,256]{2,1,0:T(8,128)S(1)}, f32[8,16,256]{2,1,0:T(8,128)}, u32[]{:S(2)}) copy-start(f32[8,16,256]{2,1,0:T(8,128)} %pres.1) | copy-start | bytes 393220
  25.0 33.8 %copy-start.1 = (f32[3,1024]{1,0:T(4,128)S(1)}, f32[3,1024]{1,0:T(4,128)}, u32[]{:S(2)}) copy-start(f32[3,1024]{1,0:T(4,128)} %motion.1) | copy-start | bytes 36868
  25.1 33.8 %copy-start.4 = (f32[1024]{0:T(1024)S(1)}, f32[1024]{0:T(1024)}, u32[]{:S(2)}) copy-start(f32[1024]{0:T(1024)} %param.17) | copy-start | bytes 12292
  25.1 2.8 %collective-permute-start.8 = (f32[5,8,128]{2,1,0:T(8,128)S(1)}, f32[5,8,128]{2,1,0:T(8,128)S(1)}, u32[]{:S(2)}, u32[]{:S(2)}) collective-permute-start(f32[5,8,128]{2,1,0:T(8,128)S(1)} %get-tuple-element.51), channel_id=1, source_target_pairs={{0,4},{4,0},{1,5},{5,1},{2,6},{6,2},{3,7},{7,3},{8,12},{12,8},{9,1... | collective-permute-start | bytes 61448 | tf_op jit(solution)/shard_map/ppermute | solution.py:502
  41.7 2.7 %collective-permute-start.9 = (f32[5,8,128]{2,1,0:T(8,128)S(1)}, f32[5,8,128]{2,1,0:T(8,128)S(1)}, u32[]{:S(2)}, u32[]{:S(2)}) collective-permute-start(f32[5,8,128]{2,1,0:T(8,128)S(1)} %reduce_sum.9), channel_id=1, source_target_pairs={{0,32},{64,96},{128,160},{192,224},{32,0},{96,64},{160,128},{224,1... | collective-permute-start | bytes 61448 | tf_op jit(solution)/shard_map/ppermute | solution.py:498
  44.5 4.0 %collective-permute-start.10 = (f32[5,8,128]{2,1,0:T(8,128)S(1)}, f32[5,8,128]{2,1,0:T(8,128)S(1)}, u32[]{:S(2)}, u32[]{:S(2)}) collective-permute-start(f32[5,8,128]{2,1,0:T(8,128)S(1)} %add.16), channel_id=1, source_target_pairs={{32,64},{96,128},{160,192},{224,0},{64,32},{128,96},{192,160},{0,2... | collective-permute-start | bytes 61448 | tf_op jit(solution)/shard_map/ppermute | solution.py:498
  48.5 9.0 %collective-permute-start.11 = (f32[5,8,128]{2,1,0:T(8,128)S(1)}, f32[5,8,128]{2,1,0:T(8,128)S(1)}, u32[]{:S(2)}, u32[]{:S(2)}) collective-permute-start(f32[5,8,128]{2,1,0:T(8,128)S(1)} %add.17), channel_id=1, source_target_pairs={{0,96},{32,192},{64,160},{96,0},{128,224},{160,64},{192,32},{224,1... | collective-permute-start | bytes 61448 | tf_op jit(solution)/shard_map/ppermute | solution.py:603
  52.7 6.1 %collective-permute-start.13 = (f32[5,8,128]{2,1,0:T(8,128)S(1)}, f32[5,8,128]{2,1,0:T(8,128)S(1)}, u32[]{:S(2)}, u32[]{:S(2)}) collective-permute-start(f32[5,8,128]{2,1,0:T(8,128)S(1)} %add.17), channel_id=1, source_target_pairs={{0,100},{4,96},{32,196},{36,192},{64,164},{68,160},{96,4},{100,0},... | collective-permute-start | bytes 61448 | tf_op jit(solution)/shard_map/ppermute | solution.py:602
  57.2 1.7 %collective-permute-start.12 = (f32[5,8,128]{2,1,0:T(8,128)S(1)}, f32[5,8,128]{2,1,0:T(8,128)S(1)}, u32[]{:S(2)}, u32[]{:S(2)}) collective-permute-start(f32[5,8,128]{2,1,0:T(8,128)S(1)} %add.17), channel_id=1, source_target_pairs={{0,4},{4,0},{1,5},{5,1},{2,6},{6,2},{3,7},{7,3},{8,12},{12,8},{9,1... | collective-permute-start | bytes 61448 | tf_op jit(solution)/shard_map/ppermute | solution.py:502
